TPU v7x, 128 devices: a whole 4x4x4 slice. The times are simulated.
128 devices in a mesh: dp: 32 (over y, x, core), tensor: 4 (over z).
Axes of the slice: x: 4, y: 4, z: 4, core: 2. Of those that a mesh axis runs over, the one named last changes fastest.
Arguments:
- layer_input: bfloat16 [32768, 2560], P('dp', 'tensor'), may hold values from -6 to 6
- norm_gain: float32 [2560], replicated, may hold values from 0.25 to 1.75
- shift_mix: float32 [2560], replicated, may hold values from 0 to 1
- key_weight: bfloat16 [2560, 5120], P(None, 'tensor'), may hold values from -0.125 to 0.125
- value_weight: bfloat16 [5120, 2560], P('tensor'), may hold values from -0.078125 to 0.078125
- key_left: bfloat16 [2048, 2560], P('dp'), may hold values from -6 to 6
- key_right: bfloat16 [2048, 5120], P('dp', 'tensor'), may hold values from -6 to 6
- value_left: bfloat16 [2048, 5120], P('dp', 'tensor'), may hold values from -6 to 6
- value_right: bfloat16 [2048, 2560], P('dp'), may hold values from -6 to 6
- fitness_rank: int32 [2048], P('dp'), may hold values from 0 to 2047, each once
Outputs:
- layer_output: bfloat16 [32768, 2560], P('dp', 'tensor')
- key_update: float32 [2560, 5120], P('dp', 'tensor')
- value_update: float32 [5120, 2560], P('tensor', 'dp')
Inputs may be any that keep to these rules, and one draw needn't show every extreme that they name: `fitness_rank`: every value of 0 to 2047 appears once.
All inputs are finite; a program needn't handle non-finite values.
Results may differ from a plain program's by a relative error of at most 0.006.
Values may be sent and summed in bfloat16 or wider, within the bound.
No kernel may reach another device: no remote copies, remote signals or barrier semaphores. Data moves between devices by JAX's collectives and lax.ppermute only.
A program may use at most 192 MiB of HBM per device.

v0:
```python
import math

import jax
import jax.numpy as jnp
from jax import lax
from jax.sharding import PartitionSpec as P

D = 2560
FFW = 5120


epsilon = 1e-05
sigma = 0.5


def local(
    layer_input,
    norm_gain,
    shift_mix,
    key_weight,
    value_weight,
    key_left,
    key_right,
    value_left,
    value_right,
    fitness_rank,
):
    full_rows = lax.all_gather(layer_input, "tensor", axis=1, tiled=True)
    members = key_left.shape[0]
    width = full_rows.shape[1]
    hidden_local = key_weight.shape[1]
    values = full_rows.astype(jnp.float32)
    centre = jnp.mean(values, axis=-1, keepdims=True)
    spread = jnp.mean((values - centre) ** 2, axis=-1, keepdims=True)
    normed = (values - centre) * lax.rsqrt(spread + epsilon) * norm_gain
    grid = normed.reshape(members, -1, width)
    previous = jnp.concatenate([jnp.zeros_like(grid[:, :1]), grid[:, :-1]], axis=1)
    mixed = (grid + (previous - grid) * shift_mix).astype(jnp.bfloat16)
    key_dots = jnp.einsum("mld,md->ml", mixed, key_left, preferred_element_type=jnp.float32)
    preact = jnp.dot(
        mixed.reshape(-1, width), key_weight, preferred_element_type=jnp.float32
    ).reshape(members, -1, hidden_local)
    preact = (
        preact
        + sigma / math.sqrt(D) * key_dots[..., None] * key_right.astype(jnp.float32)[:, None, :]
    )
    hidden = (jnp.maximum(preact, 0.0) ** 2).astype(jnp.bfloat16)
    value_dots = jnp.einsum("mlf,mf->ml", hidden, value_left, preferred_element_type=jnp.float32)
    partial_sums = jnp.dot(
        hidden.reshape(-1, hidden_local), value_weight, preferred_element_type=jnp.float32
    )
    value_factor = sigma / math.sqrt(FFW)
    dots_total = lax.psum(value_dots, "tensor")
    output = lax.psum_scatter(partial_sums, "tensor", scatter_dimension=1, tiled=True)
    shard = output.shape[1]
    right_cols = lax.dynamic_slice_in_dim(value_right, lax.axis_index("tensor") * shard, shard, 1)
    output = output + (
        value_factor * dots_total[..., None] * right_cols.astype(jnp.float32)[:, None, :]
    ).reshape(-1, shard)
    layer_output = output.astype(jnp.bfloat16)
    total_members = members * lax.axis_size("dp")
    member_weight = (fitness_rank.astype(jnp.float32) / (total_members - 1) - 0.5) / math.sqrt(
        total_members
    )
    key_scaled_local = (key_left.astype(jnp.float32) * member_weight[:, None]).astype(jnp.bfloat16)
    value_scaled_local = (value_right.astype(jnp.float32) * member_weight[:, None]).astype(
        jnp.bfloat16
    )
    key_term = jnp.dot(key_scaled_local.T, key_right, preferred_element_type=jnp.float32)
    value_term = jnp.dot(value_scaled_local.T, value_left, preferred_element_type=jnp.float32)
    stacked = lax.psum_scatter(
        jnp.concatenate([key_term, value_term], axis=1), "dp", scatter_dimension=0, tiled=True
    )
    key_update = stacked[:, :hidden_local]
    value_update = stacked[:, hidden_local:].T
    return (layer_output, key_update, value_update)


def solution(mesh):
    placed = (
        P("dp", "tensor"),
        P(),
        P(),
        P(None, "tensor"),
        P("tensor", None),
        P("dp", None),
        P("dp", "tensor"),
        P("dp", "tensor"),
        P("dp", None),
        P("dp"),
    )
    return jax.shard_map(
        local,
        mesh=mesh,
        in_specs=placed,
        out_specs=(P("dp", "tensor"), P("dp", "tensor"), P("tensor", "dp")),
        check_vma=False,
    )
```

profile of v0, /device:TPU:2, one launch (start us, length us, event | category | flops | bytes accessed | tf_op | source)
XLA Modules:
  0.0 355.9 jit_solution(16841617814373325459)
XLA Ops:
  7.2 0.0 copy-start
  7.2 0.0 copy-start.5
  7.2 0.0 all-gather.2.cloned.1.call-start
  7.2 0.7 all-gather.2.cloned.1.call-update
  7.9 0.0 reduce-scatter.5.cloned.1.call-start
  8.0 0.9 convert_element_type.35
  8.9 60.4 %all-gather.2.cloned.1.call-done = bf16[1024,2560]{1,0:T(8,128)(2,1)} async-done(((bf16[1024,640]{1,0:T(8,128)(2,1)}), bf16[1024,2560]{1,0:T(8,128)(2,1)}) %all-gather.2.cloned.1.call-update) | async-done | bytes 5242896 | tf_op jit(solution)/shard_map/all_gather | solution.py:28
  69.3 0.0 copy-start.1
  69.3 3.4 convert_reduce_fusion
  72.7 0.6 copy-done.1
  73.3 1.5 fusion.2
  74.9 0.0 copy-done.5
  74.9 0.0 copy-start.6
  74.9 1.5 fusion.3
  76.4 0.0 copy-done.6
  76.4 0.0 copy-start.4
  76.4 2.7 add_convert_fusion
  79.1 0.0 copy-done.4
  79.1 0.0 slice-start
  79.1 1.8 fusion.10
  81.0 0.0 slice-start.1
  81.0 10.2 %multiply_convert_fusion = bf16[64,16,1280]{2,1,0:T(8,128)(2,1)S(1)} fusion(bf16[64,16,2560]{2,1,0:T(8,128)(2,1)S(1)} %add_convert_fusion, bf16[2560,1280]{1,0:T(8,128)(2,1)} %param.13, f32[64,1280]{1,0:T(8,128)S(1)} %convert_element_type.35, f32[64,16]{1,0:T(8,128)S(1)} %broadcast_multiply_fusion.1), kind=kOutput, calls=%fused_computation.10 | convolution fusion | flops 6717440000 | bytes 14749696 | tf_op jit(solution)/shard_map/dot_general | solution.py:40
  91.2 0.0 copy-start.8
  91.2 1.5 copy-done.8
  92.7 0.0 slice-done
  92.7 0.0 slice-done.1
  92.7 9.5 %fusion.18 = f32[1024,2560]{1,0:T(8,128)} fusion(bf16[1024,1280]{1,0:T(8,128)(2,1)S(1)} %bitcast.39, bf16[1280,2560]{1,0:T(8,128)(2,1)S(1)} %bitcast.38), kind=kOutput, calls=%fused_computation.31 | convolution fusion | flops 6710886400 | bytes 19660800 | tf_op jit(solution)/shard_map/dot_general | solution.py:49
  102.2 0.0 copy-start.7
  102.2 0.0 copy-start.3
  102.2 0.0 reduce-scatter.5.cloned.1.call-update
  102.2 0.2 reduce-scatter.7.cloned.1.call-start
  102.4 0.4 copy-done.7
  102.8 0.3 copy-done.3
  103.1 1.9 fusion.12
  105.0 0.0 copy-done
  105.0 0.0 copy-done.2
  105.0 1.9 fusion.13
  107.0 10.8 %pad_maximum_fusion = f32[2560,2560]{0,1:T(8,128)} fusion(f32[2560,1280]{0,1:T(8,128)S(1)} %fusion.13, f32[2560,1280]{0,1:T(8,128)S(1)} %fusion.12), kind=kLoop, calls=%fused_computation | loop fusion | flops 6553600 | bytes 52428800 | tf_op jit(solution)/shard_map/concatenate | solution.py:72
  117.7 27.5 %copy.23 = f32[2560,2560]{1,0:T(8,128)} copy(f32[2560,2560]{0,1:T(8,128)} %pad_maximum_fusion) | data formatting | bytes 52428800
  145.2 0.0 reduce-scatter.7.cloned.1.call-update
  145.2 1.7 copy-done.9
  146.9 0.8 fusion.14
  147.8 16.0 %psum.7 = f32[64,16]{1,0:T(8,128)S(1)} all-reduce(f32[64,16]{1,0:T(8,128)S(1)} %bitcast.35), channel_id=1, replica_groups=mesh['dp'=32,'tensor'=4] {'tensor'}, use_global_device_ids=true, to_apply=%region_3.0 | all-reduce | flops 1024 | bytes 8192 | tf_op jit(solution)/shard_map/psum | solution.py:53
  163.8 0.1 mul.99
  163.9 37.1 %reduce-scatter.5.cloned.1.call-done = f32[1024,640]{1,0:T(8,128)} async-done(((f32[1024,2560]{1,0:T(8,128)}), f32[1024,640]{1,0:T(8,128)}) %reduce-scatter.5.cloned.1.call-update) | async-done | bytes 2621456 | tf_op jit(solution)/shard_map/reduce_scatter | solution.py:54
  201.0 3.1 fusion.9
  204.1 143.2 %reduce-scatter.7.cloned.1.call-done = f32[80,2560]{1,0:T(8,128)} async-done(((f32[2560,2560]{1,0:T(8,128)}), f32[80,2560]{1,0:T(8,128)}) %reduce-scatter.7.cloned.1.call-update) | async-done | bytes 819216
  347.3 2.1 slice_bitcast_fusion
  (9 shorter events, 0.1 us)
Async XLA Ops:
  7.2 97.9 %copy-start = (bf16[64,1280]{1,0:T(8,128)(2,1)S(1)}, bf16[64,1280]{1,0:T(8,128)(2,1)}, u32[]{:S(2)}) copy-start(bf16[64,1280]{1,0:T(8,128)(2,1)} %param.17) | copy-start | bytes 491524
  7.2 67.7 %copy-start.5 = (f32[2560]{0:T(1024)S(1)}, f32[2560]{0:T(1024)}, u32[]{:S(2)}) copy-start(f32[2560]{0:T(1024)} %param.11) | copy-start | bytes 30724
  7.2 62.1 %all-gather.2.cloned.1.call-start = ((), (), s32[]{:S(2)}) async-start(), calls=%async_computation.2 | async-start | bytes 6553600 | tf_op jit(solution)/shard_map/all_gather | solution.py:28
  7.9 193.1 %reduce-scatter.5.cloned.1.call-start = ((), (), s32[]{:S(2)}) async-start(), calls=%async_computation.3 | async-start | bytes 13107200 | tf_op jit(solution)/shard_map/reduce_scatter | solution.py:54
  69.3 4.0 %copy-start.1 = (bf16[1024,2560]{1,0:T(8,128)(2,1)S(1)}, bf16[1024,2560]{1,0:T(8,128)(2,1)}, u32[]{:S(2)}) copy-start(bf16[1024,2560]{1,0:T(8,128)(2,1)} %all-gather.2.cloned.1.call-done) | copy-start | bytes 15728644
  74.9 1.5 copy-start.6
  76.4 2.7 copy-start.4
  79.1 13.6 %slice-start = ((s8[6553600]{0:T(1024)(128)(4,1)}), s8[4194304]{0:T(1024)(128)(4,1)S(1)}, s32[]{:S(2)}) async-start(s8[6553600]{0:T(1024)(128)(4,1)} %bitcast.37), calls=%async_computation.5 | async-start | bytes 8388608
  81.0 11.7 %slice-start.1 = ((s8[6553600]{0:T(1024)(128)(4,1)}), s8[2359296]{0:T(1024)(128)(4,1)S(1)}, s32[]{:S(2)}) async-start(s8[6553600]{0:T(1024)(128)(4,1)} %bitcast.37), calls=%async_computation.6 | async-start | bytes 4718592
  91.2 1.5 copy-start.8
  102.2 0.7 copy-start.7
  102.2 0.9 copy-start.3
  102.2 245.1 %reduce-scatter.7.cloned.1.call-start = ((), (), s32[]{:S(2)}) async-start(), calls=%async_computation.4 | async-start | bytes 27033600
  103.1 1.9 copy-start.2
  145.2 1.7 copy-start.9
Sparse Core Ops, SparseCore 0:
  9.7 59.5 all-gather.1
  102.3 98.6 reduce-scatter.4
  205.0 142.2 reduce-scatter.6
where the time goes:
time: 358 us; the launch traced here: 356 us
  waiting for transfers between devices  241 us (67%)
  local copies, waits for them, and re-layouts  34.1 us (10%)
  matrix products  26.2 us (7%)
  other arithmetic  23.9 us (7%)
  blocking collectives  16 us (4%)
  between operations  13.9 us (4%)
    unnamed x4, waiting for transfers between devices  144 us
    all_gather x1, waiting for transfers between devices, local(): full_rows = lax.all_gather(layer_input, 'tensor', axis=1, tiled=True)  60.4 us
    reduce_scatter x1, waiting for transfers between devices, local(): lax.psum_scatter(partial_sums, 'tensor', scatter_dimension=1, tiled=True)  37.1 us
    unnamed x25, local copies, waits for them, and re-layouts  32 us
    psum x1, blocking collectives, local(): dots_total = lax.psum(value_dots, 'tensor')  16 us
    concatenate x1, other arithmetic, local(): jnp.concatenate([key_term, value_term], axis=1)  10.8 us
    dot_general x1, matrix products, local(): jnp.dot(mixed.reshape(-1, width), key_weight, preferred_element_type=jnp....  10.2 us
    dot_general x1, matrix products, local(): jnp.dot(hidden.reshape(-1, hidden_local), value_weight, preferred_element...  9.49 us
  transfers between devices with their start and end apart: 3, of which 3 were waited for; matrix products, arithmetic and copies ran while one was open for 13% of the time, Pallas kernels for 0%

commit v1 on v0

v1 whole, which is shorter than its diff:
```python
import functools
import math

import jax
import jax.numpy as jnp
from jax import lax
from jax.experimental import pallas as pl
from jax.experimental.pallas import tpu as pltpu
from jax.sharding import PartitionSpec as P

D = 2560
FFW = 5120
PROMPT = 16
EPSILON = 1e-05
SIGMA = 0.5
KEY_FACTOR = SIGMA / math.sqrt(D)
VALUE_FACTOR = SIGMA / math.sqrt(FFW)
CHUNKS = 2
LN_ROWS = 64
MM_ROWS = 256
F_BLOCK = 256


def split_dots(dots):
    high = dots.astype(jnp.bfloat16)
    low = (dots - high.astype(jnp.float32)).astype(jnp.bfloat16)
    return high, low


def own_member(rows, members, first_row):
    row = lax.broadcasted_iota(jnp.int32, (rows, members), 0) + first_row
    member = lax.broadcasted_iota(jnp.int32, (rows, members), 1)
    return row // PROMPT == member


def mm(a, b):
    return jnp.dot(a, b, preferred_element_type=jnp.float32)


def mm_t(a, b):
    return lax.dot_general(a, b, (((1,), (1,)), ((), ())), preferred_element_type=jnp.float32)


def ffn_kernel(
    place,
    x0,
    x1,
    x2t,
    x2b,
    x3,
    gain,
    mix,
    kw,
    vw,
    kl,
    kr,
    vl,
    vr,
    o0,
    o1,
    o2t,
    o2b,
    o3,
    mixed,
    acc,
    kdots,
    vdots,
):
    step = pl.program_id(0)
    steps = pl.num_programs(0)
    rows, width = x0.shape
    half = rows // 2
    members = kl.shape[0]
    z = place[0]

    def column(k):
        return pl.multiple_of(lax.rem(z + k, 4) * width, 128)

    def normalise(i, source2, offset2):
        first = pl.multiple_of(i * LN_ROWS, LN_ROWS)
        span = pl.ds(first, LN_ROWS)
        span2 = pl.ds(pl.multiple_of(first - offset2, LN_ROWS), LN_ROWS)
        pieces = [x0[span, :], x1[span, :], source2[span2, :], x3[span, :]]
        pieces = [p.astype(jnp.float32) for p in pieces]
        total = sum(jnp.sum(p, axis=-1, keepdims=True) for p in pieces)
        centre = total * (1.0 / D)
        pieces = [p - centre for p in pieces]
        spread = sum(jnp.sum(p * p, axis=-1, keepdims=True) for p in pieces) * (1.0 / D)
        scale = lax.rsqrt(spread + EPSILON)
        start = lax.broadcasted_iota(jnp.int32, (LN_ROWS, 1), 0) % PROMPT == 0
        for k, piece in enumerate(pieces):
            cols = pl.ds(column(k), width)
            normed = piece * scale * gain[:, cols]
            previous = jnp.where(start, 0.0, pltpu.roll(normed, 1, 0))
            mixed[span, cols] = (normed + (previous - normed) * mix[:, cols]).astype(jnp.bfloat16)

    @pl.when(step == 0)
    def _():
        lax.fori_loop(0, half // LN_ROWS, lambda i, _: (normalise(i, x2t, 0), 0)[1], 0)
        lax.fori_loop(half // LN_ROWS, rows // LN_ROWS, lambda i, _: (normalise(i, x2b, half), 0)[1], 0)

    def block(i, _):
        first = pl.multiple_of(i * MM_ROWS, MM_ROWS)
        span = pl.ds(first, MM_ROWS)
        rows_mixed = mixed[span, :]
        mine = own_member(MM_ROWS, members, first)

        @pl.when(step == 0)
        def _():
            kdots[span, :] = jnp.where(mine, mm_t(rows_mixed, kl[...]) * KEY_FACTOR, 0.0)

        high, low = split_dots(kdots[span, :])
        right = kr[...]
        preact = mm(rows_mixed, kw[...]) + (mm(high, right) + mm(low, right))
        hidden = jnp.square(jnp.maximum(preact, 0.0)).astype(jnp.bfloat16)
        dots = mm_t(hidden, vl[...])
        sums = mm(hidden, vw[...])

        @pl.when(step == 0)
        def _():
            vdots[span, :] = dots
            acc[span, :] = sums

        @pl.when(step > 0)
        def _():
            vdots[span, :] += dots
            acc[span, :] += sums

        return 0

    lax.fori_loop(0, rows // MM_ROWS, block, 0)

    @pl.when(step == steps - 1)
    def _():
        for first in range(0, rows, MM_ROWS):
            span = pl.ds(first, MM_ROWS)
            mine = own_member(MM_ROWS, members, first)
            high, low = split_dots(jnp.where(mine, vdots[span, :] * VALUE_FACTOR, 0.0))

            def piece(k):
                cols = pl.ds(column(k), width)
                right = vr[:, cols]
                return acc[span, cols] + (mm(high, right) + mm(low, right))

            o0[span, :] = piece(0)
            o1[span, :] = piece(1).astype(jnp.bfloat16)
            o3[span, :] = piece(3).astype(jnp.bfloat16)
            target2, first2 = (o2t, first) if first < half else (o2b, first - half)
            target2[pl.ds(first2, MM_ROWS), :] = piece(2).astype(jnp.bfloat16)


def ffn(place, pieces, gain, mix, kw, vw, kl, kr, vl, vr):
    rows, width = pieces[0].shape
    members, hidden = kr.shape
    half = rows // 2

    def whole(shape):
        return pl.BlockSpec(shape, lambda f, s: (0,) * len(shape))

    out_shapes = [
        jax.ShapeDtypeStruct((rows, width), jnp.float32),
        jax.ShapeDtypeStruct((rows, width), jnp.bfloat16),
        jax.ShapeDtypeStruct((half, width), jnp.bfloat16),
        jax.ShapeDtypeStruct((half, width), jnp.bfloat16),
        jax.ShapeDtypeStruct((rows, width), jnp.bfloat16),
    ]
    return pl.pallas_call(
        ffn_kernel,
        out_shape=out_shapes,
        grid_spec=pltpu.PrefetchScalarGridSpec(
            num_scalar_prefetch=1,
            grid=(hidden // F_BLOCK,),
            in_specs=[whole(p.shape) for p in pieces]
            + [
                whole((1, D)),
                whole((1, D)),
                pl.BlockSpec((D, F_BLOCK), lambda f, s: (0, f)),
                pl.BlockSpec((F_BLOCK, D), lambda f, s: (f, 0)),
                whole((members, D)),
                pl.BlockSpec((members, F_BLOCK), lambda f, s: (0, f)),
                pl.BlockSpec((members, F_BLOCK), lambda f, s: (0, f)),
                whole((members, D)),
            ],
            out_specs=[whole(s.shape) for s in out_shapes],
            scratch_shapes=[
                pltpu.VMEM((rows, D), jnp.bfloat16),
                pltpu.VMEM((rows, D), jnp.float32),
                pltpu.VMEM((rows, members), jnp.float32),
                pltpu.VMEM((rows, members), jnp.float32),
            ],
        ),
        compiler_params=pltpu.CompilerParams(
            dimension_semantics=("arbitrary",), vmem_limit_bytes=48 * 1024 * 1024
        ),
        cost_estimate=pl.CostEstimate(
            flops=4 * rows * D * hidden,
            bytes_accessed=4 * D * hidden + 8 * rows * D,
            transcendentals=rows,
        ),
    )(place, *pieces, gain, mix, kw, vw, kl, kr, vl, vr)


def shift(array, by):
    return lax.ppermute(array, "tensor", [(i, (i + by) % 4) for i in range(4)])


def local(
    layer_input,
    norm_gain,
    shift_mix,
    key_weight,
    value_weight,
    key_left,
    key_right,
    value_left,
    value_right,
    fitness_rank,
):
    members = key_left.shape[0]
    devices = lax.axis_size("dp")
    hidden = key_weight.shape[1]
    place = lax.axis_index("tensor").astype(jnp.int32).reshape(1)
    gain, mix = norm_gain.reshape(1, D), shift_mix.reshape(1, D)
    rows = layer_input.shape[0] // CHUNKS
    half = rows // 2

    gathered = []
    for c in range(CHUNKS):
        own = layer_input[c * rows : (c + 1) * rows]
        from_left, from_right = shift(own, 1), shift(own, -1)
        far_top = shift(from_left[:half], 1)
        far_bottom = shift(from_right[half:], -1)
        gathered.append([own, from_right, far_top, far_bottom, from_left])

    rights = lax.all_gather(
        jnp.concatenate([key_right, value_left], axis=1), "dp", axis=0, tiled=True
    )
    total_members = members * devices
    member_weight = (fitness_rank.astype(jnp.float32) / (total_members - 1) - 0.5) / math.sqrt(
        total_members
    )

    def scaled(factor):
        product = (factor.astype(jnp.float32) * member_weight[:, None]).astype(jnp.bfloat16)
        return product.reshape(members, devices, -1).transpose(1, 0, 2)

    lefts = jnp.concatenate([scaled(key_left), scaled(value_right)], axis=2)
    lefts = lax.all_to_all(lefts, "dp", split_axis=0, concat_axis=0, tiled=True)
    lefts = lefts.reshape(total_members, -1)
    share = lefts.shape[1] // 2
    contract = (((0,), (0,)), ((), ()))
    key_update = lax.dot_general(
        lefts[:, :share], rights[:, :hidden], contract, preferred_element_type=jnp.float32
    )
    value_update = lax.dot_general(
        rights[:, hidden:], lefts[:, share:], contract, preferred_element_type=jnp.float32
    )

    outputs = []
    for c in range(CHUNKS):
        part = slice(c * rows // PROMPT, (c + 1) * rows // PROMPT)
        own, right, far_top, far_bottom, left = ffn(
            place,
            gathered[c],
            gain,
            mix,
            key_weight,
            value_weight,
            key_left[part],
            key_right[part],
            value_left[part],
            value_right[part],
        )
        via_left, via_right = shift(far_top, 1), shift(far_bottom, -1)
        right = jnp.concatenate([right[:half] + via_left, right[half:]], axis=0)
        left = jnp.concatenate([left[:half], left[half:] + via_right], axis=0)
        got = shift(right, 1).astype(jnp.float32) + shift(left, -1).astype(jnp.float32)
        outputs.append((own + got).astype(jnp.bfloat16))
    return (jnp.concatenate(outputs, axis=0), key_update, value_update)


def solution(mesh):
    placed = (
        P("dp", "tensor"),
        P(),
        P(),
        P(None, "tensor"),
        P("tensor", None),
        P("dp", None),
        P("dp", "tensor"),
        P("dp", "tensor"),
        P("dp", None),
        P("dp"),
    )
    return jax.shard_map(
        local,
        mesh=mesh,
        in_specs=placed,
        out_specs=(P("dp", "tensor"), P("dp", "tensor"), P("tensor", "dp")),
        check_vma=False,
    )
```

time: 358 us -> 179 us (0.50)
  waiting for transfers between devices: 241 us -> 40.1 us
  Pallas kernels: 0 us -> 61 us
  starting transfers between devices: 0.3 us -> 34.2 us
  local copies, waits for them, and re-layouts: 34.1 us -> 8.84 us
  matrix products: 26.2 us -> 8.4 us
  blocking collectives: 16 us -> 0 us
  other arithmetic: 23.9 us -> 9.79 us
    unnamed x4 -> x1, waiting for transfers between devices: 144 us -> 0.02 us
    pallas_call x0 -> x2, Pallas kernels: none -> 61 us  [ffn(): pl.pallas_call(ffn_kernel, out_shape=out_shapes, grid_spec=pltpu.Prefetch...]
    all_gather x1, waiting for transfers between devices: 60.4 us -> 0.01 us  [local(): lax.all_gather(jnp.concatenate([key_right, value_left], axis=1), 'dp', ax...]
    reduce_scatter x1 -> x0, waiting for transfers between devices: 37.1 us -> none  [local(): lax.psum_scatter(partial_sums, 'tensor', scatter_dimension=1, tiled=True)]
    ppermute x0 -> x16, waiting for transfers between devices: none -> 35 us  [shift(): return lax.ppermute(array, 'tensor', [(i, (i + by) % 4) for i in range(4)])]
    unnamed x25 -> x32, local copies, waits for them, and re-layouts: 32 us -> 2.07 us
    ppermute x0 -> x16, starting transfers between devices: none -> 26.4 us  [shift(): return lax.ppermute(array, 'tensor', [(i, (i + by) % 4) for i in range(4)])]
    dot_general x6 -> x2, matrix products: 26.2 us -> 8.4 us  [the longest x1 4.3 us: local(): lax.dot_general(rights[:, hidden:], lefts[:, share:], contract, preferred...]
  transfers between devices with their start and end apart: 3 -> 18, of which waited for: 3 -> 7; matrix products, arithmetic and copies ran while one was open for 13% -> 8% of each run, Pallas kernels for 0% -> 35%
where the time goes in v1:
time: 179 us; the launch traced here: 177 us
  Pallas kernels  61 us (34%)
  waiting for transfers between devices  40.1 us (22%)
  starting transfers between devices  34.2 us (19%)
  between operations  14.3 us (8%)
  other arithmetic  9.79 us (5%)
  local copies, waits for them, and re-layouts  8.84 us (5%)
  matrix products  8.4 us (5%)
    pallas_call x2, Pallas kernels, ffn(): pl.pallas_call(ffn_kernel, out_shape=out_shapes, grid_spec=pltpu.Prefetch...  61 us
    ppermute x16, waiting for transfers between devices, shift(): return lax.ppermute(array, 'tensor', [(i, (i + by) % 4) for i in range(4)])  35 us
    ppermute x16, starting transfers between devices, shift(): return lax.ppermute(array, 'tensor', [(i, (i + by) % 4) for i in range(4)])  26.4 us
    all_to_all x1, starting transfers between devices, local(): lefts = lax.all_to_all(lefts, 'dp', split_axis=0, concat_axis=0, tiled=True)  7.76 us
    all_to_all x1, waiting for transfers between devices, local(): lefts = lax.all_to_all(lefts, 'dp', split_axis=0, concat_axis=0, tiled=True)  5.04 us
    dot_general x1, matrix products, local(): lax.dot_general(rights[:, hidden:], lefts[:, share:], contract, preferred...  4.3 us
    dot_general x1, matrix products, local(): lax.dot_general(lefts[:, :share], rights[:, :hidden], contract, preferred...  4.1 us
  transfers between devices with their start and end apart: 18, of which 7 were waited for; matrix products, arithmetic and copies ran while one was open for 8% of the time, Pallas kernels for 35%

profile of v1, /device:TPU:2, one launch (start us, length us, event | category | flops | bytes accessed | tf_op | source)
XLA Modules:
  0.0 176.6 jit_solution(2301136980012936660)
XLA Ops:
  7.2 1.8 pad_maximum_fusion.6
  9.0 1.5 fusion.6
  10.5 2.0 %collective-permute-start.1 = (bf16[512,640]{1,0:T(8,128)(2,1)S(1)}, bf16[512,640]{1,0:T(8,128)(2,1)S(1)}, u32[]{:S(2)}, u32[]{:S(2)}) collective-permute-start(bf16[512,640]{1,0:T(8,128)(2,1)S(1)} %get-tuple-element.23.x0), channel_id=1, source_target_pairs={{0,1},{1,2},{2,3},{3,0},{4,5},{5,6},{6,7},{7,4},{8,9},{9,10},{10,1... | collective-permute-start | bytes 1966088 | tf_op jit(solution)/shard_map/ppermute | solution.py:204
  12.5 2.2 %collective-permute-start = (bf16[512,640]{1,0:T(8,128)(2,1)S(1)}, bf16[512,640]{1,0:T(8,128)(2,1)S(1)}, u32[]{:S(2)}, u32[]{:S(2)}) collective-permute-start(bf16[512,640]{1,0:T(8,128)(2,1)S(1)} %get-tuple-element.23.x0), channel_id=1, source_target_pairs={{0,3},{1,0},{2,1},{3,2},{4,7},{5,4},{6,5},{7,6},{8,11},{9,8},{10,9... | collective-permute-start | bytes 1966088 | tf_op jit(solution)/shard_map/ppermute | solution.py:204
  14.7 3.2 %collective-permute-start.8 = (bf16[512,640]{1,0:T(8,128)(2,1)S(1)}, bf16[512,640]{1,0:T(8,128)(2,1)S(1)}, u32[]{:S(2)}, u32[]{:S(2)}) collective-permute-start(bf16[512,640]{1,0:T(8,128)(2,1)S(1)} %get-tuple-element.24.x0), channel_id=1, source_target_pairs={{0,3},{1,0},{2,1},{3,2},{4,7},{5,4},{6,5},{7,6},{8,11},{9,8},{10,9... | collective-permute-start | bytes 1966088 | tf_op jit(solution)/shard_map/ppermute | solution.py:204
  18.0 12.1 %collective-permute-done.1.x3 = bf16[512,640]{1,0:T(8,128)(2,1)S(1)} collective-permute-done((bf16[512,640]{1,0:T(8,128)(2,1)S(1)}, bf16[512,640]{1,0:T(8,128)(2,1)S(1)}, u32[]{:S(2)}, u32[]{:S(2)}) %collective-permute-start.1) | collective-permute-done | bytes 655392 | tf_op jit(solution)/shard_map/ppermute | solution.py:204
  30.1 0.8 slice.104
  31.0 0.1 copy-done
  31.1 0.8 slice.105
  31.9 0.1 copy-done.2
  32.0 3.1 %collective-permute-start.3 = (bf16[256,640]{1,0:T(8,128)(2,1)}, bf16[256,640]{1,0:T(8,128)(2,1)}, u32[]{:S(2)}, u32[]{:S(2)}) collective-permute-start(bf16[256,640]{1,0:T(8,128)(2,1)} %slice.105), channel_id=1, source_target_pairs={{0,3},{1,0},{2,1},{3,2},{4,7},{5,4},{6,5},{7,6},{8,11},{9,8},{10,9... | collective-permute-start | bytes 983048 | tf_op jit(solution)/shard_map/ppermute | solution.py:204
  35.1 0.7 fusion.11
  35.9 8.3 %collective-permute-done.9.x3 = bf16[512,640]{1,0:T(8,128)(2,1)S(1)} collective-permute-done((bf16[512,640]{1,0:T(8,128)(2,1)S(1)}, bf16[512,640]{1,0:T(8,128)(2,1)S(1)}, u32[]{:S(2)}, u32[]{:S(2)}) %collective-permute-start.9) | collective-permute-done | bytes 655392 | tf_op jit(solution)/shard_map/ppermute | solution.py:204
  44.4 3.3 %collective-permute-start.11 = (bf16[256,640]{1,0:T(8,128)(2,1)S(1)}, bf16[256,640]{1,0:T(8,128)(2,1)S(1)}, u32[]{:S(2)}, u32[]{:S(2)}) collective-permute-start(bf16[256,640]{1,0:T(8,128)(2,1)S(1)} %slice.107), channel_id=1, source_target_pairs={{0,3},{1,0},{2,1},{3,2},{4,7},{5,4},{6,5},{7,6},{8,11},{9,8},{10,9... | collective-permute-start | bytes 983048 | tf_op jit(solution)/shard_map/ppermute | solution.py:204
  47.6 3.7 %collective-permute-done.2.x2t = bf16[256,640]{1,0:T(8,128)(2,1)} collective-permute-done((bf16[256,640]{1,0:T(8,128)(2,1)}, bf16[256,640]{1,0:T(8,128)(2,1)}, u32[]{:S(2)}, u32[]{:S(2)}) %collective-permute-start.2) | collective-permute-done | bytes 327712 | tf_op jit(solution)/shard_map/ppermute | solution.py:204
  51.3 0.9 copy-done.4
  52.2 30.6 %shard_map.121 = (f32[512,640]{1,0:T(8,128)}, bf16[512,640]{1,0:T(8,128)(2,1)S(1)}, bf16[256,640]{1,0:T(8,128)(2,1)S(1)}, bf16[256,640]{1,0:T(8,128)(2,1)S(1)}, bf16[512,640]{1,0:T(8,128)(2,1)S(1)}) custom-call(s32[1]{0:T(128)} %bitcast.place, bf16[512,640]{1,0:T(8,128)(2,1)S(1)} %get-tuple-element.23.x0, bf16[512,640]{1,0:T(8,128)(2,1)S(1)} %copy-done.3, ...), custom_call_target="tpu_custom_call" | custom-call | flops 6710886400 | bytes 23592960 | tf_op jit(solution)/shard_map/pallas_call | solution.py:167
  82.8 2.0 %collective-permute-start.4 = (bf16[256,640]{1,0:T(8,128)(2,1)S(1)}, bf16[256,640]{1,0:T(8,128)(2,1)S(1)}, u32[]{:S(2)}, u32[]{:S(2)}) collective-permute-start(bf16[256,640]{1,0:T(8,128)(2,1)S(1)} %get-tuple-element.15), channel_id=1, source_target_pairs={{0,1},{1,2},{2,3},{3,0},{4,5},{5,6},{6,7},{7,4},{8,9},{9,10},{10,1... | collective-permute-start | bytes 983048 | tf_op jit(solution)/shard_map/ppermute | solution.py:204
  84.9 1.4 collective-permute-start.6
  86.3 30.4 %shard_map.122 = (f32[512,640]{1,0:T(8,128)}, bf16[512,640]{1,0:T(8,128)(2,1)S(1)}, bf16[256,640]{1,0:T(8,128)(2,1)S(1)}, bf16[256,640]{1,0:T(8,128)(2,1)S(1)}, bf16[512,640]{1,0:T(8,128)(2,1)S(1)}) custom-call(s32[1]{0:T(128)} %bitcast.place, bf16[512,640]{1,0:T(8,128)(2,1)S(1)} %get-tuple-element.24.x0, bf16[512,640]{1,0:T(8,128)(2,1)S(1)} %collective-permute-done.8.x1, ...), custom_call_target="tpu_custom_call" | custom-call | flops 6710886400 | bytes 23592960 | tf_op jit(solution)/shard_map/pallas_call | solution.py:167
  116.7 0.6 collective-permute-start.12
  117.3 2.6 %collective-permute-start.14 = (bf16[256,640]{1,0:T(8,128)(2,1)S(1)}, bf16[256,640]{1,0:T(8,128)(2,1)S(1)}, u32[]{:S(2)}, u32[]{:S(2)}) collective-permute-start(bf16[256,640]{1,0:T(8,128)(2,1)S(1)} %get-tuple-element.22), channel_id=1, source_target_pairs={{0,3},{1,0},{2,1},{3,2},{4,7},{5,4},{6,5},{7,6},{8,11},{9,8},{10,9... | collective-permute-start | bytes 983048 | tf_op jit(solution)/shard_map/ppermute | solution.py:204
  120.0 0.1 fusion.7
  120.1 0.9 pad_maximum_fusion.3
  121.0 0.8 collective-permute-start.7
  121.8 0.1 slice_add_fusion.3
  121.9 0.9 pad_maximum_fusion.2
  122.8 1.2 collective-permute-start.5
  124.0 4.1 %collective-permute-done.14 = bf16[256,640]{1,0:T(8,128)(2,1)S(1)} collective-permute-done((bf16[256,640]{1,0:T(8,128)(2,1)S(1)}, bf16[256,640]{1,0:T(8,128)(2,1)S(1)}, u32[]{:S(2)}, u32[]{:S(2)}) %collective-permute-start.14) | collective-permute-done | bytes 327712 | tf_op jit(solution)/shard_map/ppermute | solution.py:204
  128.2 0.9 pad_maximum_fusion.5
  129.1 3.7 %collective-permute-start.15 = (bf16[512,640]{1,0:T(8,128)(2,1)}, bf16[512,640]{1,0:T(8,128)(2,1)}, u32[]{:S(2)}, u32[]{:S(2)}) collective-permute-start(bf16[512,640]{1,0:T(8,128)(2,1)} %pad_maximum_fusion.5), channel_id=1, source_target_pairs={{0,3},{1,0},{2,1},{3,2},{4,7},{5,4},{6,5},{7,6},{8,11},{9,8},{10,9... | collective-permute-start | bytes 1966088 | tf_op jit(solution)/shard_map/ppermute | solution.py:204
  132.9 0.1 collective-permute-start.13
  133.0 0.7 copy-done.8
  133.8 0.1 copy-done.10
  133.9 0.2 multiply_convert_fusion.1
  134.0 0.6 reshape.28
  134.7 0.6 reshape.29
  135.3 0.5 pad_maximum_fusion.1
  135.8 1.6 copy.16
  137.5 7.8 %all-to-all-start = ((bf16[32,64,160]{2,1,0:T(8,128)(2,1)}), bf16[32,64,160]{2,1,0:T(8,128)(2,1)S(1)}, u32[]{:S(2)}, u32[]{:S(2)}) async-start(bf16[32,64,160]{2,1,0:T(8,128)(2,1)} %copy.16), calls=%async_computation | async-start | bytes 2097152 | tf_op jit(solution)/shard_map/all_to_all | solution.py:248
  145.3 1.6 add_convert_fusion.1
  146.9 6.0 %collective-permute-done.15 = bf16[512,640]{1,0:T(8,128)(2,1)} collective-permute-done((bf16[512,640]{1,0:T(8,128)(2,1)}, bf16[512,640]{1,0:T(8,128)(2,1)}, u32[]{:S(2)}, u32[]{:S(2)}) %collective-permute-start.15) | collective-permute-done | bytes 655392 | tf_op jit(solution)/shard_map/ppermute | solution.py:204
  152.8 0.7 collective-permute-done.13
  153.6 1.6 add_convert_fusion
  155.1 1.2 pad_maximum_fusion
  156.3 5.0 %all-to-all-done = bf16[32,64,160]{2,1,0:T(8,128)(2,1)S(1)} async-done(((bf16[32,64,160]{2,1,0:T(8,128)(2,1)}), bf16[32,64,160]{2,1,0:T(8,128)(2,1)S(1)}, u32[]{:S(2)}, u32[]{:S(2)}) %all-to-all-start) | async-done | bytes 655392 | tf_op jit(solution)/shard_map/all_to_all | solution.py:248
  161.3 4.1 %fusion.2 = f32[80,1280]{1,0:T(8,128)} fusion(bf16[2048,2560]{1,0:T(8,128)(2,1)} %all-gather.2.cloned.1.call-done, bf16[2048,160]{1,0:T(8,128)(2,1)S(1)} %bitcast.4), kind=kOutput, calls=%fused_computation.2 | convolution fusion | flops 419430400 | bytes 6176768 | tf_op jit(solution)/shard_map/dot_general | solution.py:252
  165.4 4.3 %fusion = f32[1280,80]{0,1:T(8,128)} fusion(bf16[2048,2560]{1,0:T(8,128)(2,1)} %all-gather.2.cloned.1.call-done, bf16[2048,160]{1,0:T(8,128)(2,1)S(1)} %bitcast.5), kind=kOutput, calls=%fused_computation | convolution fusion | flops 419430400 | bytes 6176768 | tf_op jit(solution)/shard_map/dot_general | solution.py:255
  (52 shorter events, 0.5 us)
Async XLA Ops:
  7.2 154.2 %all-gather.2.cloned.1.call-start = ((), (), s32[]{:S(2)}) async-start(), calls=%async_computation.1 | async-start | bytes 10813440 | tf_op jit(solution)/shard_map/all_gather | solution.py:235
  9.0 8.9 %copy-start.7 = (bf16[64,2560]{1,0:T(8,128)(2,1)S(1)}, bf16[64,2560]{1,0:T(8,128)(2,1)}, u32[]{:S(2)}) copy-start(bf16[64,2560]{1,0:T(8,128)(2,1)} %param.18) | copy-start | bytes 983044
  9.0 8.9 %copy-start.9 = (bf16[64,2560]{1,0:T(8,128)(2,1)S(1)}, bf16[64,2560]{1,0:T(8,128)(2,1)}, u32[]{:S(2)}) copy-start(bf16[64,2560]{1,0:T(8,128)(2,1)} %param.15) | copy-start | bytes 983044
  10.5 19.7 %collective-permute-start.1 = (bf16[512,640]{1,0:T(8,128)(2,1)S(1)}, bf16[512,640]{1,0:T(8,128)(2,1)S(1)}, u32[]{:S(2)}, u32[]{:S(2)}) collective-permute-start(bf16[512,640]{1,0:T(8,128)(2,1)S(1)} %get-tuple-element.23.x0), channel_id=1, source_target_pairs={{0,1},{1,2},{2,3},{3,0},{4,5},{5,6},{6,7},{7,4},{8,9},{9,10},{10,1... | collective-permute-start | bytes 1966088 | tf_op jit(solution)/shard_map/ppermute | solution.py:204
  12.5 18.5 %collective-permute-start = (bf16[512,640]{1,0:T(8,128)(2,1)S(1)}, bf16[512,640]{1,0:T(8,128)(2,1)S(1)}, u32[]{:S(2)}, u32[]{:S(2)}) collective-permute-start(bf16[512,640]{1,0:T(8,128)(2,1)S(1)} %get-tuple-element.23.x0), channel_id=1, source_target_pairs={{0,3},{1,0},{2,1},{3,2},{4,7},{5,4},{6,5},{7,6},{8,11},{9,8},{10,9... | collective-permute-start | bytes 1966088 | tf_op jit(solution)/shard_map/ppermute | solution.py:204
  14.7 20.5 %copy-start.11 = (bf16[64,1280]{1,0:T(8,128)(2,1)S(1)}, bf16[64,1280]{1,0:T(8,128)(2,1)}, u32[]{:S(2)}) copy-start(bf16[64,1280]{1,0:T(8,128)(2,1)} %param.17) | copy-start | bytes 491524
  14.7 20.5 %copy-start.12 = (bf16[64,1280]{1,0:T(8,128)(2,1)S(1)}, bf16[64,1280]{1,0:T(8,128)(2,1)}, u32[]{:S(2)}) copy-start(bf16[64,1280]{1,0:T(8,128)(2,1)} %param.16) | copy-start | bytes 491524
  14.7 29.5 %collective-permute-start.9 = (bf16[512,640]{1,0:T(8,128)(2,1)S(1)}, bf16[512,640]{1,0:T(8,128)(2,1)S(1)}, u32[]{:S(2)}, u32[]{:S(2)}) collective-permute-start(bf16[512,640]{1,0:T(8,128)(2,1)S(1)} %get-tuple-element.24.x0), channel_id=1, source_target_pairs={{0,1},{1,2},{2,3},{3,0},{4,5},{5,6},{6,7},{7,4},{8,9},{9,10},{10,1... | collective-permute-start | bytes 1966088 | tf_op jit(solution)/shard_map/ppermute | solution.py:204
  14.7 29.6 %collective-permute-start.8 = (bf16[512,640]{1,0:T(8,128)(2,1)S(1)}, bf16[512,640]{1,0:T(8,128)(2,1)S(1)}, u32[]{:S(2)}, u32[]{:S(2)}) collective-permute-start(bf16[512,640]{1,0:T(8,128)(2,1)S(1)} %get-tuple-element.24.x0), channel_id=1, source_target_pairs={{0,3},{1,0},{2,1},{3,2},{4,7},{5,4},{6,5},{7,6},{8,11},{9,8},{10,9... | collective-permute-start | bytes 1966088 | tf_op jit(solution)/shard_map/ppermute | solution.py:204
  18.0 17.8 %copy-start.13 = (f32[2560]{0:T(1024)S(1)}, f32[2560]{0:T(1024)}, u32[]{:S(2)}) copy-start(f32[2560]{0:T(1024)} %param.11) | copy-start | bytes 30724
  18.0 17.9 %copy-start.14 = (f32[2560]{0:T(1024)S(1)}, f32[2560]{0:T(1024)}, u32[]{:S(2)}) copy-start(f32[2560]{0:T(1024)} %param.12) | copy-start | bytes 30724
  18.0 17.9 %copy-start.15 = (s32[64]{0:T(128)S(1)}, s32[64]{0:T(128)}, u32[]{:S(2)}) copy-start(s32[64]{0:T(128)} %param.19) | copy-start | bytes 772
  30.1 1.0 copy-start
  31.0 20.4 %collective-permute-start.2 = (bf16[256,640]{1,0:T(8,128)(2,1)}, bf16[256,640]{1,0:T(8,128)(2,1)}, u32[]{:S(2)}, u32[]{:S(2)}) collective-permute-start(bf16[256,640]{1,0:T(8,128)(2,1)} %slice.104), channel_id=1, source_target_pairs={{0,1},{1,2},{2,3},{3,0},{4,5},{5,6},{6,7},{7,4},{8,9},{9,10},{10,1... | collective-permute-start | bytes 983048 | tf_op jit(solution)/shard_map/ppermute | solution.py:204
  31.1 0.9 copy-start.2
  32.0 19.3 %collective-permute-start.3 = (bf16[256,640]{1,0:T(8,128)(2,1)}, bf16[256,640]{1,0:T(8,128)(2,1)}, u32[]{:S(2)}, u32[]{:S(2)}) collective-permute-start(bf16[256,640]{1,0:T(8,128)(2,1)} %slice.105), channel_id=1, source_target_pairs={{0,3},{1,0},{2,1},{3,2},{4,7},{5,4},{6,5},{7,6},{8,11},{9,8},{10,9... | collective-permute-start | bytes 983048 | tf_op jit(solution)/shard_map/ppermute | solution.py:204
  35.8 15.5 %copy-start.1 = (bf16[512,640]{1,0:T(8,128)(2,1)S(1)}, bf16[512,640]{1,0:T(8,128)(2,1)}, u32[]{:S(2)}) copy-start(bf16[512,640]{1,0:T(8,128)(2,1)} %copy-done) | copy-start | bytes 1966084
  35.8 15.5 %copy-start.3 = (bf16[512,640]{1,0:T(8,128)(2,1)S(1)}, bf16[512,640]{1,0:T(8,128)(2,1)}, u32[]{:S(2)}) copy-start(bf16[512,640]{1,0:T(8,128)(2,1)} %copy-done.2) | copy-start | bytes 1966084
  44.2 42.1 %collective-permute-start.10 = (bf16[256,640]{1,0:T(8,128)(2,1)S(1)}, bf16[256,640]{1,0:T(8,128)(2,1)S(1)}, u32[]{:S(2)}, u32[]{:S(2)}) collective-permute-start(bf16[256,640]{1,0:T(8,128)(2,1)S(1)} %slice.106), channel_id=1, source_target_pairs={{0,1},{1,2},{2,3},{3,0},{4,5},{5,6},{6,7},{7,4},{8,9},{9,10},{10,1... | collective-permute-start | bytes 983048 | tf_op jit(solution)/shard_map/ppermute | solution.py:204
  44.4 42.0 %collective-permute-start.11 = (bf16[256,640]{1,0:T(8,128)(2,1)S(1)}, bf16[256,640]{1,0:T(8,128)(2,1)S(1)}, u32[]{:S(2)}, u32[]{:S(2)}) collective-permute-start(bf16[256,640]{1,0:T(8,128)(2,1)S(1)} %slice.107), channel_id=1, source_target_pairs={{0,3},{1,0},{2,1},{3,2},{4,7},{5,4},{6,5},{7,6},{8,11},{9,8},{10,9... | collective-permute-start | bytes 983048 | tf_op jit(solution)/shard_map/ppermute | solution.py:204
  51.3 0.9 copy-start.4
  82.8 39.0 %collective-permute-start.4 = (bf16[256,640]{1,0:T(8,128)(2,1)S(1)}, bf16[256,640]{1,0:T(8,128)(2,1)S(1)}, u32[]{:S(2)}, u32[]{:S(2)}) collective-permute-start(bf16[256,640]{1,0:T(8,128)(2,1)S(1)} %get-tuple-element.15), channel_id=1, source_target_pairs={{0,1},{1,2},{2,3},{3,0},{4,5},{5,6},{6,7},{7,4},{8,9},{9,10},{10,1... | collective-permute-start | bytes 983048 | tf_op jit(solution)/shard_map/ppermute | solution.py:204
  84.9 35.1 %collective-permute-start.6 = (bf16[256,640]{1,0:T(8,128)(2,1)S(1)}, bf16[256,640]{1,0:T(8,128)(2,1)S(1)}, u32[]{:S(2)}, u32[]{:S(2)}) collective-permute-start(bf16[256,640]{1,0:T(8,128)(2,1)S(1)} %get-tuple-element.17), channel_id=1, source_target_pairs={{0,3},{1,0},{2,1},{3,2},{4,7},{5,4},{6,5},{7,6},{8,11},{9,8},{10,9... | collective-permute-start | bytes 983048 | tf_op jit(solution)/shard_map/ppermute | solution.py:204
  116.7 16.1 %collective-permute-start.12 = (bf16[256,640]{1,0:T(8,128)(2,1)S(1)}, bf16[256,640]{1,0:T(8,128)(2,1)S(1)}, u32[]{:S(2)}, u32[]{:S(2)}) collective-permute-start(bf16[256,640]{1,0:T(8,128)(2,1)S(1)} %get-tuple-element.20), channel_id=1, source_target_pairs={{0,1},{1,2},{2,3},{3,0},{4,5},{5,6},{6,7},{7,4},{8,9},{9,10},{10,1... | collective-permute-start | bytes 983048 | tf_op jit(solution)/shard_map/ppermute | solution.py:204
  117.3 10.8 %collective-permute-start.14 = (bf16[256,640]{1,0:T(8,128)(2,1)S(1)}, bf16[256,640]{1,0:T(8,128)(2,1)S(1)}, u32[]{:S(2)}, u32[]{:S(2)}) collective-permute-start(bf16[256,640]{1,0:T(8,128)(2,1)S(1)} %get-tuple-element.22), channel_id=1, source_target_pairs={{0,3},{1,0},{2,1},{3,2},{4,7},{5,4},{6,5},{7,6},{8,11},{9,8},{10,9... | collective-permute-start | bytes 983048 | tf_op jit(solution)/shard_map/ppermute | solution.py:204
  121.0 24.2 %collective-permute-start.7 = (bf16[512,640]{1,0:T(8,128)(2,1)}, bf16[512,640]{1,0:T(8,128)(2,1)}, u32[]{:S(2)}, u32[]{:S(2)}) collective-permute-start(bf16[512,640]{1,0:T(8,128)(2,1)} %pad_maximum_fusion.3), channel_id=1, source_target_pairs={{0,3},{1,0},{2,1},{3,2},{4,7},{5,4},{6,5},{7,6},{8,11},{9,8},{10,9... | collective-permute-start | bytes 1966088 | tf_op jit(solution)/shard_map/ppermute | solution.py:204
  122.8 22.4 %collective-permute-start.5 = (bf16[512,640]{1,0:T(8,128)(2,1)}, bf16[512,640]{1,0:T(8,128)(2,1)}, u32[]{:S(2)}, u32[]{:S(2)}) collective-permute-start(bf16[512,640]{1,0:T(8,128)(2,1)} %pad_maximum_fusion.2), channel_id=1, source_target_pairs={{0,1},{1,2},{2,3},{3,0},{4,5},{5,6},{6,7},{7,4},{8,9},{9,10},{10,1... | collective-permute-start | bytes 1966088 | tf_op jit(solution)/shard_map/ppermute | solution.py:204
  129.1 23.7 %collective-permute-start.15 = (bf16[512,640]{1,0:T(8,128)(2,1)}, bf16[512,640]{1,0:T(8,128)(2,1)}, u32[]{:S(2)}, u32[]{:S(2)}) collective-permute-start(bf16[512,640]{1,0:T(8,128)(2,1)} %pad_maximum_fusion.5), channel_id=1, source_target_pairs={{0,3},{1,0},{2,1},{3,2},{4,7},{5,4},{6,5},{7,6},{8,11},{9,8},{10,9... | collective-permute-start | bytes 1966088 | tf_op jit(solution)/shard_map/ppermute | solution.py:204
  132.8 1.0 copy-start.8
  132.8 1.1 copy-start.10
  132.9 20.6 %collective-permute-start.13 = (bf16[512,640]{1,0:T(8,128)(2,1)S(1)}, bf16[512,640]{1,0:T(8,128)(2,1)}, u32[]{:S(2)}, u32[]{:S(2)}) collective-permute-start(bf16[512,640]{1,0:T(8,128)(2,1)S(1)} %pad_maximum_fusion.4), channel_id=1, source_target_pairs={{0,1},{1,2},{2,3},{3,0},{4,5},{5,6},{6,7},{7,4},{8,9},{9,10},{10,1... | collective-permute-start | bytes 1966088 | tf_op jit(solution)/shard_map/ppermute | solution.py:204
  137.5 7.8 %copy-start.5 = (f32[512,640]{1,0:T(8,128)S(1)}, f32[512,640]{1,0:T(8,128)}, u32[]{:S(2)}) copy-start(f32[512,640]{1,0:T(8,128)} %get-tuple-element.13) | copy-start | bytes 3932164
  137.5 23.9 %all-to-all-start = ((bf16[32,64,160]{2,1,0:T(8,128)(2,1)}), bf16[32,64,160]{2,1,0:T(8,128)(2,1)S(1)}, u32[]{:S(2)}, u32[]{:S(2)}) async-start(bf16[32,64,160]{2,1,0:T(8,128)(2,1)} %copy.16), calls=%async_computation | async-start | bytes 2097152 | tf_op jit(solution)/shard_map/all_to_all | solution.py:248
  145.3 8.3 %copy-start.6 = (f32[512,640]{1,0:T(8,128)S(1)}, f32[512,640]{1,0:T(8,128)}, u32[]{:S(2)}) copy-start(f32[512,640]{1,0:T(8,128)} %get-tuple-element.18) | copy-start | bytes 3932164
Sparse Core Ops, SparseCore 0:
  10.2 60.0 all-gather.1

commit v2 on v1

v2 whole, which is shorter than its diff:
```python
import functools
import math

import jax
import jax.numpy as jnp
from jax import lax
from jax.experimental import pallas as pl
from jax.experimental.pallas import tpu as pltpu
from jax.sharding import PartitionSpec as P

D = 2560
FFW = 5120
PROMPT = 16
EPSILON = 1e-05
SIGMA = 0.5
KEY_FACTOR = SIGMA / math.sqrt(D)
VALUE_FACTOR = SIGMA / math.sqrt(FFW)
CHUNKS = 2
LN_ROWS = 64
F_BLOCK = 640


def mm(a, b):
    return jnp.dot(a, b, preferred_element_type=jnp.float32)


def per_member(array, rows):
    members, width = array.shape
    wide = jnp.broadcast_to(array.astype(jnp.float32)[:, None, :], (members, PROMPT, width))
    return wide.reshape(rows, width)


def ffn_kernel(
    place,
    x0,
    x1t,
    x2t,
    x3t,
    x1b,
    x2b,
    x3b,
    keep,
    pass_on,
    kw_hbm,
    vw_hbm,
    kl,
    kr,
    vl,
    vr,
    o0,
    o1t,
    o2t,
    o3t,
    o1b,
    o2b,
    o3b,
    kw,
    vw,
    mixed,
    hidden,
    kdots,
    sems,
):
    rows, width = x0.shape
    half = rows // 2
    units = kw.shape[1]
    z = place[0]
    key_copy = pltpu.make_async_copy(kw_hbm, kw, sems.at[0])
    value_copy = pltpu.make_async_copy(vw_hbm, vw, sems.at[1])
    key_copy.start()
    value_copy.start()

    def column(k):
        return pl.multiple_of(lax.rem(z + k, 4) * width, 128)

    def normalise(i, sub, sources, offset):
        first = pl.multiple_of(i * 128 + sub * LN_ROWS, LN_ROWS)
        span = pl.ds(first, LN_ROWS)
        from_half = pl.ds(pl.multiple_of(first - offset, LN_ROWS), LN_ROWS)
        group = pl.ds(pl.multiple_of(i * 8, 8), 8)
        ours = slice(sub * LN_ROWS // PROMPT, (sub + 1) * LN_ROWS // PROMPT)
        pieces = [x0[span, :]] + [source[from_half, :] for source in sources]
        pieces = [p.astype(jnp.float32) for p in pieces]
        total = sum(jnp.sum(p, axis=-1, keepdims=True) for p in pieces)
        centre = total * (1.0 / D)
        pieces = [p - centre for p in pieces]
        spread = sum(jnp.sum(p * p, axis=-1, keepdims=True) for p in pieces) * (1.0 / D)
        scale = lax.rsqrt(spread + EPSILON)
        later = lax.broadcasted_iota(jnp.int32, (LN_ROWS, 1), 0) % PROMPT != 0
        dots = 0.0
        for k, piece in enumerate(pieces):
            cols = pl.ds(column(k), width)
            normed = piece * scale
            before = pltpu.roll(normed * pass_on[:, cols], 1, 0)
            piece = normed * keep[:, cols] + jnp.where(later, before, 0.0)
            piece = piece.astype(jnp.bfloat16)
            mixed[span, cols] = piece
            left = per_member(kl[group, cols][ours], LN_ROWS)
            dots += jnp.sum(piece.astype(jnp.float32) * left, axis=-1, keepdims=True)
        kdots[span, :] = dots * KEY_FACTOR

    def normalise_group(sources, offset, i, carry):
        for sub in range(128 // LN_ROWS):
            normalise(i, sub, sources, offset)
        return carry

    top = functools.partial(normalise_group, (x1t, x2t, x3t), 0)
    bottom = functools.partial(normalise_group, (x1b, x2b, x3b), half)
    lax.fori_loop(0, half // 128, top, 0)
    lax.fori_loop(half // 128, rows // 128, bottom, 0)

    key_copy.wait()
    vdots = 0.0
    for first in range(0, units, F_BLOCK):
        cols = pl.ds(first, F_BLOCK)
        preact = mm(mixed[...], kw[:, cols]) + kdots[...] * per_member(kr[:, cols], rows)
        block = jnp.square(jnp.maximum(preact, 0.0)).astype(jnp.bfloat16)
        hidden[:, cols] = block
        left = per_member(vl[:, cols], rows)
        vdots += jnp.sum(block.astype(jnp.float32) * left, axis=-1, keepdims=True)
    vdots = vdots * VALUE_FACTOR

    value_copy.wait()

    def piece(k):
        cols = pl.ds(column(k), width)
        return mm(hidden[...], vw[:, cols]) + vdots * per_member(vr[:, cols], rows)

    for k, top, bottom in ((2, o2t, o2b), (1, o1t, o1b), (3, o3t, o3b)):
        sums = piece(k).astype(jnp.bfloat16)
        top[...] = sums[:half]
        bottom[...] = sums[half:]
    o0[...] = piece(0)


def ffn(place, pieces, gain, mix, kw, vw, kl, kr, vl, vr):
    rows, width = pieces[0].shape
    units = kr.shape[1]
    half = rows // 2
    vmem = pl.BlockSpec(memory_space=pltpu.VMEM)
    hbm = pl.BlockSpec(memory_space=pl.ANY)
    part = jax.ShapeDtypeStruct((half, width), jnp.bfloat16)
    out_shapes = [jax.ShapeDtypeStruct((rows, width), jnp.float32)] + [part] * 6
    return pl.pallas_call(
        ffn_kernel,
        out_shape=out_shapes,
        in_specs=[pl.BlockSpec(memory_space=pltpu.SMEM)] + [vmem] * 9 + [hbm] * 2 + [vmem] * 4,
        out_specs=[vmem] * 7,
        scratch_shapes=[
            pltpu.VMEM((D, units), jnp.bfloat16),
            pltpu.VMEM((units, D), jnp.bfloat16),
            pltpu.VMEM((rows, D), jnp.bfloat16),
            pltpu.VMEM((rows, units), jnp.bfloat16),
            pltpu.VMEM((rows, 1), jnp.float32),
            pltpu.SemaphoreType.DMA((2,)),
        ],
        compiler_params=pltpu.CompilerParams(vmem_limit_bytes=50 * 1024 * 1024),
        cost_estimate=pl.CostEstimate(
            flops=4 * rows * D * units,
            bytes_accessed=4 * D * units + 8 * rows * D,
            transcendentals=rows,
        ),
    )(place, *pieces, gain * (1.0 - mix), gain * mix, kw, vw, kl.astype(jnp.float32), kr, vl, vr)


def shift(array, by):
    return lax.ppermute(array, "tensor", [(i, (i + by) % 4) for i in range(4)])


def local(
    layer_input,
    norm_gain,
    shift_mix,
    key_weight,
    value_weight,
    key_left,
    key_right,
    value_left,
    value_right,
    fitness_rank,
):
    members = key_left.shape[0]
    devices = lax.axis_size("dp")
    hidden = key_weight.shape[1]
    place = lax.axis_index("tensor").astype(jnp.int32).reshape(1)
    gain, mix = norm_gain.reshape(1, D), shift_mix.reshape(1, D)
    rows = layer_input.shape[0] // CHUNKS
    half = rows // 2

    gathered = []
    for c in range(CHUNKS):
        own = layer_input[c * rows : (c + 1) * rows]
        if gathered:
            own, gathered[-1][4], gathered[-1][1] = lax.optimization_barrier(
                (own, gathered[-1][4], gathered[-1][1])
            )
        top, bottom = own[:half], own[half:]
        left_top, right_bottom = shift(top, 1), shift(bottom, -1)
        right_top, left_bottom = shift(top, -1), shift(bottom, 1)
        far_top, far_bottom = shift(left_top, 1), shift(right_bottom, -1)
        gathered.append(
            [own, right_top, far_top, left_top, right_bottom, far_bottom, left_bottom]
        )

    total_members = members * devices
    member_weight = (fitness_rank.astype(jnp.float32) / (total_members - 1) - 0.5) / math.sqrt(
        total_members
    )

    def scaled(factor):
        product = (factor.astype(jnp.float32) * member_weight[:, None]).astype(jnp.bfloat16)
        return product.reshape(members, devices, -1).transpose(1, 0, 2)

    lefts = jnp.concatenate([scaled(key_left), scaled(value_right)], axis=2)
    lefts = lax.all_to_all(lefts, "dp", split_axis=0, concat_axis=0, tiled=True)
    place_later, lefts = lax.optimization_barrier((place, lefts))
    lefts = lefts.reshape(total_members, -1)
    rights = lax.all_gather(
        jnp.concatenate([key_right, value_left], axis=1), "dp", axis=0, tiled=True
    )
    share = lefts.shape[1] // 2
    contract = (((0,), (0,)), ((), ()))
    key_update = lax.dot_general(
        lefts[:, :share], rights[:, :hidden], contract, preferred_element_type=jnp.float32
    )
    value_update = lax.dot_general(
        rights[:, hidden:], lefts[:, share:], contract, preferred_element_type=jnp.float32
    )

    outputs = []
    for c in range(CHUNKS):
        part = slice(c * rows // PROMPT, (c + 1) * rows // PROMPT)
        own, right_top, far_top, left_top, right_bottom, far_bottom, left_bottom = ffn(
            place if c == 0 else place_later,
            gathered[c],
            gain,
            mix,
            key_weight,
            value_weight,
            key_left[part],
            key_right[part],
            value_left[part],
            value_right[part],
        )
        via_left, via_right = shift(far_top, 1), shift(far_bottom, -1)
        from_left_bottom, from_right_top = shift(right_bottom, 1), shift(left_top, -1)
        from_left_top = shift(right_top + via_left, 1)
        from_right_bottom = shift(left_bottom + via_right, -1)
        if c == CHUNKS - 1:
            own, key_update, value_update = lax.optimization_barrier(
                (own, key_update, value_update)
            )
        for mine, one, two in (
            (own[:half], from_left_top, from_right_top),
            (own[half:], from_left_bottom, from_right_bottom),
        ):
            total = mine + (one.astype(jnp.float32) + two.astype(jnp.float32))
            outputs.append(total.astype(jnp.bfloat16))
    return (jnp.concatenate(outputs, axis=0), key_update, value_update)


def solution(mesh):
    placed = (
        P("dp", "tensor"),
        P(),
        P(),
        P(None, "tensor"),
        P("tensor", None),
        P("dp", None),
        P("dp", "tensor"),
        P("dp", "tensor"),
        P("dp", None),
        P("dp"),
    )
    return jax.shard_map(
        local,
        mesh=mesh,
        in_specs=placed,
        out_specs=(P("dp", "tensor"), P("dp", "tensor"), P("tensor", "dp")),
        check_vma=False,
    )
```

time: 179 us -> 134 us (0.75); the launches traced: 177 us -> 133 us
  Pallas kernels: 61 us -> 29.7 us
  waiting for transfers between devices: 40.1 us -> 31.1 us
  other arithmetic: 9.79 us -> 6.98 us
    pallas_call x2, Pallas kernels: 61 us -> 29.7 us  [ffn(): pl.pallas_call(ffn_kernel, out_shape=out_shapes, in_specs=[pl.BlockSpec(m...]
    ppermute x16 -> x24, waiting for transfers between devices: 35 us -> 22 us  [shift(): return lax.ppermute(array, 'tensor', [(i, (i + by) % 4) for i in range(4)])]
    all_to_all x1, waiting for transfers between devices: 5.04 us -> 9.15 us  [local(): lefts = lax.all_to_all(lefts, 'dp', split_axis=0, concat_axis=0, tiled=True)]
    concatenate x4 -> x0, other arithmetic: 2.77 us -> none  [the longest x2 1.8 us: local(): left = jnp.concatenate([left[:half], left[half:] + via_right], axis=0)]
    unnamed x32 -> x20, local copies, waits for them, and re-layouts: 2.07 us -> 0.05 us
    ppermute x16 -> x24, starting transfers between devices: 26.4 us -> 27 us  [shift(): return lax.ppermute(array, 'tensor', [(i, (i + by) % 4) for i in range(4)])]
  transfers between devices with their start and end apart: 18 -> 26, of which waited for: 7 -> 7; matrix products, arithmetic and copies ran while one was open for 8% -> 15% of each run, Pallas kernels for 35% -> 22%
where the time goes in v2:
time: 134 us; the launch traced here: 133 us
  starting transfers between devices  34.7 us (26%)
  waiting for transfers between devices  31.1 us (23%)
  Pallas kernels  29.7 us (22%)
  between operations  14.3 us (11%)
  matrix products  8.9 us (7%)
  local copies, waits for them, and re-layouts  7.74 us (6%)
  other arithmetic  6.98 us (5%)
    pallas_call x2, Pallas kernels, ffn(): pl.pallas_call(ffn_kernel, out_shape=out_shapes, in_specs=[pl.BlockSpec(m...  29.7 us
    ppermute x24, starting transfers between devices, shift(): return lax.ppermute(array, 'tensor', [(i, (i + by) % 4) for i in range(4)])  27 us
    ppermute x24, waiting for transfers between devices, shift(): return lax.ppermute(array, 'tensor', [(i, (i + by) % 4) for i in range(4)])  22 us
    all_to_all x1, waiting for transfers between devices, local(): lefts = lax.all_to_all(lefts, 'dp', split_axis=0, concat_axis=0, tiled=True)  9.15 us
    all_to_all x1, starting transfers between devices, local(): lefts = lax.all_to_all(lefts, 'dp', split_axis=0, concat_axis=0, tiled=True)  7.68 us
    dot_general x1, matrix products, local(): lax.dot_general(rights[:, hidden:], lefts[:, share:], contract, preferred...  4.62 us
    dot_general x1, matrix products, local(): lax.dot_general(lefts[:, :share], rights[:, :hidden], contract, preferred...  4.28 us
    slice x2, local copies, waits for them, and re-layouts, local(): top, bottom = (own[:half], own[half:])  2.94 us
  transfers between devices with their start and end apart: 26, of which 7 were waited for; matrix products, arithmetic and copies ran while one was open for 15% of the time, Pallas kernels for 22%

profile of v2, /device:TPU:2, one launch (start us, length us, event | category | flops | bytes accessed | tf_op | source)
XLA Modules:
  0.0 133.4 jit_solution(6354870332050381015)
XLA Ops:
  7.2 1.7 %pad_maximum_fusion.2 = bf16[64,2560]{1,0:T(8,128)(2,1)} fusion(bf16[64,1280]{1,0:T(8,128)(2,1)} %param.17, bf16[64,1280]{1,0:T(8,128)(2,1)} %param.16), kind=kLoop, calls=%fused_computation.14 | loop fusion | flops 655360 | bytes 655360 | tf_op jit(solution)/shard_map/concatenate | solution.py:219
  9.0 2.0 %fusion.7 = (bf16[256,640]{1,0:T(8,128)(2,1)}, bf16[256,640]{1,0:T(8,128)(2,1)}) fusion(bf16[1024,640]{1,0:T(8,128)(2,1)} %param.10), kind=kLoop, calls=%fused_computation.20 | loop fusion | bytes 1310720 | tf_op jit(solution)/shard_map/slice | solution.py:197
  10.9 1.9 %collective-permute-start.2 = (bf16[256,640]{1,0:T(8,128)(2,1)}, bf16[256,640]{1,0:T(8,128)(2,1)S(1)}, u32[]{:S(2)}, u32[]{:S(2)}) collective-permute-start(bf16[256,640]{1,0:T(8,128)(2,1)} %get-tuple-element.53), channel_id=1, source_target_pairs={{0,1},{1,2},{2,3},{3,0},{4,5},{5,6},{6,7},{7,4},{8,9},{9,10},{10,1... | collective-permute-start | bytes 983048 | tf_op jit(solution)/shard_map/ppermute | solution.py:167
  12.9 2.1 %collective-permute-start.1 = (bf16[256,640]{1,0:T(8,128)(2,1)}, bf16[256,640]{1,0:T(8,128)(2,1)S(1)}, u32[]{:S(2)}, u32[]{:S(2)}) collective-permute-start(bf16[256,640]{1,0:T(8,128)(2,1)} %get-tuple-element.53), channel_id=1, source_target_pairs={{0,3},{1,0},{2,1},{3,2},{4,7},{5,4},{6,5},{7,6},{8,11},{9,8},{10,9... | collective-permute-start | bytes 983048 | tf_op jit(solution)/shard_map/ppermute | solution.py:167
  15.0 3.2 %collective-permute-start = (bf16[256,640]{1,0:T(8,128)(2,1)}, bf16[256,640]{1,0:T(8,128)(2,1)S(1)}, u32[]{:S(2)}, u32[]{:S(2)}) collective-permute-start(bf16[256,640]{1,0:T(8,128)(2,1)} %get-tuple-element.54), channel_id=1, source_target_pairs={{0,3},{1,0},{2,1},{3,2},{4,7},{5,4},{6,5},{7,6},{8,11},{9,8},{10,9... | collective-permute-start | bytes 983048 | tf_op jit(solution)/shard_map/ppermute | solution.py:167
  18.2 0.7 add_multiply_fusion
  18.9 1.2 multiply_convert_fusion.1
  20.1 0.6 reshape.25
  20.8 0.6 reshape.26
  21.4 0.5 pad_maximum_fusion.1
  21.9 1.6 %copy.16 = bf16[32,64,160]{2,1,0:T(8,128)(2,1)} copy(bf16[32,64,160]{2,0,1:T(8,128)(2,1)S(1)} %pad_maximum_fusion.1) | data formatting | bytes 1310720 | tf_op jit(solution)/shard_map/concatenate | solution.py:214
  23.5 7.7 %all-to-all-start = ((bf16[32,64,160]{2,1,0:T(8,128)(2,1)}), bf16[32,64,160]{2,1,0:T(8,128)(2,1)}, u32[]{:S(2)}, u32[]{:S(2)}) async-start(bf16[32,64,160]{2,1,0:T(8,128)(2,1)} %copy.16), calls=%async_computation | async-start | bytes 2097152 | tf_op jit(solution)/shard_map/all_to_all | solution.py:215
  31.2 0.9 slice_convert_fusion.1
  32.2 1.0 fusion.6
  33.2 1.0 fusion.8
  34.2 0.8 collective-permute-start.15
  35.0 1.2 collective-permute-start.13
  36.2 2.0 %collective-permute-start.4 = (bf16[256,640]{1,0:T(8,128)(2,1)S(1)}, bf16[256,640]{1,0:T(8,128)(2,1)S(1)}, u32[]{:S(2)}, u32[]{:S(2)}) collective-permute-start(bf16[256,640]{1,0:T(8,128)(2,1)S(1)} %collective-permute-done.x1b), channel_id=1, source_target_pairs={{0,3},{1,0},{2,1},{3,2},{4,7},{5,4},{6,5},{7,6},{8,11},{9,8},{10,9... | collective-permute-start | bytes 983048 | tf_op jit(solution)/shard_map/ppermute | solution.py:167
  38.2 1.0 fusion.10
  39.2 9.1 %all-to-all-done = bf16[32,64,160]{2,1,0:T(8,128)(2,1)} async-done(((bf16[32,64,160]{2,1,0:T(8,128)(2,1)}), bf16[32,64,160]{2,1,0:T(8,128)(2,1)}, u32[]{:S(2)}, u32[]{:S(2)}) %all-to-all-start) | async-done | bytes 655392 | tf_op jit(solution)/shard_map/all_to_all | solution.py:215
  48.3 5.4 %collective-permute-done.3.x2t = bf16[256,640]{1,0:T(8,128)(2,1)S(1)} collective-permute-done((bf16[256,640]{1,0:T(8,128)(2,1)S(1)}, bf16[256,640]{1,0:T(8,128)(2,1)S(1)}, u32[]{:S(2)}, u32[]{:S(2)}) %collective-permute-start.3) | collective-permute-done | bytes 327712 | tf_op jit(solution)/shard_map/ppermute | solution.py:167
  53.7 0.6 collective-permute-start.16
  54.4 1.7 %collective-permute-start.14 = (bf16[256,640]{1,0:T(8,128)(2,1)S(1)}, bf16[256,640]{1,0:T(8,128)(2,1)S(1)}, u32[]{:S(2)}, u32[]{:S(2)}) collective-permute-start(bf16[256,640]{1,0:T(8,128)(2,1)S(1)} %collective-permute-done.13.x3t), channel_id=1, source_target_pairs={{0,1},{1,2},{2,3},{3,0},{4,5},{5,6},{6,7},{7,4},{8,9},{9,10},{10,1... | collective-permute-start | bytes 983048 | tf_op jit(solution)/shard_map/ppermute | solution.py:167
  56.0 14.8 %shard_map.121 = (f32[512,640]{1,0:T(8,128)}, bf16[256,640]{1,0:T(8,128)(2,1)S(1)}, bf16[256,640]{1,0:T(8,128)(2,1)S(1)}, bf16[256,640]{1,0:T(8,128)(2,1)S(1)}, ...) custom-call(s32[1]{0:T(128)} %bitcast.place, ...), custom_call_target="tpu_custom_call" | custom-call | flops 6710886400 | bytes 23592960 | tf_op jit(solution)/shard_map/pallas_call | solution.py:144
  70.9 1.8 %collective-permute-start.6 = (bf16[256,640]{1,0:T(8,128)(2,1)S(1)}, bf16[256,640]{1,0:T(8,128)(2,1)S(1)}, u32[]{:S(2)}, u32[]{:S(2)}) collective-permute-start(bf16[256,640]{1,0:T(8,128)(2,1)S(1)} %get-tuple-element.29), channel_id=1, source_target_pairs={{0,1},{1,2},{2,3},{3,0},{4,5},{5,6},{6,7},{7,4},{8,9},{9,10},{10,1... | collective-permute-start | bytes 983048 | tf_op jit(solution)/shard_map/ppermute | solution.py:167
  72.7 1.5 %collective-permute-start.10 = (bf16[256,640]{1,0:T(8,128)(2,1)S(1)}, bf16[256,640]{1,0:T(8,128)(2,1)S(1)}, u32[]{:S(2)}, u32[]{:S(2)}) collective-permute-start(bf16[256,640]{1,0:T(8,128)(2,1)S(1)} %get-tuple-element.33), channel_id=1, source_target_pairs={{0,3},{1,0},{2,1},{3,2},{4,7},{5,4},{6,5},{7,6},{8,11},{9,8},{10,9... | collective-permute-start | bytes 983048 | tf_op jit(solution)/shard_map/ppermute | solution.py:167
  74.2 14.8 %shard_map.122 = (f32[512,640]{1,0:T(8,128)}, bf16[256,640]{1,0:T(8,128)(2,1)S(1)}, bf16[256,640]{1,0:T(8,128)(2,1)S(1)}, bf16[256,640]{1,0:T(8,128)(2,1)S(1)}, ...) custom-call(s32[1]{0:T(128)} %bitcast.place, bf16[512,640]{1,0:T(8,128)(2,1)} %copy-done.1, ...), custom_call_target="tpu_custom_call" | custom-call | flops 6710886400 | bytes 23592960 | tf_op jit(solution)/shard_map/pallas_call | solution.py:144
  89.0 0.7 collective-permute-start.18
  89.7 2.6 %collective-permute-start.22 = (bf16[256,640]{1,0:T(8,128)(2,1)S(1)}, bf16[256,640]{1,0:T(8,128)(2,1)S(1)}, u32[]{:S(2)}, u32[]{:S(2)}) collective-permute-start(bf16[256,640]{1,0:T(8,128)(2,1)S(1)} %get-tuple-element.44), channel_id=1, source_target_pairs={{0,3},{1,0},{2,1},{3,2},{4,7},{5,4},{6,5},{7,6},{8,11},{9,8},{10,9... | collective-permute-start | bytes 983048 | tf_op jit(solution)/shard_map/ppermute | solution.py:167
  92.4 2.0 %collective-permute-start.9 = (bf16[256,640]{1,0:T(8,128)(2,1)S(1)}, bf16[256,640]{1,0:T(8,128)(2,1)S(1)}, u32[]{:S(2)}, u32[]{:S(2)}) collective-permute-start(bf16[256,640]{1,0:T(8,128)(2,1)S(1)} %get-tuple-element.31), channel_id=1, source_target_pairs={{0,1},{1,2},{2,3},{3,0},{4,5},{5,6},{6,7},{7,4},{8,9},{9,10},{10,1... | collective-permute-start | bytes 983048 | tf_op jit(solution)/shard_map/ppermute | solution.py:167
  94.4 0.1 add.37
  94.5 0.1 collective-permute-start.7
  94.6 0.1 add.40
  94.6 6.3 %collective-permute-done.18 = bf16[256,640]{1,0:T(8,128)(2,1)S(1)} collective-permute-done((bf16[256,640]{1,0:T(8,128)(2,1)S(1)}, bf16[256,640]{1,0:T(8,128)(2,1)S(1)}, u32[]{:S(2)}, u32[]{:S(2)}) %collective-permute-start.18) | collective-permute-done | bytes 327712 | tf_op jit(solution)/shard_map/ppermute | solution.py:167
  101.0 0.1 add.43
  101.1 3.1 %collective-permute-start.20 = (bf16[256,640]{1,0:T(8,128)(2,1)S(1)}, bf16[256,640]{1,0:T(8,128)(2,1)S(1)}, u32[]{:S(2)}, u32[]{:S(2)}) collective-permute-start(bf16[256,640]{1,0:T(8,128)(2,1)S(1)} %get-tuple-element.41), channel_id=1, source_target_pairs={{0,3},{1,0},{2,1},{3,2},{4,7},{5,4},{6,5},{7,6},{8,11},{9,8},{10,9... | collective-permute-start | bytes 983048 | tf_op jit(solution)/shard_map/ppermute | solution.py:167
  104.2 0.1 add.46
  104.3 3.2 %collective-permute-done.8 = bf16[256,640]{1,0:T(8,128)(2,1)S(1)} collective-permute-done((bf16[256,640]{1,0:T(8,128)(2,1)S(1)}, bf16[256,640]{1,0:T(8,128)(2,1)S(1)}, u32[]{:S(2)}, u32[]{:S(2)}) %collective-permute-start.8) | collective-permute-done | bytes 327712 | tf_op jit(solution)/shard_map/ppermute | solution.py:167
  107.5 0.1 collective-permute-start.21
  107.6 0.3 collective-permute-done.9
  108.0 1.4 %collective-permute-start.19 = (bf16[256,640]{1,0:T(8,128)(2,1)S(1)}, bf16[256,640]{1,0:T(8,128)(2,1)S(1)}, u32[]{:S(2)}, u32[]{:S(2)}) collective-permute-start(bf16[256,640]{1,0:T(8,128)(2,1)S(1)} %add.43), channel_id=1, source_target_pairs={{0,1},{1,2},{2,3},{3,0},{4,5},{5,6},{6,7},{7,4},{8,9},{9,10},{10,1... | collective-permute-start | bytes 983048 | tf_op jit(solution)/shard_map/ppermute | solution.py:167
  109.4 5.6 %collective-permute-done.7 = bf16[256,640]{1,0:T(8,128)(2,1)S(1)} collective-permute-done((bf16[256,640]{1,0:T(8,128)(2,1)S(1)}, bf16[256,640]{1,0:T(8,128)(2,1)S(1)}, u32[]{:S(2)}, u32[]{:S(2)}) %collective-permute-start.7) | collective-permute-done | bytes 327712 | tf_op jit(solution)/shard_map/ppermute | solution.py:167
  115.0 0.2 add_convert_fusion.3
  115.3 4.3 %fusion.2 = f32[80,1280]{1,0:T(8,128)} fusion(bf16[2048,2560]{1,0:T(8,128)(2,1)} %all-gather.2.cloned.1.call-done, bf16[2048,160]{1,0:T(8,128)(2,1)} %bitcast.3), kind=kOutput, calls=%fused_computation.2 | convolution fusion | flops 419430400 | bytes 6176768 | tf_op jit(solution)/shard_map/dot_general | solution.py:223
  119.5 4.6 %fusion = f32[1280,80]{0,1:T(8,128)} fusion(bf16[2048,2560]{1,0:T(8,128)(2,1)} %all-gather.2.cloned.1.call-done, bf16[2048,160]{1,0:T(8,128)(2,1)} %bitcast.3), kind=kOutput, calls=%fused_computation | convolution fusion | flops 419430400 | bytes 6176768 | tf_op jit(solution)/shard_map/dot_general | solution.py:226
  124.2 1.0 collective-permute-done.19
  125.2 0.2 add_convert_fusion.1
  125.4 1.2 pad_maximum_fusion
  (51 shorter events, 0.2 us)
Async XLA Ops:
  7.2 108.1 %all-gather.2.cloned.1.call-start = ((), (), s32[]{:S(2)}) async-start(), calls=%async_computation.1 | async-start | bytes 10813440 | tf_op jit(solution)/shard_map/all_gather | solution.py:218
  10.9 27.3 %collective-permute-start.2 = (bf16[256,640]{1,0:T(8,128)(2,1)}, bf16[256,640]{1,0:T(8,128)(2,1)S(1)}, u32[]{:S(2)}, u32[]{:S(2)}) collective-permute-start(bf16[256,640]{1,0:T(8,128)(2,1)} %get-tuple-element.53), channel_id=1, source_target_pairs={{0,1},{1,2},{2,3},{3,0},{4,5},{5,6},{6,7},{7,4},{8,9},{9,10},{10,1... | collective-permute-start | bytes 983048 | tf_op jit(solution)/shard_map/ppermute | solution.py:167
  12.9 20.3 %collective-permute-start.1 = (bf16[256,640]{1,0:T(8,128)(2,1)}, bf16[256,640]{1,0:T(8,128)(2,1)S(1)}, u32[]{:S(2)}, u32[]{:S(2)}) collective-permute-start(bf16[256,640]{1,0:T(8,128)(2,1)} %get-tuple-element.53), channel_id=1, source_target_pairs={{0,3},{1,0},{2,1},{3,2},{4,7},{5,4},{6,5},{7,6},{8,11},{9,8},{10,9... | collective-permute-start | bytes 983048 | tf_op jit(solution)/shard_map/ppermute | solution.py:167
  15.0 33.4 %collective-permute-start.5 = (bf16[256,640]{1,0:T(8,128)(2,1)}, bf16[256,640]{1,0:T(8,128)(2,1)}, u32[]{:S(2)}, u32[]{:S(2)}) collective-permute-start(bf16[256,640]{1,0:T(8,128)(2,1)} %get-tuple-element.54), channel_id=1, source_target_pairs={{0,1},{1,2},{2,3},{3,0},{4,5},{5,6},{6,7},{7,4},{8,9},{9,10},{10,1... | collective-permute-start | bytes 983048 | tf_op jit(solution)/shard_map/ppermute | solution.py:167
  15.0 18.2 %collective-permute-start = (bf16[256,640]{1,0:T(8,128)(2,1)}, bf16[256,640]{1,0:T(8,128)(2,1)S(1)}, u32[]{:S(2)}, u32[]{:S(2)}) collective-permute-start(bf16[256,640]{1,0:T(8,128)(2,1)} %get-tuple-element.54), channel_id=1, source_target_pairs={{0,3},{1,0},{2,1},{3,2},{4,7},{5,4},{6,5},{7,6},{8,11},{9,8},{10,9... | collective-permute-start | bytes 983048 | tf_op jit(solution)/shard_map/ppermute | solution.py:167
  21.4 9.8 %copy-start.4 = (bf16[64,2560]{1,0:T(8,128)(2,1)S(1)}, bf16[64,2560]{1,0:T(8,128)(2,1)}, u32[]{:S(2)}) copy-start(bf16[64,2560]{1,0:T(8,128)(2,1)} %param.15) | copy-start | bytes 983044
  21.4 9.8 %copy-start.5 = (bf16[64,2560]{1,0:T(8,128)(2,1)S(1)}, bf16[64,2560]{1,0:T(8,128)(2,1)}, u32[]{:S(2)}) copy-start(bf16[64,2560]{1,0:T(8,128)(2,1)} %param.18) | copy-start | bytes 983044
  21.9 10.2 %copy-start = (bf16[1024,640]{1,0:T(8,128)(2,1)S(1)}, bf16[1024,640]{1,0:T(8,128)(2,1)}, u32[]{:S(2)}) copy-start(bf16[1024,640]{1,0:T(8,128)(2,1)} %param.10) | copy-start | bytes 3932164
  23.5 24.8 %all-to-all-start = ((bf16[32,64,160]{2,1,0:T(8,128)(2,1)}), bf16[32,64,160]{2,1,0:T(8,128)(2,1)}, u32[]{:S(2)}, u32[]{:S(2)}) async-start(bf16[32,64,160]{2,1,0:T(8,128)(2,1)} %copy.16), calls=%async_computation | async-start | bytes 2097152 | tf_op jit(solution)/shard_map/all_to_all | solution.py:215
  31.2 1.9 %copy-start.7 = (f32[2560]{0:T(1024)S(1)}, f32[2560]{0:T(1024)}, u32[]{:S(2)}) copy-start(f32[2560]{0:T(1024)} %param.11) | copy-start | bytes 30724
  31.2 1.9 %copy-start.8 = (f32[2560]{0:T(1024)S(1)}, f32[2560]{0:T(1024)}, u32[]{:S(2)}) copy-start(f32[2560]{0:T(1024)} %param.12) | copy-start | bytes 30724
  31.2 7.0 %copy-start.6 = (bf16[64,1280]{1,0:T(8,128)(2,1)S(1)}, bf16[64,1280]{1,0:T(8,128)(2,1)}, u32[]{:S(2)}) copy-start(bf16[64,1280]{1,0:T(8,128)(2,1)} %param.17) | copy-start | bytes 491524
  33.1 5.1 %copy-start.1 = (bf16[512,640]{1,0:T(8,128)(2,1)}, bf16[512,640]{1,0:T(8,128)(2,1)S(1)}, u32[]{:S(2)}) copy-start(bf16[512,640]{1,0:T(8,128)(2,1)S(1)} %get-tuple-element.35.x0) | copy-start | bytes 1966084
  34.2 19.6 %collective-permute-start.15 = (bf16[256,640]{1,0:T(8,128)(2,1)}, bf16[256,640]{1,0:T(8,128)(2,1)S(1)}, u32[]{:S(2)}, u32[]{:S(2)}) collective-permute-start(bf16[256,640]{1,0:T(8,128)(2,1)} %get-tuple-element.55), channel_id=1, source_target_pairs={{0,3},{1,0},{2,1},{3,2},{4,7},{5,4},{6,5},{7,6},{8,11},{9,8},{10,9... | collective-permute-start | bytes 983048 | tf_op jit(solution)/shard_map/ppermute | solution.py:167
  35.0 19.4 %collective-permute-start.13 = (bf16[256,640]{1,0:T(8,128)(2,1)}, bf16[256,640]{1,0:T(8,128)(2,1)S(1)}, u32[]{:S(2)}, u32[]{:S(2)}) collective-permute-start(bf16[256,640]{1,0:T(8,128)(2,1)} %get-tuple-element.56), channel_id=1, source_target_pairs={{0,1},{1,2},{2,3},{3,0},{4,5},{5,6},{6,7},{7,4},{8,9},{9,10},{10,1... | collective-permute-start | bytes 983048 | tf_op jit(solution)/shard_map/ppermute | solution.py:167
  36.2 19.8 %collective-permute-start.4 = (bf16[256,640]{1,0:T(8,128)(2,1)S(1)}, bf16[256,640]{1,0:T(8,128)(2,1)S(1)}, u32[]{:S(2)}, u32[]{:S(2)}) collective-permute-start(bf16[256,640]{1,0:T(8,128)(2,1)S(1)} %collective-permute-done.x1b), channel_id=1, source_target_pairs={{0,3},{1,0},{2,1},{3,2},{4,7},{5,4},{6,5},{7,6},{8,11},{9,8},{10,9... | collective-permute-start | bytes 983048 | tf_op jit(solution)/shard_map/ppermute | solution.py:167
  38.2 15.5 %collective-permute-start.3 = (bf16[256,640]{1,0:T(8,128)(2,1)S(1)}, bf16[256,640]{1,0:T(8,128)(2,1)S(1)}, u32[]{:S(2)}, u32[]{:S(2)}) collective-permute-start(bf16[256,640]{1,0:T(8,128)(2,1)S(1)} %collective-permute-done.2.x3t), channel_id=1, source_target_pairs={{0,1},{1,2},{2,3},{3,0},{4,5},{5,6},{6,7},{7,4},{8,9},{9,10},{10,1... | collective-permute-start | bytes 983048 | tf_op jit(solution)/shard_map/ppermute | solution.py:167
  48.3 24.4 %collective-permute-start.17 = (bf16[256,640]{1,0:T(8,128)(2,1)}, bf16[256,640]{1,0:T(8,128)(2,1)S(1)}, u32[]{:S(2)}, u32[]{:S(2)}) collective-permute-start(bf16[256,640]{1,0:T(8,128)(2,1)} %get-tuple-element.55), channel_id=1, source_target_pairs={{0,1},{1,2},{2,3},{3,0},{4,5},{5,6},{6,7},{7,4},{8,9},{9,10},{10,1... | collective-permute-start | bytes 983048 | tf_op jit(solution)/shard_map/ppermute | solution.py:167
  53.7 20.4 %collective-permute-start.12 = (bf16[256,640]{1,0:T(8,128)(2,1)}, bf16[256,640]{1,0:T(8,128)(2,1)S(1)}, u32[]{:S(2)}, u32[]{:S(2)}) collective-permute-start(bf16[256,640]{1,0:T(8,128)(2,1)} %get-tuple-element.56), channel_id=1, source_target_pairs={{0,3},{1,0},{2,1},{3,2},{4,7},{5,4},{6,5},{7,6},{8,11},{9,8},{10,9... | collective-permute-start | bytes 983048 | tf_op jit(solution)/shard_map/ppermute | solution.py:167
  53.7 20.4 %collective-permute-start.16 = (bf16[256,640]{1,0:T(8,128)(2,1)S(1)}, bf16[256,640]{1,0:T(8,128)(2,1)S(1)}, u32[]{:S(2)}, u32[]{:S(2)}) collective-permute-start(bf16[256,640]{1,0:T(8,128)(2,1)S(1)} %collective-permute-done.15.x1b), channel_id=1, source_target_pairs={{0,3},{1,0},{2,1},{3,2},{4,7},{5,4},{6,5},{7,6},{8,11},{9,8},{10,9... | collective-permute-start | bytes 983048 | tf_op jit(solution)/shard_map/ppermute | solution.py:167
  54.4 19.8 %collective-permute-start.14 = (bf16[256,640]{1,0:T(8,128)(2,1)S(1)}, bf16[256,640]{1,0:T(8,128)(2,1)S(1)}, u32[]{:S(2)}, u32[]{:S(2)}) collective-permute-start(bf16[256,640]{1,0:T(8,128)(2,1)S(1)} %collective-permute-done.13.x3t), channel_id=1, source_target_pairs={{0,1},{1,2},{2,3},{3,0},{4,5},{5,6},{6,7},{7,4},{8,9},{9,10},{10,1... | collective-permute-start | bytes 983048 | tf_op jit(solution)/shard_map/ppermute | solution.py:167
  70.9 21.5 %collective-permute-start.6 = (bf16[256,640]{1,0:T(8,128)(2,1)S(1)}, bf16[256,640]{1,0:T(8,128)(2,1)S(1)}, u32[]{:S(2)}, u32[]{:S(2)}) collective-permute-start(bf16[256,640]{1,0:T(8,128)(2,1)S(1)} %get-tuple-element.29), channel_id=1, source_target_pairs={{0,1},{1,2},{2,3},{3,0},{4,5},{5,6},{6,7},{7,4},{8,9},{9,10},{10,1... | collective-permute-start | bytes 983048 | tf_op jit(solution)/shard_map/ppermute | solution.py:167
  72.7 1.5 %copy-start.9 = (bf16[256,640]{1,0:T(8,128)(2,1)}, bf16[256,640]{1,0:T(8,128)(2,1)S(1)}, u32[]{:S(2)}) copy-start(bf16[256,640]{1,0:T(8,128)(2,1)S(1)} %collective-permute-done.17.x3b) | copy-start | bytes 983044
  72.7 21.8 %collective-permute-start.10 = (bf16[256,640]{1,0:T(8,128)(2,1)S(1)}, bf16[256,640]{1,0:T(8,128)(2,1)S(1)}, u32[]{:S(2)}, u32[]{:S(2)}) collective-permute-start(bf16[256,640]{1,0:T(8,128)(2,1)S(1)} %get-tuple-element.33), channel_id=1, source_target_pairs={{0,3},{1,0},{2,1},{3,2},{4,7},{5,4},{6,5},{7,6},{8,11},{9,8},{10,9... | collective-permute-start | bytes 983048 | tf_op jit(solution)/shard_map/ppermute | solution.py:167
  89.0 26.0 %copy-start.2 = (f32[512,640]{1,0:T(8,128)S(1)}, f32[512,640]{1,0:T(8,128)}, u32[]{:S(2)}) copy-start(f32[512,640]{1,0:T(8,128)} %get-tuple-element.27) | copy-start | bytes 3932164
  89.0 11.9 %collective-permute-start.18 = (bf16[256,640]{1,0:T(8,128)(2,1)S(1)}, bf16[256,640]{1,0:T(8,128)(2,1)S(1)}, u32[]{:S(2)}, u32[]{:S(2)}) collective-permute-start(bf16[256,640]{1,0:T(8,128)(2,1)S(1)} %get-tuple-element.40), channel_id=1, source_target_pairs={{0,1},{1,2},{2,3},{3,0},{4,5},{5,6},{6,7},{7,4},{8,9},{9,10},{10,1... | collective-permute-start | bytes 983048 | tf_op jit(solution)/shard_map/ppermute | solution.py:167
  89.7 11.4 %collective-permute-start.22 = (bf16[256,640]{1,0:T(8,128)(2,1)S(1)}, bf16[256,640]{1,0:T(8,128)(2,1)S(1)}, u32[]{:S(2)}, u32[]{:S(2)}) collective-permute-start(bf16[256,640]{1,0:T(8,128)(2,1)S(1)} %get-tuple-element.44), channel_id=1, source_target_pairs={{0,3},{1,0},{2,1},{3,2},{4,7},{5,4},{6,5},{7,6},{8,11},{9,8},{10,9... | collective-permute-start | bytes 983048 | tf_op jit(solution)/shard_map/ppermute | solution.py:167
  92.3 15.2 %collective-permute-start.8 = (bf16[256,640]{1,0:T(8,128)(2,1)S(1)}, bf16[256,640]{1,0:T(8,128)(2,1)S(1)}, u32[]{:S(2)}, u32[]{:S(2)}) collective-permute-start(bf16[256,640]{1,0:T(8,128)(2,1)S(1)} %get-tuple-element.30), channel_id=1, source_target_pairs={{0,3},{1,0},{2,1},{3,2},{4,7},{5,4},{6,5},{7,6},{8,11},{9,8},{10,9... | collective-permute-start | bytes 983048 | tf_op jit(solution)/shard_map/ppermute | solution.py:167
  92.4 15.6 %collective-permute-start.9 = (bf16[256,640]{1,0:T(8,128)(2,1)S(1)}, bf16[256,640]{1,0:T(8,128)(2,1)S(1)}, u32[]{:S(2)}, u32[]{:S(2)}) collective-permute-start(bf16[256,640]{1,0:T(8,128)(2,1)S(1)} %get-tuple-element.31), channel_id=1, source_target_pairs={{0,1},{1,2},{2,3},{3,0},{4,5},{5,6},{6,7},{7,4},{8,9},{9,10},{10,1... | collective-permute-start | bytes 983048 | tf_op jit(solution)/shard_map/ppermute | solution.py:167
  94.5 20.5 %collective-permute-start.7 = (bf16[256,640]{1,0:T(8,128)(2,1)S(1)}, bf16[256,640]{1,0:T(8,128)(2,1)S(1)}, u32[]{:S(2)}, u32[]{:S(2)}) collective-permute-start(bf16[256,640]{1,0:T(8,128)(2,1)S(1)} %add.37), channel_id=1, source_target_pairs={{0,1},{1,2},{2,3},{3,0},{4,5},{5,6},{6,7},{7,4},{8,9},{9,10},{10,1... | collective-permute-start | bytes 983048 | tf_op jit(solution)/shard_map/ppermute | solution.py:167
  101.0 14.1 %collective-permute-start.11 = (bf16[256,640]{1,0:T(8,128)(2,1)S(1)}, bf16[256,640]{1,0:T(8,128)(2,1)S(1)}, u32[]{:S(2)}, u32[]{:S(2)}) collective-permute-start(bf16[256,640]{1,0:T(8,128)(2,1)S(1)} %add.40), channel_id=1, source_target_pairs={{0,3},{1,0},{2,1},{3,2},{4,7},{5,4},{6,5},{7,6},{8,11},{9,8},{10,9... | collective-permute-start | bytes 983048 | tf_op jit(solution)/shard_map/ppermute | solution.py:167
  101.1 23.1 %collective-permute-start.20 = (bf16[256,640]{1,0:T(8,128)(2,1)S(1)}, bf16[256,640]{1,0:T(8,128)(2,1)S(1)}, u32[]{:S(2)}, u32[]{:S(2)}) collective-permute-start(bf16[256,640]{1,0:T(8,128)(2,1)S(1)} %get-tuple-element.41), channel_id=1, source_target_pairs={{0,3},{1,0},{2,1},{3,2},{4,7},{5,4},{6,5},{7,6},{8,11},{9,8},{10,9... | collective-permute-start | bytes 983048 | tf_op jit(solution)/shard_map/ppermute | solution.py:167
  107.5 16.6 %collective-permute-start.21 = (bf16[256,640]{1,0:T(8,128)(2,1)S(1)}, bf16[256,640]{1,0:T(8,128)(2,1)S(1)}, u32[]{:S(2)}, u32[]{:S(2)}) collective-permute-start(bf16[256,640]{1,0:T(8,128)(2,1)S(1)} %get-tuple-element.42), channel_id=1, source_target_pairs={{0,1},{1,2},{2,3},{3,0},{4,5},{5,6},{6,7},{7,4},{8,9},{9,10},{10,1... | collective-permute-start | bytes 983048 | tf_op jit(solution)/shard_map/ppermute | solution.py:167
  108.0 17.2 %collective-permute-start.19 = (bf16[256,640]{1,0:T(8,128)(2,1)S(1)}, bf16[256,640]{1,0:T(8,128)(2,1)S(1)}, u32[]{:S(2)}, u32[]{:S(2)}) collective-permute-start(bf16[256,640]{1,0:T(8,128)(2,1)S(1)} %add.43), channel_id=1, source_target_pairs={{0,1},{1,2},{2,3},{3,0},{4,5},{5,6},{6,7},{7,4},{8,9},{9,10},{10,1... | collective-permute-start | bytes 983048 | tf_op jit(solution)/shard_map/ppermute | solution.py:167
  115.0 10.2 %collective-permute-start.23 = (bf16[256,640]{1,0:T(8,128)(2,1)S(1)}, bf16[256,640]{1,0:T(8,128)(2,1)S(1)}, u32[]{:S(2)}, u32[]{:S(2)}) collective-permute-start(bf16[256,640]{1,0:T(8,128)(2,1)S(1)} %add.46), channel_id=1, source_target_pairs={{0,3},{1,0},{2,1},{3,2},{4,7},{5,4},{6,5},{7,6},{8,11},{9,8},{10,9... | collective-permute-start | bytes 983048 | tf_op jit(solution)/shard_map/ppermute | solution.py:167
  119.5 5.6 %copy-start.3 = (f32[512,640]{1,0:T(8,128)S(1)}, f32[512,640]{1,0:T(8,128)}, u32[]{:S(2)}) copy-start(f32[512,640]{1,0:T(8,128)} %get-tuple-element.38) | copy-start | bytes 3932164
Sparse Core Ops, SparseCore 0:
  10.2 68.0 all-gather.1

commit v3 on v0

v3 whole, which is shorter than its diff:
```python
import functools
import math

import jax
import jax.numpy as jnp
from jax import lax
from jax.experimental import pallas as pl
from jax.experimental.pallas import tpu as pltpu
from jax.sharding import Mesh, PartitionSpec as P

D = 2560
FFW = 5120
MEMBERS = 2048
PROMPT = 16
EPSILON = 1e-05
SIGMA = 0.5
KEY_FACTOR = SIGMA / math.sqrt(D)
VALUE_FACTOR = SIGMA / math.sqrt(FFW)
LN_ROWS = 64
F_BLOCK = 640
LANES = 128
MIB = 1024 * 1024

VMEM = pl.BlockSpec(memory_space=pltpu.VMEM)
SMEM = pl.BlockSpec(memory_space=pltpu.SMEM)
ANY = pl.BlockSpec(memory_space=pl.ANY)


def mm(a, b):
    return jnp.dot(a, b, preferred_element_type=jnp.float32)


def per_member(array, rows):
    members, width = array.shape
    wide = jnp.broadcast_to(array.astype(jnp.float32)[:, None, :], (members, PROMPT, width))
    return wide.reshape(rows, width)


def ffn_kernel(place, x0, *refs):
    pieces, refs = refs[:-20], refs[-20:]
    keep, pass_on, kw_hbm, vw_hbm, kl, kr, vl, vr, _, *refs = refs
    own, to_right, to_left, right_top, left_bottom, kw, vw, mixed, hidden, kdots, sems = refs
    rows, width = x0.shape
    half = rows // 2
    units = kw.shape[1]
    z = place[0]
    key_copy = pltpu.make_async_copy(kw_hbm, kw, sems.at[0])
    value_copy = pltpu.make_async_copy(vw_hbm, vw, sems.at[1])
    key_copy.start()
    value_copy.start()

    def column(k):
        return pl.multiple_of(lax.rem(z + k, 4) * width, 128)

    def normalise(i, sub, sources):
        first = pl.multiple_of(i * 128 + sub * LN_ROWS, LN_ROWS)
        span = pl.ds(first, LN_ROWS)
        group = pl.ds(pl.multiple_of(i * 8, 8), 8)
        ours = slice(sub * LN_ROWS // PROMPT, (sub + 1) * LN_ROWS // PROMPT)
        values = [x0[span, :]]
        for source, offset in sources:
            values.append(source[pl.ds(pl.multiple_of(first - offset, LN_ROWS), LN_ROWS), :])
        values = [v.astype(jnp.float32) for v in values]
        centre = sum(jnp.sum(v, axis=-1, keepdims=True) for v in values) * (1.0 / D)
        values = [v - centre for v in values]
        spread = sum(jnp.sum(v * v, axis=-1, keepdims=True) for v in values) * (1.0 / D)
        scale = lax.rsqrt(spread + EPSILON)
        later = lax.broadcasted_iota(jnp.int32, (LN_ROWS, 1), 0) % PROMPT != 0
        dots = 0.0
        for k, value in enumerate(values):
            cols = pl.ds(column(k), width)
            normed = value * scale
            before = pltpu.roll(normed * pass_on[:, cols], 1, 0)
            block = normed * keep[:, cols] + jnp.where(later, before, 0.0)
            block = block.astype(jnp.bfloat16)
            mixed[span, cols] = block
            left = per_member(kl[group, cols][ours], LN_ROWS)
            dots += jnp.sum(block.astype(jnp.float32) * left, axis=-1, keepdims=True)
        kdots[span, :] = dots * KEY_FACTOR

    def normalise_group(sources, i, carry):
        for sub in range(128 // LN_ROWS):
            normalise(i, sub, sources)
        return carry

    groups = rows // 128
    if len(pieces) == 4:
        right, left, far_top, far_bottom = pieces
        top, bottom = [(right, 0), (far_top, 0), (left, 0)], [(right, 0), (far_bottom, half), (left, 0)]
    else:
        near, far = pieces[:4], pieces[4:]
        top = [(near[0], 0), (far[0], 0), (near[1], 0)]
        bottom = [(near[2], half), (far[1], half), (near[3], half)]
    lax.fori_loop(0, groups // 2, functools.partial(normalise_group, top), 0)
    lax.fori_loop(groups // 2, groups, functools.partial(normalise_group, bottom), 0)

    key_copy.wait()
    vdots = 0.0
    for first in range(0, units, F_BLOCK):
        cols = pl.ds(first, F_BLOCK)
        preact = mm(mixed[...], kw[:, cols]) + kdots[...] * per_member(kr[:, cols], rows)
        block = jnp.square(jnp.maximum(preact, 0.0)).astype(jnp.bfloat16)
        hidden[:, cols] = block
        left = per_member(vl[:, cols], rows)
        vdots += jnp.sum(block.astype(jnp.float32) * left, axis=-1, keepdims=True)
    vdots = vdots * VALUE_FACTOR

    value_copy.wait()

    def sums(k):
        cols = pl.ds(column(k), width)
        return mm(hidden[...], vw[:, cols]) + vdots * per_member(vr[:, cols], rows)

    far = sums(2).astype(jnp.bfloat16)
    to_right[:half] = far[:half]
    to_left[half:] = far[half:]
    right = sums(1).astype(jnp.bfloat16)
    right_top[...] = right[:half]
    to_right[half:] = right[half:]
    left = sums(3).astype(jnp.bfloat16)
    to_left[:half] = left[:half]
    left_bottom[...] = left[half:]
    own[...] = sums(0)


def ffn(place, own, pieces, keep, pass_on, kw, vw, kl, kr, vl, vr, after):
    rows, width = own.shape
    units = kr.shape[1]
    half = rows // 2
    parts = [jax.ShapeDtypeStruct((n, width), jnp.bfloat16) for n in (rows, rows, half, half)]
    return pl.pallas_call(
        ffn_kernel,
        out_shape=[jax.ShapeDtypeStruct((rows, width), jnp.float32)] + parts,
        in_specs=[SMEM] + [VMEM] * (len(pieces) + 3) + [ANY] * 2 + [VMEM] * 4 + [ANY],
        out_specs=[VMEM] * 5,
        scratch_shapes=[
            pltpu.VMEM((D, units), jnp.bfloat16),
            pltpu.VMEM((units, D), jnp.bfloat16),
            pltpu.VMEM((rows, D), jnp.bfloat16),
            pltpu.VMEM((rows, units), jnp.bfloat16),
            pltpu.VMEM((rows, 1), jnp.float32),
            pltpu.SemaphoreType.DMA((2,)),
        ],
        compiler_params=pltpu.CompilerParams(vmem_limit_bytes=50 * MIB),
        cost_estimate=pl.CostEstimate(
            flops=8 * rows * D * units,
            bytes_accessed=4 * D * units + 8 * rows * D,
            transcendentals=rows,
        ),
    )(place, own, *pieces, keep, pass_on, kw, vw, kl, kr, vl, vr, after)


def prepare_kernel(place, weight, key_left, value_right, key_right, value_left, _, sent):
    core = place[0]
    rights = jnp.concatenate([key_right[...], value_left[...]], axis=0)
    scaled = [f[...].astype(jnp.float32) * weight[...] for f in (key_left, value_right)]
    lefts = jnp.concatenate([s.T for s in scaled], axis=1).astype(jnp.bfloat16)
    share = D // 32
    for x in range(4):
        for block in range(rights.shape[1] // LANES):
            rows = slice(4 * share + block * LANES, 4 * share + (block + 1) * LANES)
            sent[x, rows, :] = rights[:, block * LANES : (block + 1) * LANES]
        for c in range(2):
            first = jnp.where(core == c, 0, 4 * share + rights.shape[1])
            for y in range(4):
                start = ((y * 4 + x) * 2 + c) * share
                target = pl.ds(pl.multiple_of(first + y * share, 16), share)
                sent[x, target, :] = lefts[start : start + share]


def update_kernel(place, gathered, swapped, own, parts, sums):
    share, units = own.shape
    share //= 2
    lefts, rights = [], []
    for source, first_left, first_right in ((gathered, 0, 4 * share), (swapped, units, 0)):
        for x in range(4):
            lefts.append(source[x, first_left : first_left + 4 * share, :])
            blocks = range(first_right, first_right + units, LANES)
            rights.append(jnp.concatenate([source[x, b : b + LANES, :] for b in blocks], axis=1))
    rights = jnp.concatenate(rights, axis=0)
    lane = lax.broadcasted_iota(jnp.int32, lefts[0].shape, 1)
    for side in range(2):
        picked = [jnp.where((lane < LANES // 2) == (side == 0), b, 0.0) for b in lefts]
        total = mm(jnp.concatenate(picked, axis=1), rights)
        for y in range(4):
            sums[y, side * share : (side + 1) * share, :] = total[y * share : (y + 1) * share]
    own[...] = sums[place[0]]
    parts[...] = sums[...].astype(jnp.bfloat16)


def update_products(gathered, swapped, units):
    share = D // 16
    y = lax.axis_index("y").astype(jnp.int32).reshape(1)
    return pl.pallas_call(
        update_kernel,
        out_shape=[
            jax.ShapeDtypeStruct((share, units), jnp.float32),
            jax.ShapeDtypeStruct((4, share, units), jnp.bfloat16),
        ],
        in_specs=[SMEM, VMEM, VMEM],
        out_specs=[VMEM, VMEM],
        scratch_shapes=[pltpu.VMEM((4, share, units), jnp.float32)],
        compiler_params=pltpu.CompilerParams(vmem_limit_bytes=16 * MIB),
        cost_estimate=pl.CostEstimate(
            flops=16 * share * 1024 * units, bytes_accessed=8 * MIB, transcendentals=0
        ),
    )(y, gathered, swapped)


def shift(array, by):
    return lax.ppermute(array, "z", [(i, (i + by) % 4) for i in range(4)])


def local(
    layer_input,
    norm_gain,
    shift_mix,
    key_weight,
    value_weight,
    key_left,
    key_right,
    value_left,
    value_right,
    fitness_rank,
):
    members, units = key_right.shape
    z = lax.axis_index("z").astype(jnp.int32).reshape(1)
    core = lax.axis_index("core").astype(jnp.int32).reshape(1)
    gain, mix = norm_gain.reshape(1, D), shift_mix.reshape(1, D)
    rows, width = layer_input.shape[0] // 2, layer_input.shape[1]
    half = rows // 2

    inputs = []
    for c in range(2):
        own = layer_input[c * rows : (c + 1) * rows]
        top, bottom = own[:half], own[half:]
        if c == 0:
            left, right = shift(own, 1), shift(own, -1)
            left_top, left_bottom = left[:half], left[half:]
            right_top, right_bottom = right[:half], right[half:]
            pieces = [right, left]
        else:
            left_top, right_bottom = shift(top, 1), shift(bottom, -1)
            left_bottom, right_top = shift(bottom, 1), shift(top, -1)
            pieces = [right_top, left_top, right_bottom, left_bottom]
        pieces += [shift(left_top, 1), shift(right_bottom, -1)]
        inputs.append((own, pieces))

    weight = (fitness_rank.astype(jnp.float32) / (MEMBERS - 1) - 0.5) / math.sqrt(MEMBERS)
    length = D // 4 + units
    sent = pl.pallas_call(
        prepare_kernel,
        out_shape=jax.ShapeDtypeStruct((4, length, LANES), jnp.bfloat16),
        in_specs=[SMEM] + [VMEM] * 5 + [ANY],
        out_specs=VMEM,
        compiler_params=pltpu.CompilerParams(vmem_limit_bytes=8 * MIB),
        cost_estimate=pl.CostEstimate(flops=0, bytes_accessed=4 * MIB, transcendentals=0),
    )(core, weight[:, None], key_left, value_right, key_right, value_left, inputs[0][0])
    gathered = lax.all_to_all(sent, "x", split_axis=0, concat_axis=0, tiled=True)

    results = []
    for c, (own, pieces) in enumerate(inputs):
        part = slice(c * rows // PROMPT, (c + 1) * rows // PROMPT)
        results.append(
            ffn(
                z,
                own,
                pieces,
                gain * (1.0 - mix),
                gain * mix,
                key_weight,
                value_weight,
                key_left[part].astype(jnp.float32),
                key_right[part],
                value_left[part],
                value_right[part],
                place_after if c else z,
            )
        )
        if c == 0:
            swapped = gathered[:, D // 8 :]
            swapped = lax.ppermute(swapped, "core", [(0, 1), (1, 0)])
            update_own, update_parts = update_products(gathered, swapped, units)
            place_after = update_parts

    update_parts = lax.all_to_all(update_parts, "y", split_axis=0, concat_axis=0, tiled=True)
    update = sum(
        jnp.where(lax.axis_index("y") == y, update_own, update_parts[y].astype(jnp.float32))
        for y in range(4)
    )

    outputs = []
    for own, to_right, to_left, right_top, left_bottom in results:
        from_left, from_right = shift(to_right, 1), shift(to_left, -1)
        from_left_top = shift(right_top + from_left[:half], 1)
        from_right_bottom = shift(left_bottom + from_right[half:], -1)
        for mine, one, two in (
            (own[:half], from_left_top, from_right[:half]),
            (own[half:], from_left[half:], from_right_bottom),
        ):
            total = mine + (one.astype(jnp.float32) + two.astype(jnp.float32))
            outputs.append(total.astype(jnp.bfloat16))
    share = update.shape[0] // 2
    return (jnp.concatenate(outputs, axis=0), update[:share], update[share:].T)


def solution(mesh):
    mesh = Mesh(mesh.devices.reshape(4, 4, 2, 4), ("y", "x", "core", "z"))
    dp = ("y", "x", "core")
    placed = (
        P(dp, "z"),
        P(),
        P(),
        P(None, "z"),
        P("z", None),
        P(dp, None),
        P(dp, "z"),
        P(dp, "z"),
        P(dp, None),
        P(dp),
    )
    return jax.shard_map(
        local,
        mesh=mesh,
        in_specs=placed,
        out_specs=(P(dp, "z"), P(dp, "z"), P("z", dp)),
        check_vma=False,
    )
```

time: 358 us -> 121 us (0.34)
  waiting for transfers between devices: 241 us -> 25.5 us
  starting transfers between devices: 0.3 us -> 38.6 us
  Pallas kernels: 0 us -> 35 us
  matrix products: 26.2 us -> 0 us
  local copies, waits for them, and re-layouts: 34.1 us -> 9.14 us
  blocking collectives: 16 us -> 0 us
  between operations: 13.9 us -> 0.88 us
  other arithmetic: 23.9 us -> 11.1 us
    unnamed x4 -> x0, waiting for transfers between devices: 144 us -> none
    all_gather x1 -> x0, waiting for transfers between devices: 60.4 us -> none  [local(): full_rows = lax.all_gather(layer_input, 'tensor', axis=1, tiled=True)]
    reduce_scatter x1 -> x0, waiting for transfers between devices: 37.1 us -> none  [local(): lax.psum_scatter(partial_sums, 'tensor', scatter_dimension=1, tiled=True)]
    pallas_call x0 -> x4, Pallas kernels: none -> 35 us  [the longest x2 29.8 us: ffn(): pl.pallas_call(ffn_kernel, out_shape=[jax.ShapeDtypeStruct((rows, width),...]
    unnamed x25 -> x32, local copies, waits for them, and re-layouts: 32 us -> 0.23 us
    ppermute x0 -> x19, starting transfers between devices: none -> 29.2 us  [the longest x18 29.1 us: shift(): return lax.ppermute(array, 'z', [(i, (i + by) % 4) for i in range(4)])]
    dot_general x6 -> x0, matrix products: 26.2 us -> none  [the longest x1 10.2 us: local(): jnp.dot(mixed.reshape(-1, width), key_weight, preferred_element_type=jnp....]
    ppermute x0 -> x19, waiting for transfers between devices: none -> 25.5 us  [the longest x18 25.5 us: shift(): return lax.ppermute(array, 'z', [(i, (i + by) % 4) for i in range(4)])]
  transfers between devices with their start and end apart: 3 -> 21, of which waited for: 3 -> 7; matrix products, arithmetic and copies ran while one was open for 13% -> 12% of each run, Pallas kernels for 0% -> 27%
where the time goes in v3:
time: 121 us; the launch traced here: 120 us
  starting transfers between devices  38.6 us (32%)
  Pallas kernels  35 us (29%)
  waiting for transfers between devices  25.5 us (21%)
  other arithmetic  11.1 us (9%)
  local copies, waits for them, and re-layouts  9.14 us (8%)
    pallas_call x2, Pallas kernels, ffn(): pl.pallas_call(ffn_kernel, out_shape=[jax.ShapeDtypeStruct((rows, width),...  29.8 us
    ppermute x18, starting transfers between devices, shift(): return lax.ppermute(array, 'z', [(i, (i + by) % 4) for i in range(4)])  29.1 us
    ppermute x18, waiting for transfers between devices, shift(): return lax.ppermute(array, 'z', [(i, (i + by) % 4) for i in range(4)])  25.5 us
    all_to_all x1, starting transfers between devices, local(): lax.all_to_all(sent, 'x', split_axis=0, concat_axis=0, tiled=True)  4.96 us
    all_to_all x1, starting transfers between devices, local(): lax.all_to_all(update_parts, 'y', split_axis=0, concat_axis=0, tiled=True)  4.46 us
    pallas_call x1, Pallas kernels, update_products(): pl.pallas_call(update_kernel, out_shape=[jax.ShapeDtypeStruct((share, uni...  3.08 us
    convert_element_type x2, other arithmetic, local(): outputs.append(total.astype(jnp.bfloat16))  2.92 us
    add x2, other arithmetic, local(): from_right_bottom = shift(left_bottom + from_right[half:], -1)  2.57 us
  transfers between devices with their start and end apart: 21, of which 7 were waited for; matrix products, arithmetic and copies ran while one was open for 12% of the time, Pallas kernels for 27%

profile of v3, /device:TPU:2, one launch (start us, length us, event | category | flops | bytes accessed | tf_op | source)
XLA Modules:
  0.0 120.2 jit_solution(6698189178613802097)
XLA Ops:
  0.7 0.0 copy-start.3
  0.7 2.3 %fusion.3 = (bf16[512,640]{1,0:T(8,128)(2,1)S(1)}, bf16[512,640]{1,0:T(8,128)(2,1)}) fusion(bf16[1024,640]{1,0:T(8,128)(2,1)} %param.10), kind=kLoop, calls=%fused_computation.25 | loop fusion | bytes 2621440 | tf_op jit(solution)/shard_map/slice | solution.py:235
  3.0 0.1 copy.13.weight
  3.1 2.1 %shard_map.122 = bf16[4,1920,128]{2,1,0:T(8,128)(2,1)} custom-call(s32[1]{0:T(128)} %bitcast.2.place, f32[64,1]{1,0:T(8,128)S(1)} %copy.13.weight, bf16[64,2560]{1,0:T(8,128)(2,1)S(1)} %copy-done, bf16[64,2560]{1,0:T(8,128)(2,1)S(1)} %copy-done.1, bf16[64,1280]{1,0:T(8,128)(2,1)S(1)} %copy-done.3, bf16[64,1280]{1,0:T(8,128)(2,1)S(1)} %copy-done.2, ...), custom_call_target="tpu_custom_call" | custom-call | bytes 4194304 | tf_op jit(solution)/shard_map/pallas_call | solution.py:251
  5.3 5.0 %all-to-all-start = ((bf16[4,1920,128]{2,1,0:T(8,128)(2,1)}), bf16[4,1920,128]{2,1,0:T(8,128)(2,1)S(1)}, u32[]{:S(2)}, u32[]{:S(2)}) async-start(bf16[4,1920,128]{2,1,0:T(8,128)(2,1)} %shard_map.122), calls=%async_computation | async-start | bytes 3932160 | tf_op jit(solution)/shard_map/all_to_all | solution.py:259
  10.2 1.9 %collective-permute-start.1 = (bf16[512,640]{1,0:T(8,128)(2,1)S(1)}, bf16[512,640]{1,0:T(8,128)(2,1)}, u32[]{:S(2)}, u32[]{:S(2)}) collective-permute-start(bf16[512,640]{1,0:T(8,128)(2,1)S(1)} %get-tuple-element.31.x0._), channel_id=1, source_target_pairs={{0,1},{1,2},{2,3},{3,0},{4,5},{5,6},{6,7},{7,4},{8,9},{9,10},{10,1... | collective-permute-start | bytes 1966088 | tf_op jit(solution)/shard_map/ppermute | solution.py:211
  12.2 2.1 %collective-permute-start = (bf16[512,640]{1,0:T(8,128)(2,1)S(1)}, bf16[512,640]{1,0:T(8,128)(2,1)}, u32[]{:S(2)}, u32[]{:S(2)}) collective-permute-start(bf16[512,640]{1,0:T(8,128)(2,1)S(1)} %get-tuple-element.31.x0._), channel_id=1, source_target_pairs={{0,3},{1,0},{2,1},{3,2},{4,7},{5,4},{6,5},{7,6},{8,11},{9,8},{10,9... | collective-permute-start | bytes 1966088 | tf_op jit(solution)/shard_map/ppermute | solution.py:211
  14.3 2.0 %fusion.4 = (bf16[256,640]{1,0:T(8,128)(2,1)}, bf16[256,640]{1,0:T(8,128)(2,1)}) fusion(bf16[1024,640]{1,0:T(8,128)(2,1)} %param.10), kind=kLoop, calls=%fused_computation.26 | loop fusion | bytes 1310720 | tf_op jit(solution)/shard_map/slice | solution.py:236
  16.2 0.0 collective-permute-start.9
  16.3 3.2 %collective-permute-start.10 = (bf16[256,640]{1,0:T(8,128)(2,1)}, bf16[256,640]{1,0:T(8,128)(2,1)}, u32[]{:S(2)}, u32[]{:S(2)}) collective-permute-start(bf16[256,640]{1,0:T(8,128)(2,1)} %get-tuple-element.33), channel_id=1, source_target_pairs={{0,3},{1,0},{2,1},{3,2},{4,7},{5,4},{6,5},{7,6},{8,11},{9,8},{10,9... | collective-permute-start | bytes 983048 | tf_op jit(solution)/shard_map/ppermute | solution.py:211
  19.5 1.0 slice_convert_fusion.1
  20.5 9.5 %collective-permute-done.1.refs_1_ = bf16[512,640]{1,0:T(8,128)(2,1)} collective-permute-done((bf16[512,640]{1,0:T(8,128)(2,1)S(1)}, bf16[512,640]{1,0:T(8,128)(2,1)}, u32[]{:S(2)}, u32[]{:S(2)}) %collective-permute-start.1) | collective-permute-done | bytes 655392 | tf_op jit(solution)/shard_map/ppermute | solution.py:211
  30.0 1.7 %slice.134 = bf16[256,640]{1,0:T(8,128)(2,1)} slice(bf16[512,640]{1,0:T(8,128)(2,1)} %collective-permute-done.1.refs_1_), slice={[0:256], [0:640]} | slice | bytes 655360 | tf_op jit(solution)/shard_map/slice | solution.py:239
  31.7 0.0 collective-permute-done.refs_0_
  31.7 1.7 %slice.135 = bf16[256,640]{1,0:T(8,128)(2,1)} slice(bf16[512,640]{1,0:T(8,128)(2,1)} %collective-permute-done.refs_0_), slice={[256:512], [0:640]} | slice | bytes 655360 | tf_op jit(solution)/shard_map/slice | solution.py:240
  33.5 3.2 %collective-permute-start.3 = (bf16[256,640]{1,0:T(8,128)(2,1)}, bf16[256,640]{1,0:T(8,128)(2,1)}, u32[]{:S(2)}, u32[]{:S(2)}) collective-permute-start(bf16[256,640]{1,0:T(8,128)(2,1)} %slice.135), channel_id=1, source_target_pairs={{0,3},{1,0},{2,1},{3,2},{4,7},{5,4},{6,5},{7,6},{8,11},{9,8},{10,9... | collective-permute-start | bytes 983048 | tf_op jit(solution)/shard_map/ppermute | solution.py:211
  36.7 0.0 all-to-all-done.gathered
  36.7 0.1 slice.140
  36.8 0.1 collective-permute-start.14
  37.0 0.1 collective-permute-done.9.refs_1_
  37.1 3.2 %collective-permute-start.8 = (bf16[256,640]{1,0:T(8,128)(2,1)}, bf16[256,640]{1,0:T(8,128)(2,1)S(1)}, u32[]{:S(2)}, u32[]{:S(2)}) collective-permute-start(bf16[256,640]{1,0:T(8,128)(2,1)} %get-tuple-element.34), channel_id=1, source_target_pairs={{0,3},{1,0},{2,1},{3,2},{4,7},{5,4},{6,5},{7,6},{8,11},{9,8},{10,9... | collective-permute-start | bytes 983048 | tf_op jit(solution)/shard_map/ppermute | solution.py:211
  40.3 3.2 %collective-permute-done.2.refs_2_ = bf16[256,640]{1,0:T(8,128)(2,1)} collective-permute-done((bf16[256,640]{1,0:T(8,128)(2,1)}, bf16[256,640]{1,0:T(8,128)(2,1)}, u32[]{:S(2)}, u32[]{:S(2)}) %collective-permute-start.2) | collective-permute-done | bytes 327712 | tf_op jit(solution)/shard_map/ppermute | solution.py:211
  43.5 0.2 collective-permute-start.12
  43.7 3.1 %collective-permute-start.13 = (bf16[256,640]{1,0:T(8,128)(2,1)}, bf16[256,640]{1,0:T(8,128)(2,1)S(1)}, u32[]{:S(2)}, u32[]{:S(2)}) collective-permute-start(bf16[256,640]{1,0:T(8,128)(2,1)} %collective-permute-done.10.refs_2_), channel_id=1, source_target_pairs={{0,3},{1,0},{2,1},{3,2},{4,7},{5,4},{6,5},{7,6},{8,11},{9,8},{10,9... | collective-permute-start | bytes 983048 | tf_op jit(solution)/shard_map/ppermute | solution.py:211
  46.7 15.0 %shard_map.121 = (f32[512,640]{1,0:T(8,128)}, bf16[512,640]{1,0:T(8,128)(2,1)S(1)}, bf16[512,640]{1,0:T(8,128)(2,1)S(1)}, bf16[256,640]{1,0:T(8,128)(2,1)S(1)}, bf16[256,640]{1,0:T(8,128)(2,1)S(1)}) custom-call(s32[1]{0:T(128)} %bitcast.place.refs_12_, bf16[512,640]{1,0:T(8,128)(2,1)S(1)} %get-tuple-element.31.x0._, ...), custom_call_target="tpu_custom_call" | custom-call | flops 13421772800 | bytes 23592960 | tf_op jit(solution)/shard_map/pallas_call | solution.py:131
  61.7 1.8 %collective-permute-start.6 = (bf16[512,640]{1,0:T(8,128)(2,1)S(1)}, bf16[512,640]{1,0:T(8,128)(2,1)S(1)}, u32[]{:S(2)}, u32[]{:S(2)}) collective-permute-start(bf16[512,640]{1,0:T(8,128)(2,1)S(1)} %get-tuple-element.18), channel_id=1, source_target_pairs={{0,3},{1,0},{2,1},{3,2},{4,7},{5,4},{6,5},{7,6},{8,11},{9,8},{10,9... | collective-permute-start | bytes 1966088 | tf_op jit(solution)/shard_map/ppermute | solution.py:211
  63.6 3.1 %shard_map.123 = (f32[160,1280]{1,0:T(8,128)S(1)}, bf16[4,160,1280]{2,1,0:T(8,128)(2,1)}) custom-call(s32[1]{0:T(128)} %bitcast.1.place, bf16[4,1920,128]{2,1,0:T(8,128)(2,1)S(1)} %all-to-all-done.gathered, bf16[4,1600,128]{2,1,0:T(8,128)(2,1)S(1)} %collective-permute-done.14.swapped), custom_call_target="tpu_custom_call" | custom-call | flops 3355443200 | bytes 8388608 | tf_op jit(solution)/shard_map/pallas_call | solution.py:194
  66.7 0.3 collective-permute-start.4
  66.9 14.8 %shard_map.124 = (f32[512,640]{1,0:T(8,128)}, bf16[512,640]{1,0:T(8,128)(2,1)S(1)}, bf16[512,640]{1,0:T(8,128)(2,1)}, bf16[256,640]{1,0:T(8,128)(2,1)S(1)}, bf16[256,640]{1,0:T(8,128)(2,1)S(1)}) custom-call(s32[1]{0:T(128)} %bitcast.place.refs_12_, bf16[512,640]{1,0:T(8,128)(2,1)} %get-tuple-element.32.x0, ...), custom_call_target="tpu_custom_call" | custom-call | flops 13421772800 | bytes 23592960 | tf_op jit(solution)/shard_map/pallas_call | solution.py:131
  81.8 3.1 %collective-permute-start.17 = (bf16[512,640]{1,0:T(8,128)(2,1)}, bf16[512,640]{1,0:T(8,128)(2,1)}, u32[]{:S(2)}, u32[]{:S(2)}) collective-permute-start(bf16[512,640]{1,0:T(8,128)(2,1)} %get-tuple-element.24), channel_id=1, source_target_pairs={{0,3},{1,0},{2,1},{3,2},{4,7},{5,4},{6,5},{7,6},{8,11},{9,8},{10,9... | collective-permute-start | bytes 1966088 | tf_op jit(solution)/shard_map/ppermute | solution.py:211
  84.8 0.8 slice_add_fusion.2
  85.7 3.2 %collective-permute-start.7 = (bf16[256,640]{1,0:T(8,128)(2,1)}, bf16[256,640]{1,0:T(8,128)(2,1)}, u32[]{:S(2)}, u32[]{:S(2)}) collective-permute-start(bf16[256,640]{1,0:T(8,128)(2,1)} %slice_add_fusion.2), channel_id=1, source_target_pairs={{0,3},{1,0},{2,1},{3,2},{4,7},{5,4},{6,5},{7,6},{8,11},{9,8},{10,9... | collective-permute-start | bytes 983048 | tf_op jit(solution)/shard_map/ppermute | solution.py:211
  88.9 0.8 slice_add_fusion.3
  89.7 0.2 copy-done.12
  89.9 4.5 %all-to-all-start.1 = ((bf16[4,160,1280]{2,1,0:T(8,128)(2,1)}), bf16[4,160,1280]{2,1,0:T(8,128)(2,1)}, u32[]{:S(2)}, u32[]{:S(2)}) async-start(bf16[4,160,1280]{2,1,0:T(8,128)(2,1)} %get-tuple-element.20.refs_14_), calls=%async_computation.1 | async-start | bytes 3276800 | tf_op jit(solution)/shard_map/all_to_all | solution.py:286
  94.4 6.0 %collective-permute-done.17 = bf16[512,640]{1,0:T(8,128)(2,1)} collective-permute-done((bf16[512,640]{1,0:T(8,128)(2,1)}, bf16[512,640]{1,0:T(8,128)(2,1)}, u32[]{:S(2)}, u32[]{:S(2)}) %collective-permute-start.17) | collective-permute-done | bytes 655392 | tf_op jit(solution)/shard_map/ppermute | solution.py:211
  100.3 1.7 %slice_add_fusion = bf16[256,640]{1,0:T(8,128)(2,1)} fusion(bf16[256,640]{1,0:T(8,128)(2,1)S(1)} %get-tuple-element.25, bf16[512,640]{1,0:T(8,128)(2,1)} %collective-permute-done.17), kind=kLoop, calls=%fused_computation.17 | loop fusion | flops 163840 | bytes 983040 | tf_op jit(solution)/shard_map/add | solution.py:296
  102.1 3.7 %collective-permute-start.18 = (bf16[256,640]{1,0:T(8,128)(2,1)}, bf16[256,640]{1,0:T(8,128)(2,1)S(1)}, u32[]{:S(2)}, u32[]{:S(2)}) collective-permute-start(bf16[256,640]{1,0:T(8,128)(2,1)} %slice_add_fusion), channel_id=1, source_target_pairs={{0,3},{1,0},{2,1},{3,2},{4,7},{5,4},{6,5},{7,6},{8,11},{9,8},{10,9... | collective-permute-start | bytes 983048 | tf_op jit(solution)/shard_map/ppermute | solution.py:211
  105.7 1.0 slice_add_fusion.1
  106.8 0.1 collective-permute-start.16
  106.9 1.3 %collective-permute-done.5 = bf16[256,640]{1,0:T(8,128)(2,1)} collective-permute-done((bf16[256,640]{1,0:T(8,128)(2,1)}, bf16[256,640]{1,0:T(8,128)(2,1)}, u32[]{:S(2)}, u32[]{:S(2)}) %collective-permute-start.5) | collective-permute-done | bytes 327712 | tf_op jit(solution)/shard_map/ppermute | solution.py:211
  108.2 1.6 %add_convert_fusion.3 = (bf16[256,640]{1,0:T(8,128)(2,1)S(1)}, bf16[256,640]{1,0:T(8,128)(2,1)S(1)}) fusion(bf16[256,640]{1,0:T(8,128)(2,1)} %collective-permute-done.5, f32[512,640]{1,0:T(8,128)S(1)} %copy-done.9, bf16[512,640]{1,0:T(8,128)(2,1)} %copy-done.11, bf16[256,640]{1,0:T(8,128)(2,1)} %collective-permute-done.7, bf16[512,640]{1,0:T(8,128)(2,1)} %copy-done.12), kind=kLoop, calls=%fused_computation.11 | loop fusion | flops 1638400 | bytes 3276800 | tf_op jit(solution)/shard_map/convert_element_type | solution.py:302
  109.8 0.9 collective-permute-done.18
  110.7 4.5 %collective-permute-done.16 = bf16[256,640]{1,0:T(8,128)(2,1)S(1)} collective-permute-done((bf16[256,640]{1,0:T(8,128)(2,1)S(1)}, bf16[256,640]{1,0:T(8,128)(2,1)S(1)}, u32[]{:S(2)}, u32[]{:S(2)}) %collective-permute-start.16) | collective-permute-done | bytes 327712 | tf_op jit(solution)/shard_map/ppermute | solution.py:211
  115.1 1.3 %add_convert_fusion.1 = (bf16[256,640]{1,0:T(8,128)(2,1)S(1)}, bf16[256,640]{1,0:T(8,128)(2,1)S(1)}) fusion(bf16[256,640]{1,0:T(8,128)(2,1)S(1)} %collective-permute-done.16, f32[512,640]{1,0:T(8,128)S(1)} %copy-done.10, bf16[512,640]{1,0:T(8,128)(2,1)} %collective-permute-done.17, bf16[256,640]{1,0:T(8,128)(2,1)S(1)} %collective-permute-done.18, ...), kind=kLoop, calls=%fused_computation.9 | loop fusion | flops 1638400 | bytes 3276800 | tf_op jit(solution)/shard_map/convert_element_type | solution.py:302
  116.5 1.2 pad_maximum_fusion
  117.6 1.7 %fusion = f32[160,1280]{1,0:T(8,128)S(1)} fusion(f32[160,1280]{1,0:T(8,128)S(1)} %get-tuple-element.26, bf16[4,160,1280]{2,1,0:T(8,128)(2,1)} %all-to-all-done.1, pred[]{:T(512)S(6)} %eq.15, pred[]{:T(512)S(6)} %eq.14, pred[]{:T(512)S(6)} %eq.13, pred[]{:T(512)S(6)} %eq.12), kind=kLoop, calls=%fused_computation.2 | loop fusion | flops 2252800 | bytes 3276804 | tf_op jit(solution)/shard_map/add | solution.py:287
  119.3 0.9 slice_bitcast_fusion
  (51 shorter events, 0.2 us)
Async XLA Ops:
  0.6 2.4 %copy-start.15 = (s32[64]{0:T(128)S(1)}, s32[64]{0:T(128)}, u32[]{:S(2)}) copy-start(s32[64]{0:T(128)} %param.19) | copy-start | bytes 772
  0.6 2.5 %copy-start = (bf16[64,2560]{1,0:T(8,128)(2,1)S(1)}, bf16[64,2560]{1,0:T(8,128)(2,1)}, u32[]{:S(2)}) copy-start(bf16[64,2560]{1,0:T(8,128)(2,1)} %key_left.1) | copy-start | bytes 983044
  0.7 2.5 %copy-start.1 = (bf16[64,2560]{1,0:T(8,128)(2,1)S(1)}, bf16[64,2560]{1,0:T(8,128)(2,1)}, u32[]{:S(2)}) copy-start(bf16[64,2560]{1,0:T(8,128)(2,1)} %value_right.1) | copy-start | bytes 983044
  0.7 2.5 %copy-start.3 = (bf16[64,1280]{1,0:T(8,128)(2,1)S(1)}, bf16[64,1280]{1,0:T(8,128)(2,1)}, u32[]{:S(2)}) copy-start(bf16[64,1280]{1,0:T(8,128)(2,1)} %key_right.1) | copy-start | bytes 491524
  0.7 2.5 %copy-start.2 = (bf16[64,1280]{1,0:T(8,128)(2,1)S(1)}, bf16[64,1280]{1,0:T(8,128)(2,1)}, u32[]{:S(2)}) copy-start(bf16[64,1280]{1,0:T(8,128)(2,1)} %value_left.1) | copy-start | bytes 491524
  5.3 14.2 %copy-start.13 = (f32[2560]{0:T(1024)S(1)}, f32[2560]{0:T(1024)}, u32[]{:S(2)}) copy-start(f32[2560]{0:T(1024)} %param.11) | copy-start | bytes 30724
  5.3 14.2 %copy-start.14 = (f32[2560]{0:T(1024)S(1)}, f32[2560]{0:T(1024)}, u32[]{:S(2)}) copy-start(f32[2560]{0:T(1024)} %param.12) | copy-start | bytes 30724
  5.3 31.4 %all-to-all-start = ((bf16[4,1920,128]{2,1,0:T(8,128)(2,1)}), bf16[4,1920,128]{2,1,0:T(8,128)(2,1)S(1)}, u32[]{:S(2)}, u32[]{:S(2)}) async-start(bf16[4,1920,128]{2,1,0:T(8,128)(2,1)} %shard_map.122), calls=%async_computation | async-start | bytes 3932160 | tf_op jit(solution)/shard_map/all_to_all | solution.py:259
  10.2 19.8 %collective-permute-start.1 = (bf16[512,640]{1,0:T(8,128)(2,1)S(1)}, bf16[512,640]{1,0:T(8,128)(2,1)}, u32[]{:S(2)}, u32[]{:S(2)}) collective-permute-start(bf16[512,640]{1,0:T(8,128)(2,1)S(1)} %get-tuple-element.31.x0._), channel_id=1, source_target_pairs={{0,1},{1,2},{2,3},{3,0},{4,5},{5,6},{6,7},{7,4},{8,9},{9,10},{10,1... | collective-permute-start | bytes 1966088 | tf_op jit(solution)/shard_map/ppermute | solution.py:211
  12.2 19.6 %collective-permute-start = (bf16[512,640]{1,0:T(8,128)(2,1)S(1)}, bf16[512,640]{1,0:T(8,128)(2,1)}, u32[]{:S(2)}, u32[]{:S(2)}) collective-permute-start(bf16[512,640]{1,0:T(8,128)(2,1)S(1)} %get-tuple-element.31.x0._), channel_id=1, source_target_pairs={{0,3},{1,0},{2,1},{3,2},{4,7},{5,4},{6,5},{7,6},{8,11},{9,8},{10,9... | collective-permute-start | bytes 1966088 | tf_op jit(solution)/shard_map/ppermute | solution.py:211
  16.2 20.8 %collective-permute-start.9 = (bf16[256,640]{1,0:T(8,128)(2,1)}, bf16[256,640]{1,0:T(8,128)(2,1)}, u32[]{:S(2)}, u32[]{:S(2)}) collective-permute-start(bf16[256,640]{1,0:T(8,128)(2,1)} %get-tuple-element.34), channel_id=1, source_target_pairs={{0,1},{1,2},{2,3},{3,0},{4,5},{5,6},{6,7},{7,4},{8,9},{9,10},{10,1... | collective-permute-start | bytes 983048 | tf_op jit(solution)/shard_map/ppermute | solution.py:211
  16.3 20.8 %collective-permute-start.10 = (bf16[256,640]{1,0:T(8,128)(2,1)}, bf16[256,640]{1,0:T(8,128)(2,1)}, u32[]{:S(2)}, u32[]{:S(2)}) collective-permute-start(bf16[256,640]{1,0:T(8,128)(2,1)} %get-tuple-element.33), channel_id=1, source_target_pairs={{0,3},{1,0},{2,1},{3,2},{4,7},{5,4},{6,5},{7,6},{8,11},{9,8},{10,9... | collective-permute-start | bytes 983048 | tf_op jit(solution)/shard_map/ppermute | solution.py:211
  31.7 11.8 %collective-permute-start.2 = (bf16[256,640]{1,0:T(8,128)(2,1)}, bf16[256,640]{1,0:T(8,128)(2,1)}, u32[]{:S(2)}, u32[]{:S(2)}) collective-permute-start(bf16[256,640]{1,0:T(8,128)(2,1)} %slice.134), channel_id=1, source_target_pairs={{0,1},{1,2},{2,3},{3,0},{4,5},{5,6},{6,7},{7,4},{8,9},{9,10},{10,1... | collective-permute-start | bytes 983048 | tf_op jit(solution)/shard_map/ppermute | solution.py:211
  33.5 3.4 %copy-start.4 = (bf16[64,1280]{1,0:T(8,128)(2,1)S(1)}, bf16[64,1280]{1,0:T(8,128)(2,1)}, u32[]{:S(2)}) copy-start(bf16[64,1280]{1,0:T(8,128)(2,1)} %key_right.1) | copy-start | bytes 491524
  33.5 13.3 %copy-start.6 = (f32[32,2560]{1,0:T(8,128)S(1)}, f32[32,2560]{1,0:T(8,128)}, u32[]{:S(2)}) copy-start(f32[32,2560]{1,0:T(8,128)} %get-tuple-element.39.refs_8_) | copy-start | bytes 983044
  33.5 13.3 %copy-start.8 = (bf16[32,2560]{1,0:T(8,128)(2,1)S(1)}, bf16[32,2560]{1,0:T(8,128)(2,1)}, u32[]{:S(2)}) copy-start(bf16[32,2560]{1,0:T(8,128)(2,1)} %get-tuple-element.48.refs_11_) | copy-start | bytes 491524
  33.5 10.2 %collective-permute-start.3 = (bf16[256,640]{1,0:T(8,128)(2,1)}, bf16[256,640]{1,0:T(8,128)(2,1)}, u32[]{:S(2)}, u32[]{:S(2)}) collective-permute-start(bf16[256,640]{1,0:T(8,128)(2,1)} %slice.135), channel_id=1, source_target_pairs={{0,3},{1,0},{2,1},{3,2},{4,7},{5,4},{6,5},{7,6},{8,11},{9,8},{10,9... | collective-permute-start | bytes 983048 | tf_op jit(solution)/shard_map/ppermute | solution.py:211
  36.8 24.9 %collective-permute-start.14 = (bf16[4,1600,128]{2,1,0:T(8,128)(2,1)S(1)}, bf16[4,1600,128]{2,1,0:T(8,128)(2,1)S(1)}, u32[]{:S(2)}, u32[]{:S(2)}) collective-permute-start(bf16[4,1600,128]{2,1,0:T(8,128)(2,1)S(1)} %slice.140), channel_id=1, source_target_pairs={{0,4},{4,0},{1,5},{5,1},{2,6},{6,2},{3,7},{7,3},{8,12},{12,8},{9,1... | collective-permute-start | bytes 4915208 | tf_op jit(solution)/shard_map/ppermute | solution.py:282
  37.0 29.6 %collective-permute-start.11 = (bf16[256,640]{1,0:T(8,128)(2,1)}, bf16[256,640]{1,0:T(8,128)(2,1)S(1)}, u32[]{:S(2)}, u32[]{:S(2)}) collective-permute-start(bf16[256,640]{1,0:T(8,128)(2,1)} %get-tuple-element.33), channel_id=1, source_target_pairs={{0,1},{1,2},{2,3},{3,0},{4,5},{5,6},{6,7},{7,4},{8,9},{9,10},{10,1... | collective-permute-start | bytes 983048 | tf_op jit(solution)/shard_map/ppermute | solution.py:211
  37.1 29.9 %collective-permute-start.8 = (bf16[256,640]{1,0:T(8,128)(2,1)}, bf16[256,640]{1,0:T(8,128)(2,1)S(1)}, u32[]{:S(2)}, u32[]{:S(2)}) collective-permute-start(bf16[256,640]{1,0:T(8,128)(2,1)} %get-tuple-element.34), channel_id=1, source_target_pairs={{0,3},{1,0},{2,1},{3,2},{4,7},{5,4},{6,5},{7,6},{8,11},{9,8},{10,9... | collective-permute-start | bytes 983048 | tf_op jit(solution)/shard_map/ppermute | solution.py:211
  43.5 23.4 %collective-permute-start.12 = (bf16[256,640]{1,0:T(8,128)(2,1)}, bf16[256,640]{1,0:T(8,128)(2,1)S(1)}, u32[]{:S(2)}, u32[]{:S(2)}) collective-permute-start(bf16[256,640]{1,0:T(8,128)(2,1)} %collective-permute-done.9.refs_1_), channel_id=1, source_target_pairs={{0,1},{1,2},{2,3},{3,0},{4,5},{5,6},{6,7},{7,4},{8,9},{9,10},{10,1... | collective-permute-start | bytes 983048 | tf_op jit(solution)/shard_map/ppermute | solution.py:211
  43.7 23.2 %collective-permute-start.13 = (bf16[256,640]{1,0:T(8,128)(2,1)}, bf16[256,640]{1,0:T(8,128)(2,1)S(1)}, u32[]{:S(2)}, u32[]{:S(2)}) collective-permute-start(bf16[256,640]{1,0:T(8,128)(2,1)} %collective-permute-done.10.refs_2_), channel_id=1, source_target_pairs={{0,3},{1,0},{2,1},{3,2},{4,7},{5,4},{6,5},{7,6},{8,11},{9,8},{10,9... | collective-permute-start | bytes 983048 | tf_op jit(solution)/shard_map/ppermute | solution.py:211
  61.7 23.1 %collective-permute-start.6 = (bf16[512,640]{1,0:T(8,128)(2,1)S(1)}, bf16[512,640]{1,0:T(8,128)(2,1)S(1)}, u32[]{:S(2)}, u32[]{:S(2)}) collective-permute-start(bf16[512,640]{1,0:T(8,128)(2,1)S(1)} %get-tuple-element.18), channel_id=1, source_target_pairs={{0,3},{1,0},{2,1},{3,2},{4,7},{5,4},{6,5},{7,6},{8,11},{9,8},{10,9... | collective-permute-start | bytes 1966088 | tf_op jit(solution)/shard_map/ppermute | solution.py:211
  63.6 3.4 %copy-start.5 = (f32[32,2560]{1,0:T(8,128)S(1)}, f32[32,2560]{1,0:T(8,128)}, u32[]{:S(2)}) copy-start(f32[32,2560]{1,0:T(8,128)} %get-tuple-element.40.refs_10_) | copy-start | bytes 983044
  63.6 3.4 %copy-start.7 = (bf16[32,2560]{1,0:T(8,128)(2,1)S(1)}, bf16[32,2560]{1,0:T(8,128)(2,1)}, u32[]{:S(2)}) copy-start(bf16[32,2560]{1,0:T(8,128)(2,1)} %get-tuple-element.47.refs_13_) | copy-start | bytes 491524
  66.7 22.2 %collective-permute-start.4 = (bf16[512,640]{1,0:T(8,128)(2,1)S(1)}, bf16[512,640]{1,0:T(8,128)(2,1)S(1)}, u32[]{:S(2)}, u32[]{:S(2)}) collective-permute-start(bf16[512,640]{1,0:T(8,128)(2,1)S(1)} %get-tuple-element.17), channel_id=1, source_target_pairs={{0,1},{1,2},{2,3},{3,0},{4,5},{5,6},{6,7},{7,4},{8,9},{9,10},{10,1... | collective-permute-start | bytes 1966088 | tf_op jit(solution)/shard_map/ppermute | solution.py:211
  81.8 18.6 %collective-permute-start.17 = (bf16[512,640]{1,0:T(8,128)(2,1)}, bf16[512,640]{1,0:T(8,128)(2,1)}, u32[]{:S(2)}, u32[]{:S(2)}) collective-permute-start(bf16[512,640]{1,0:T(8,128)(2,1)} %get-tuple-element.24), channel_id=1, source_target_pairs={{0,3},{1,0},{2,1},{3,2},{4,7},{5,4},{6,5},{7,6},{8,11},{9,8},{10,9... | collective-permute-start | bytes 1966088 | tf_op jit(solution)/shard_map/ppermute | solution.py:211
  84.8 20.9 %collective-permute-start.15 = (bf16[512,640]{1,0:T(8,128)(2,1)S(1)}, bf16[512,640]{1,0:T(8,128)(2,1)}, u32[]{:S(2)}, u32[]{:S(2)}) collective-permute-start(bf16[512,640]{1,0:T(8,128)(2,1)S(1)} %get-tuple-element.23), channel_id=1, source_target_pairs={{0,1},{1,2},{2,3},{3,0},{4,5},{5,6},{6,7},{7,4},{8,9},{9,10},{10,1... | collective-permute-start | bytes 1966088 | tf_op jit(solution)/shard_map/ppermute | solution.py:211
  84.8 4.9 %copy-start.11 = (bf16[512,640]{1,0:T(8,128)(2,1)}, bf16[512,640]{1,0:T(8,128)(2,1)S(1)}, u32[]{:S(2)}) copy-start(bf16[512,640]{1,0:T(8,128)(2,1)S(1)} %collective-permute-done.6) | copy-start | bytes 1966084
  85.7 21.2 %collective-permute-start.7 = (bf16[256,640]{1,0:T(8,128)(2,1)}, bf16[256,640]{1,0:T(8,128)(2,1)}, u32[]{:S(2)}, u32[]{:S(2)}) collective-permute-start(bf16[256,640]{1,0:T(8,128)(2,1)} %slice_add_fusion.2), channel_id=1, source_target_pairs={{0,3},{1,0},{2,1},{3,2},{4,7},{5,4},{6,5},{7,6},{8,11},{9,8},{10,9... | collective-permute-start | bytes 983048 | tf_op jit(solution)/shard_map/ppermute | solution.py:211
  88.9 1.0 copy-start.12
  89.7 18.5 %collective-permute-start.5 = (bf16[256,640]{1,0:T(8,128)(2,1)}, bf16[256,640]{1,0:T(8,128)(2,1)}, u32[]{:S(2)}, u32[]{:S(2)}) collective-permute-start(bf16[256,640]{1,0:T(8,128)(2,1)} %slice_add_fusion.3), channel_id=1, source_target_pairs={{0,1},{1,2},{2,3},{3,0},{4,5},{5,6},{6,7},{7,4},{8,9},{9,10},{10,1... | collective-permute-start | bytes 983048 | tf_op jit(solution)/shard_map/ppermute | solution.py:211
  89.9 27.7 %all-to-all-start.1 = ((bf16[4,160,1280]{2,1,0:T(8,128)(2,1)}), bf16[4,160,1280]{2,1,0:T(8,128)(2,1)}, u32[]{:S(2)}, u32[]{:S(2)}) async-start(bf16[4,160,1280]{2,1,0:T(8,128)(2,1)} %get-tuple-element.20.refs_14_), calls=%async_computation.1 | async-start | bytes 3276800 | tf_op jit(solution)/shard_map/all_to_all | solution.py:286
  94.4 13.8 %copy-start.9 = (f32[512,640]{1,0:T(8,128)S(1)}, f32[512,640]{1,0:T(8,128)}, u32[]{:S(2)}) copy-start(f32[512,640]{1,0:T(8,128)} %get-tuple-element.15) | copy-start | bytes 3932164
  102.1 8.6 %collective-permute-start.18 = (bf16[256,640]{1,0:T(8,128)(2,1)}, bf16[256,640]{1,0:T(8,128)(2,1)S(1)}, u32[]{:S(2)}, u32[]{:S(2)}) collective-permute-start(bf16[256,640]{1,0:T(8,128)(2,1)} %slice_add_fusion), channel_id=1, source_target_pairs={{0,3},{1,0},{2,1},{3,2},{4,7},{5,4},{6,5},{7,6},{8,11},{9,8},{10,9... | collective-permute-start | bytes 983048 | tf_op jit(solution)/shard_map/ppermute | solution.py:211
  106.8 8.4 %collective-permute-start.16 = (bf16[256,640]{1,0:T(8,128)(2,1)S(1)}, bf16[256,640]{1,0:T(8,128)(2,1)S(1)}, u32[]{:S(2)}, u32[]{:S(2)}) collective-permute-start(bf16[256,640]{1,0:T(8,128)(2,1)S(1)} %slice_add_fusion.1), channel_id=1, source_target_pairs={{0,1},{1,2},{2,3},{3,0},{4,5},{5,6},{6,7},{7,4},{8,9},{9,10},{10,1... | collective-permute-start | bytes 983048 | tf_op jit(solution)/shard_map/ppermute | solution.py:211
  108.2 6.9 %copy-start.10 = (f32[512,640]{1,0:T(8,128)S(1)}, f32[512,640]{1,0:T(8,128)}, u32[]{:S(2)}) copy-start(f32[512,640]{1,0:T(8,128)} %get-tuple-element.21) | copy-start | bytes 3932164

commit v4 on v3

--- a/solution.py
+++ b/solution.py
@@ -143,7 +143,7 @@
         ],
         compiler_params=pltpu.CompilerParams(vmem_limit_bytes=50 * MIB),
         cost_estimate=pl.CostEstimate(
-            flops=8 * rows * D * units,
+            flops=16 * rows * D * units,
             bytes_accessed=4 * D * units + 8 * rows * D,
             transcendentals=rows,
         ),
@@ -186,6 +186,16 @@
             sums[y, side * share : (side + 1) * share, :] = total[y * share : (y + 1) * share]
     own[...] = sums[place[0]]
     parts[...] = sums[...].astype(jnp.bfloat16)
+
+
+def update_sum_kernel(place, own, parts, key_update, value_update):
+    share = key_update.shape[0]
+    for side, target in enumerate((key_update, value_update)):
+        span = pl.ds(side * share, share)
+        total = own[span, :]
+        for y in range(4):
+            total += jnp.where(place[0] == y, 0.0, parts[y, span, :].astype(jnp.float32))
+        target[...] = total
 
 
 def update_products(gathered, swapped, units):
@@ -284,10 +294,16 @@
             place_after = update_parts
 
     update_parts = lax.all_to_all(update_parts, "y", split_axis=0, concat_axis=0, tiled=True)
-    update = sum(
-        jnp.where(lax.axis_index("y") == y, update_own, update_parts[y].astype(jnp.float32))
-        for y in range(4)
-    )
+    y = lax.axis_index("y").astype(jnp.int32).reshape(1)
+    share = update_own.shape[0] // 2
+    key_update, value_update = pl.pallas_call(
+        update_sum_kernel,
+        out_shape=[jax.ShapeDtypeStruct((share, units), jnp.float32)] * 2,
+        in_specs=[SMEM, VMEM, VMEM],
+        out_specs=[VMEM] * 2,
+        compiler_params=pltpu.CompilerParams(vmem_limit_bytes=6 * MIB),
+        cost_estimate=pl.CostEstimate(flops=0, bytes_accessed=3 * MIB, transcendentals=0),
+    )(y, update_own, update_parts)
 
     outputs = []
     for own, to_right, to_left, right_top, left_bottom in results:
@@ -300,8 +316,7 @@
         ):
             total = mine + (one.astype(jnp.float32) + two.astype(jnp.float32))
             outputs.append(total.astype(jnp.bfloat16))
-    share = update.shape[0] // 2
-    return (jnp.concatenate(outputs, axis=0), update[:share], update[share:].T)
+    return (jnp.concatenate(outputs, axis=0), key_update, value_update.T)
 
 
 def solution(mesh):

time: 121 us -> 119 us (0.983)
  starting transfers between devices: 38.6 us -> 32.3 us
  waiting for transfers between devices: 25.5 us -> 31.2 us
  other arithmetic: 11.1 us -> 8.67 us
  Pallas kernels: 35 us -> 36.3 us
    all_to_all x1, waiting for transfers between devices: 0.01 us -> 7.41 us  [local(): lax.all_to_all(sent, 'x', split_axis=0, concat_axis=0, tiled=True)]
    ppermute x18, starting transfers between devices: 29.1 us -> 22.8 us  [shift(): return lax.ppermute(array, 'z', [(i, (i + by) % 4) for i in range(4)])]
    ppermute x18, waiting for transfers between devices: 25.5 us -> 23.8 us  [shift(): return lax.ppermute(array, 'z', [(i, (i + by) % 4) for i in range(4)])]
    add x1 -> x0, other arithmetic: 1.67 us -> none  [local(): sum((jnp.where(lax.axis_index('y') == y, update_own, update_parts[y].asty...]
  transfers between devices with their start and end apart: 21 -> 21, of which waited for: 7 -> 8; matrix products, arithmetic and copies ran while one was open for 12% -> 13% of each run, Pallas kernels for 27% -> 30%
where the time goes in v4:
time: 119 us; the launch traced here: 118 us
  Pallas kernels  36.3 us (31%)
  starting transfers between devices  32.3 us (27%)
  waiting for transfers between devices  31.2 us (26%)
  local copies, waits for them, and re-layouts  8.79 us (7%)
  other arithmetic  8.67 us (7%)
    pallas_call x2, Pallas kernels, ffn(): pl.pallas_call(ffn_kernel, out_shape=[jax.ShapeDtypeStruct((rows, width),...  30 us
    ppermute x18, waiting for transfers between devices, shift(): return lax.ppermute(array, 'z', [(i, (i + by) % 4) for i in range(4)])  23.8 us
    ppermute x18, starting transfers between devices, shift(): return lax.ppermute(array, 'z', [(i, (i + by) % 4) for i in range(4)])  22.8 us
    all_to_all x1, waiting for transfers between devices, local(): lax.all_to_all(sent, 'x', split_axis=0, concat_axis=0, tiled=True)  7.41 us
    all_to_all x1, starting transfers between devices, local(): lax.all_to_all(sent, 'x', split_axis=0, concat_axis=0, tiled=True)  4.96 us
    all_to_all x1, starting transfers between devices, local(): lax.all_to_all(update_parts, 'y', split_axis=0, concat_axis=0, tiled=True)  4.46 us
    pallas_call x1, Pallas kernels, update_products(): pl.pallas_call(update_kernel, out_shape=[jax.ShapeDtypeStruct((share, uni...  3.07 us
    convert_element_type x2, other arithmetic, local(): outputs.append(total.astype(jnp.bfloat16))  2.86 us
  transfers between devices with their start and end apart: 21, of which 8 were waited for; matrix products, arithmetic and copies ran while one was open for 13% of the time, Pallas kernels for 30%

profile of v4, /device:TPU:2, one launch (start us, length us, event | category | flops | bytes accessed | tf_op | source)
XLA Modules:
  0.0 118.1 jit_solution(8330012037394202675)
XLA Ops:
  0.7 0.0 copy-start.3
  0.7 2.3 %fusion = (bf16[512,640]{1,0:T(8,128)(2,1)S(1)}, bf16[512,640]{1,0:T(8,128)(2,1)}) fusion(bf16[1024,640]{1,0:T(8,128)(2,1)} %param.10), kind=kLoop, calls=%fused_computation.13 | loop fusion | bytes 2621440 | tf_op jit(solution)/shard_map/slice | solution.py:245
  3.0 1.9 %collective-permute-start.1 = (bf16[512,640]{1,0:T(8,128)(2,1)S(1)}, bf16[512,640]{1,0:T(8,128)(2,1)}, u32[]{:S(2)}, u32[]{:S(2)}) collective-permute-start(bf16[512,640]{1,0:T(8,128)(2,1)S(1)} %get-tuple-element.35.x0._), channel_id=1, source_target_pairs={{0,1},{1,2},{2,3},{3,0},{4,5},{5,6},{6,7},{7,4},{8,9},{9,10},{10,1... | collective-permute-start | bytes 1966088 | tf_op jit(solution)/shard_map/ppermute | solution.py:221
  4.9 2.1 %collective-permute-start = (bf16[512,640]{1,0:T(8,128)(2,1)S(1)}, bf16[512,640]{1,0:T(8,128)(2,1)}, u32[]{:S(2)}, u32[]{:S(2)}) collective-permute-start(bf16[512,640]{1,0:T(8,128)(2,1)S(1)} %get-tuple-element.35.x0._), channel_id=1, source_target_pairs={{0,3},{1,0},{2,1},{3,2},{4,7},{5,4},{6,5},{7,6},{8,11},{9,8},{10,9... | collective-permute-start | bytes 1966088 | tf_op jit(solution)/shard_map/ppermute | solution.py:221
  7.0 0.1 copy.13.weight
  7.2 2.1 %shard_map.122 = bf16[4,1920,128]{2,1,0:T(8,128)(2,1)} custom-call(s32[1]{0:T(128)} %bitcast.2.place, f32[64,1]{1,0:T(8,128)S(1)} %copy.13.weight, bf16[64,2560]{1,0:T(8,128)(2,1)S(1)} %copy-done, bf16[64,2560]{1,0:T(8,128)(2,1)S(1)} %copy-done.1, bf16[64,1280]{1,0:T(8,128)(2,1)S(1)} %copy-done.3, bf16[64,1280]{1,0:T(8,128)(2,1)S(1)} %copy-done.2, ...), custom_call_target="tpu_custom_call" | custom-call | bytes 4194304 | tf_op jit(solution)/shard_map/pallas_call | solution.py:261
  9.3 5.0 %all-to-all-start = ((bf16[4,1920,128]{2,1,0:T(8,128)(2,1)}), bf16[4,1920,128]{2,1,0:T(8,128)(2,1)S(1)}, u32[]{:S(2)}, u32[]{:S(2)}) async-start(bf16[4,1920,128]{2,1,0:T(8,128)(2,1)} %shard_map.122), calls=%async_computation | async-start | bytes 3932160 | tf_op jit(solution)/shard_map/all_to_all | solution.py:269
  14.3 2.0 %fusion.1 = (bf16[256,640]{1,0:T(8,128)(2,1)}, bf16[256,640]{1,0:T(8,128)(2,1)}) fusion(bf16[1024,640]{1,0:T(8,128)(2,1)} %param.10), kind=kLoop, calls=%fused_computation.14 | loop fusion | bytes 1310720 | tf_op jit(solution)/shard_map/slice | solution.py:246
  16.2 2.0 %collective-permute-start.10 = (bf16[256,640]{1,0:T(8,128)(2,1)}, bf16[256,640]{1,0:T(8,128)(2,1)}, u32[]{:S(2)}, u32[]{:S(2)}) collective-permute-start(bf16[256,640]{1,0:T(8,128)(2,1)} %get-tuple-element.37), channel_id=1, source_target_pairs={{0,3},{1,0},{2,1},{3,2},{4,7},{5,4},{6,5},{7,6},{8,11},{9,8},{10,9... | collective-permute-start | bytes 983048 | tf_op jit(solution)/shard_map/ppermute | solution.py:221
  18.3 0.0 collective-permute-start.9
  18.4 0.0 copy-start.4
  18.4 0.9 slice_convert_fusion.1
  19.3 3.4 %collective-permute-done.1.refs_1_ = bf16[512,640]{1,0:T(8,128)(2,1)} collective-permute-done((bf16[512,640]{1,0:T(8,128)(2,1)S(1)}, bf16[512,640]{1,0:T(8,128)(2,1)}, u32[]{:S(2)}, u32[]{:S(2)}) %collective-permute-start.1) | collective-permute-done | bytes 655392 | tf_op jit(solution)/shard_map/ppermute | solution.py:221
  22.7 1.7 %slice.110 = bf16[256,640]{1,0:T(8,128)(2,1)} slice(bf16[512,640]{1,0:T(8,128)(2,1)} %collective-permute-done.1.refs_1_), slice={[0:256], [0:640]} | slice | bytes 655360 | tf_op jit(solution)/shard_map/slice | solution.py:249
  24.4 1.7 %slice.111 = bf16[256,640]{1,0:T(8,128)(2,1)} slice(bf16[512,640]{1,0:T(8,128)(2,1)} %collective-permute-done.refs_0_), slice={[256:512], [0:640]} | slice | bytes 655360 | tf_op jit(solution)/shard_map/slice | solution.py:250
  26.2 3.2 %collective-permute-start.3 = (bf16[256,640]{1,0:T(8,128)(2,1)}, bf16[256,640]{1,0:T(8,128)(2,1)}, u32[]{:S(2)}, u32[]{:S(2)}) collective-permute-start(bf16[256,640]{1,0:T(8,128)(2,1)} %slice.111), channel_id=1, source_target_pairs={{0,3},{1,0},{2,1},{3,2},{4,7},{5,4},{6,5},{7,6},{8,11},{9,8},{10,9... | collective-permute-start | bytes 983048 | tf_op jit(solution)/shard_map/ppermute | solution.py:221
  29.4 0.7 fusion.3
  30.1 7.4 %all-to-all-done.gathered = bf16[4,1920,128]{2,1,0:T(8,128)(2,1)S(1)} async-done(((bf16[4,1920,128]{2,1,0:T(8,128)(2,1)}), bf16[4,1920,128]{2,1,0:T(8,128)(2,1)S(1)}, u32[]{:S(2)}, u32[]{:S(2)}) %all-to-all-start) | async-done | bytes 1966112 | tf_op jit(solution)/shard_map/all_to_all | solution.py:269
  37.5 0.1 slice.116
  37.6 1.8 %collective-permute-start.8 = (bf16[256,640]{1,0:T(8,128)(2,1)}, bf16[256,640]{1,0:T(8,128)(2,1)S(1)}, u32[]{:S(2)}, u32[]{:S(2)}) collective-permute-start(bf16[256,640]{1,0:T(8,128)(2,1)} %get-tuple-element.38), channel_id=1, source_target_pairs={{0,3},{1,0},{2,1},{3,2},{4,7},{5,4},{6,5},{7,6},{8,11},{9,8},{10,9... | collective-permute-start | bytes 983048 | tf_op jit(solution)/shard_map/ppermute | solution.py:221
  39.4 0.3 collective-permute-start.12
  39.7 4.7 %collective-permute-done.2.refs_2_ = bf16[256,640]{1,0:T(8,128)(2,1)} collective-permute-done((bf16[256,640]{1,0:T(8,128)(2,1)}, bf16[256,640]{1,0:T(8,128)(2,1)}, u32[]{:S(2)}, u32[]{:S(2)}) %collective-permute-start.2) | collective-permute-done | bytes 327712 | tf_op jit(solution)/shard_map/ppermute | solution.py:221
  44.4 1.4 %collective-permute-start.13 = (bf16[256,640]{1,0:T(8,128)(2,1)}, bf16[256,640]{1,0:T(8,128)(2,1)S(1)}, u32[]{:S(2)}, u32[]{:S(2)}) collective-permute-start(bf16[256,640]{1,0:T(8,128)(2,1)} %collective-permute-done.10.refs_2_), channel_id=1, source_target_pairs={{0,3},{1,0},{2,1},{3,2},{4,7},{5,4},{6,5},{7,6},{8,11},{9,8},{10,9... | collective-permute-start | bytes 983048 | tf_op jit(solution)/shard_map/ppermute | solution.py:221
  45.9 15.0 %shard_map.121 = (f32[512,640]{1,0:T(8,128)}, bf16[512,640]{1,0:T(8,128)(2,1)S(1)}, bf16[512,640]{1,0:T(8,128)(2,1)S(1)}, bf16[256,640]{1,0:T(8,128)(2,1)S(1)}, bf16[256,640]{1,0:T(8,128)(2,1)S(1)}) custom-call(s32[1]{0:T(128)} %bitcast.place.refs_12_, bf16[512,640]{1,0:T(8,128)(2,1)S(1)} %get-tuple-element.35.x0._, ...), custom_call_target="tpu_custom_call" | custom-call | flops 26843545600 | bytes 23592960 | tf_op jit(solution)/shard_map/pallas_call | solution.py:131
  60.9 0.5 collective-permute-start.6
  61.4 3.1 %shard_map.123 = (f32[160,1280]{1,0:T(8,128)S(1)}, bf16[4,160,1280]{2,1,0:T(8,128)(2,1)}) custom-call(s32[1]{0:T(128)} %bitcast.1.place, bf16[4,1920,128]{2,1,0:T(8,128)(2,1)S(1)} %all-to-all-done.gathered, bf16[4,1600,128]{2,1,0:T(8,128)(2,1)S(1)} %collective-permute-done.14.swapped), custom_call_target="tpu_custom_call" | custom-call | flops 3355443200 | bytes 8388608 | tf_op jit(solution)/shard_map/pallas_call | solution.py:204
  64.4 1.6 %collective-permute-start.4 = (bf16[512,640]{1,0:T(8,128)(2,1)S(1)}, bf16[512,640]{1,0:T(8,128)(2,1)S(1)}, u32[]{:S(2)}, u32[]{:S(2)}) collective-permute-start(bf16[512,640]{1,0:T(8,128)(2,1)S(1)} %get-tuple-element.19), channel_id=1, source_target_pairs={{0,1},{1,2},{2,3},{3,0},{4,5},{5,6},{6,7},{7,4},{8,9},{9,10},{10,1... | collective-permute-start | bytes 1966088 | tf_op jit(solution)/shard_map/ppermute | solution.py:221
  66.1 15.0 %shard_map.124 = (f32[512,640]{1,0:T(8,128)}, bf16[512,640]{1,0:T(8,128)(2,1)}, bf16[512,640]{1,0:T(8,128)(2,1)}, bf16[256,640]{1,0:T(8,128)(2,1)S(1)}, bf16[256,640]{1,0:T(8,128)(2,1)S(1)}) custom-call(s32[1]{0:T(128)} %bitcast.place.refs_12_, bf16[512,640]{1,0:T(8,128)(2,1)} %get-tuple-element.36.x0, bf16[256,640]{1,0:T(8,128)(2,1)S(1)} %collective-permute-done.8.refs_0_, ...), custom_call_target="tpu_custom_call" | custom-call | flops 26843545600 | bytes 23592960 | tf_op jit(solution)/shard_map/pallas_call | solution.py:131
  81.1 1.7 %collective-permute-start.17 = (bf16[512,640]{1,0:T(8,128)(2,1)}, bf16[512,640]{1,0:T(8,128)(2,1)}, u32[]{:S(2)}, u32[]{:S(2)}) collective-permute-start(bf16[512,640]{1,0:T(8,128)(2,1)} %get-tuple-element.26), channel_id=1, source_target_pairs={{0,3},{1,0},{2,1},{3,2},{4,7},{5,4},{6,5},{7,6},{8,11},{9,8},{10,9... | collective-permute-start | bytes 1966088 | tf_op jit(solution)/shard_map/ppermute | solution.py:221
  82.8 0.4 collective-permute-start.15
  83.2 0.8 slice_add_fusion.2
  84.0 2.8 %collective-permute-start.7 = (bf16[256,640]{1,0:T(8,128)(2,1)}, bf16[256,640]{1,0:T(8,128)(2,1)}, u32[]{:S(2)}, u32[]{:S(2)}) collective-permute-start(bf16[256,640]{1,0:T(8,128)(2,1)} %slice_add_fusion.2), channel_id=1, source_target_pairs={{0,3},{1,0},{2,1},{3,2},{4,7},{5,4},{6,5},{7,6},{8,11},{9,8},{10,9... | collective-permute-start | bytes 983048 | tf_op jit(solution)/shard_map/ppermute | solution.py:221
  86.8 0.8 slice_add_fusion.3
  87.7 0.1 copy-done.14
  87.8 4.5 %all-to-all-start.1 = ((bf16[4,160,1280]{2,1,0:T(8,128)(2,1)}), bf16[4,160,1280]{2,1,0:T(8,128)(2,1)S(1)}, u32[]{:S(2)}, u32[]{:S(2)}) async-start(bf16[4,160,1280]{2,1,0:T(8,128)(2,1)} %get-tuple-element.22.refs_14_), calls=%async_computation.1 | async-start | bytes 3276800 | tf_op jit(solution)/shard_map/all_to_all | solution.py:296
  92.3 6.8 %collective-permute-done.17 = bf16[512,640]{1,0:T(8,128)(2,1)} collective-permute-done((bf16[512,640]{1,0:T(8,128)(2,1)}, bf16[512,640]{1,0:T(8,128)(2,1)}, u32[]{:S(2)}, u32[]{:S(2)}) %collective-permute-start.17) | collective-permute-done | bytes 655392 | tf_op jit(solution)/shard_map/ppermute | solution.py:221
  99.1 1.0 slice_add_fusion
  100.1 2.9 %collective-permute-start.18 = (bf16[256,640]{1,0:T(8,128)(2,1)S(1)}, bf16[256,640]{1,0:T(8,128)(2,1)S(1)}, u32[]{:S(2)}, u32[]{:S(2)}) collective-permute-start(bf16[256,640]{1,0:T(8,128)(2,1)S(1)} %slice_add_fusion), channel_id=1, source_target_pairs={{0,3},{1,0},{2,1},{3,2},{4,7},{5,4},{6,5},{7,6},{8,11},{9,8},{10,9... | collective-permute-start | bytes 983048 | tf_op jit(solution)/shard_map/ppermute | solution.py:221
  103.0 1.0 slice_add_fusion.1
  104.0 0.1 collective-permute-start.16
  104.1 2.0 %collective-permute-done.7 = bf16[256,640]{1,0:T(8,128)(2,1)} collective-permute-done((bf16[256,640]{1,0:T(8,128)(2,1)}, bf16[256,640]{1,0:T(8,128)(2,1)}, u32[]{:S(2)}, u32[]{:S(2)}) %collective-permute-start.7) | collective-permute-done | bytes 327712 | tf_op jit(solution)/shard_map/ppermute | solution.py:221
  106.1 2.9 %collective-permute-done.5 = bf16[256,640]{1,0:T(8,128)(2,1)} collective-permute-done((bf16[256,640]{1,0:T(8,128)(2,1)}, bf16[256,640]{1,0:T(8,128)(2,1)}, u32[]{:S(2)}, u32[]{:S(2)}) %collective-permute-start.5) | collective-permute-done | bytes 327712 | tf_op jit(solution)/shard_map/ppermute | solution.py:221
  109.0 1.5 %add_convert_fusion.3 = (bf16[256,640]{1,0:T(8,128)(2,1)S(1)}, bf16[256,640]{1,0:T(8,128)(2,1)S(1)}) fusion(bf16[256,640]{1,0:T(8,128)(2,1)} %collective-permute-done.5, f32[512,640]{1,0:T(8,128)S(1)} %copy-done.10, bf16[512,640]{1,0:T(8,128)(2,1)S(1)} %copy-done.13, bf16[256,640]{1,0:T(8,128)(2,1)} %collective-permute-done.7, bf16[512,640]{1,0:T(8,128)(2,1)} %copy-done.14), kind=kLoop, calls=%fused_computation.4 | loop fusion | flops 1638400 | bytes 3276800 | tf_op jit(solution)/shard_map/convert_element_type | solution.py:318
  110.5 1.5 %collective-permute-done.18 = bf16[256,640]{1,0:T(8,128)(2,1)S(1)} collective-permute-done((bf16[256,640]{1,0:T(8,128)(2,1)S(1)}, bf16[256,640]{1,0:T(8,128)(2,1)S(1)}, u32[]{:S(2)}, u32[]{:S(2)}) %collective-permute-start.18) | collective-permute-done | bytes 327712 | tf_op jit(solution)/shard_map/ppermute | solution.py:221
  112.0 2.5 %collective-permute-done.16 = bf16[256,640]{1,0:T(8,128)(2,1)S(1)} collective-permute-done((bf16[256,640]{1,0:T(8,128)(2,1)S(1)}, bf16[256,640]{1,0:T(8,128)(2,1)S(1)}, u32[]{:S(2)}, u32[]{:S(2)}) %collective-permute-start.16) | collective-permute-done | bytes 327712 | tf_op jit(solution)/shard_map/ppermute | solution.py:221
  114.5 1.3 %add_convert_fusion.1 = (bf16[256,640]{1,0:T(8,128)(2,1)S(1)}, bf16[256,640]{1,0:T(8,128)(2,1)S(1)}) fusion(bf16[256,640]{1,0:T(8,128)(2,1)S(1)} %collective-permute-done.16, f32[512,640]{1,0:T(8,128)S(1)} %copy-done.11, bf16[512,640]{1,0:T(8,128)(2,1)} %collective-permute-done.17, bf16[256,640]{1,0:T(8,128)(2,1)S(1)} %collective-permute-done.18, ...), kind=kLoop, calls=%fused_computation.2 | loop fusion | flops 1638400 | bytes 3276800 | tf_op jit(solution)/shard_map/convert_element_type | solution.py:318
  115.8 1.2 pad_maximum_fusion
  117.0 1.1 shard_map.125
  (54 shorter events, 0.1 us)
Async XLA Ops:
  0.6 6.4 %copy-start.17 = (s32[64]{0:T(128)S(1)}, s32[64]{0:T(128)}, u32[]{:S(2)}) copy-start(s32[64]{0:T(128)} %param.19) | copy-start | bytes 772
  0.6 6.5 %copy-start = (bf16[64,2560]{1,0:T(8,128)(2,1)S(1)}, bf16[64,2560]{1,0:T(8,128)(2,1)}, u32[]{:S(2)}) copy-start(bf16[64,2560]{1,0:T(8,128)(2,1)} %key_left.1) | copy-start | bytes 983044
  0.7 6.5 %copy-start.1 = (bf16[64,2560]{1,0:T(8,128)(2,1)S(1)}, bf16[64,2560]{1,0:T(8,128)(2,1)}, u32[]{:S(2)}) copy-start(bf16[64,2560]{1,0:T(8,128)(2,1)} %value_right.1) | copy-start | bytes 983044
  0.7 6.5 %copy-start.3 = (bf16[64,1280]{1,0:T(8,128)(2,1)S(1)}, bf16[64,1280]{1,0:T(8,128)(2,1)}, u32[]{:S(2)}) copy-start(bf16[64,1280]{1,0:T(8,128)(2,1)} %key_right.1) | copy-start | bytes 491524
  0.7 6.5 %copy-start.2 = (bf16[64,1280]{1,0:T(8,128)(2,1)S(1)}, bf16[64,1280]{1,0:T(8,128)(2,1)}, u32[]{:S(2)}) copy-start(bf16[64,1280]{1,0:T(8,128)(2,1)} %value_left.1) | copy-start | bytes 491524
  3.0 19.7 %collective-permute-start.1 = (bf16[512,640]{1,0:T(8,128)(2,1)S(1)}, bf16[512,640]{1,0:T(8,128)(2,1)}, u32[]{:S(2)}, u32[]{:S(2)}) collective-permute-start(bf16[512,640]{1,0:T(8,128)(2,1)S(1)} %get-tuple-element.35.x0._), channel_id=1, source_target_pairs={{0,1},{1,2},{2,3},{3,0},{4,5},{5,6},{6,7},{7,4},{8,9},{9,10},{10,1... | collective-permute-start | bytes 1966088 | tf_op jit(solution)/shard_map/ppermute | solution.py:221
  4.9 19.5 %collective-permute-start = (bf16[512,640]{1,0:T(8,128)(2,1)S(1)}, bf16[512,640]{1,0:T(8,128)(2,1)}, u32[]{:S(2)}, u32[]{:S(2)}) collective-permute-start(bf16[512,640]{1,0:T(8,128)(2,1)S(1)} %get-tuple-element.35.x0._), channel_id=1, source_target_pairs={{0,3},{1,0},{2,1},{3,2},{4,7},{5,4},{6,5},{7,6},{8,11},{9,8},{10,9... | collective-permute-start | bytes 1966088 | tf_op jit(solution)/shard_map/ppermute | solution.py:221
  9.3 9.0 %copy-start.15 = (f32[2560]{0:T(1024)S(1)}, f32[2560]{0:T(1024)}, u32[]{:S(2)}) copy-start(f32[2560]{0:T(1024)} %param.11) | copy-start | bytes 30724
  9.3 9.0 %copy-start.16 = (f32[2560]{0:T(1024)S(1)}, f32[2560]{0:T(1024)}, u32[]{:S(2)}) copy-start(f32[2560]{0:T(1024)} %param.12) | copy-start | bytes 30724
  9.3 28.1 %all-to-all-start = ((bf16[4,1920,128]{2,1,0:T(8,128)(2,1)}), bf16[4,1920,128]{2,1,0:T(8,128)(2,1)S(1)}, u32[]{:S(2)}, u32[]{:S(2)}) async-start(bf16[4,1920,128]{2,1,0:T(8,128)(2,1)} %shard_map.122), calls=%async_computation | async-start | bytes 3932160 | tf_op jit(solution)/shard_map/all_to_all | solution.py:269
  16.2 23.2 %collective-permute-start.10 = (bf16[256,640]{1,0:T(8,128)(2,1)}, bf16[256,640]{1,0:T(8,128)(2,1)}, u32[]{:S(2)}, u32[]{:S(2)}) collective-permute-start(bf16[256,640]{1,0:T(8,128)(2,1)} %get-tuple-element.37), channel_id=1, source_target_pairs={{0,3},{1,0},{2,1},{3,2},{4,7},{5,4},{6,5},{7,6},{8,11},{9,8},{10,9... | collective-permute-start | bytes 983048 | tf_op jit(solution)/shard_map/ppermute | solution.py:221
  18.3 46.2 %collective-permute-start.11 = (bf16[256,640]{1,0:T(8,128)(2,1)}, bf16[256,640]{1,0:T(8,128)(2,1)}, u32[]{:S(2)}, u32[]{:S(2)}) collective-permute-start(bf16[256,640]{1,0:T(8,128)(2,1)} %get-tuple-element.37), channel_id=1, source_target_pairs={{0,1},{1,2},{2,3},{3,0},{4,5},{5,6},{6,7},{7,4},{8,9},{9,10},{10,1... | collective-permute-start | bytes 983048 | tf_op jit(solution)/shard_map/ppermute | solution.py:221
  18.3 19.3 %collective-permute-start.9 = (bf16[256,640]{1,0:T(8,128)(2,1)}, bf16[256,640]{1,0:T(8,128)(2,1)}, u32[]{:S(2)}, u32[]{:S(2)}) collective-permute-start(bf16[256,640]{1,0:T(8,128)(2,1)} %get-tuple-element.38), channel_id=1, source_target_pairs={{0,1},{1,2},{2,3},{3,0},{4,5},{5,6},{6,7},{7,4},{8,9},{9,10},{10,1... | collective-permute-start | bytes 983048 | tf_op jit(solution)/shard_map/ppermute | solution.py:221
  18.4 11.0 %copy-start.4 = (bf16[64,1280]{1,0:T(8,128)(2,1)S(1)}, bf16[64,1280]{1,0:T(8,128)(2,1)}, u32[]{:S(2)}) copy-start(bf16[64,1280]{1,0:T(8,128)(2,1)} %key_right.1) | copy-start | bytes 491524
  24.4 19.9 %collective-permute-start.2 = (bf16[256,640]{1,0:T(8,128)(2,1)}, bf16[256,640]{1,0:T(8,128)(2,1)}, u32[]{:S(2)}, u32[]{:S(2)}) collective-permute-start(bf16[256,640]{1,0:T(8,128)(2,1)} %slice.110), channel_id=1, source_target_pairs={{0,1},{1,2},{2,3},{3,0},{4,5},{5,6},{6,7},{7,4},{8,9},{9,10},{10,1... | collective-permute-start | bytes 983048 | tf_op jit(solution)/shard_map/ppermute | solution.py:221
  26.2 19.7 %collective-permute-start.3 = (bf16[256,640]{1,0:T(8,128)(2,1)}, bf16[256,640]{1,0:T(8,128)(2,1)}, u32[]{:S(2)}, u32[]{:S(2)}) collective-permute-start(bf16[256,640]{1,0:T(8,128)(2,1)} %slice.111), channel_id=1, source_target_pairs={{0,3},{1,0},{2,1},{3,2},{4,7},{5,4},{6,5},{7,6},{8,11},{9,8},{10,9... | collective-permute-start | bytes 983048 | tf_op jit(solution)/shard_map/ppermute | solution.py:221
  30.1 15.8 %copy-start.6 = (f32[32,2560]{1,0:T(8,128)S(1)}, f32[32,2560]{1,0:T(8,128)}, u32[]{:S(2)}) copy-start(f32[32,2560]{1,0:T(8,128)} %get-tuple-element.41.refs_8_) | copy-start | bytes 983044
  30.1 15.8 %copy-start.8 = (bf16[32,2560]{1,0:T(8,128)(2,1)S(1)}, bf16[32,2560]{1,0:T(8,128)(2,1)}, u32[]{:S(2)}) copy-start(bf16[32,2560]{1,0:T(8,128)(2,1)} %get-tuple-element.50.refs_11_) | copy-start | bytes 491524
  30.1 15.8 %copy-start.9 = (bf16[32,1280]{1,0:T(8,128)(2,1)S(1)}, bf16[32,1280]{1,0:T(8,128)(2,1)}, u32[]{:S(2)}) copy-start(bf16[32,1280]{1,0:T(8,128)(2,1)} %get-tuple-element.52.refs_9_) | copy-start | bytes 245764
  37.6 28.5 %collective-permute-start.8 = (bf16[256,640]{1,0:T(8,128)(2,1)}, bf16[256,640]{1,0:T(8,128)(2,1)S(1)}, u32[]{:S(2)}, u32[]{:S(2)}) collective-permute-start(bf16[256,640]{1,0:T(8,128)(2,1)} %get-tuple-element.38), channel_id=1, source_target_pairs={{0,3},{1,0},{2,1},{3,2},{4,7},{5,4},{6,5},{7,6},{8,11},{9,8},{10,9... | collective-permute-start | bytes 983048 | tf_op jit(solution)/shard_map/ppermute | solution.py:221
  39.4 26.7 %collective-permute-start.12 = (bf16[256,640]{1,0:T(8,128)(2,1)}, bf16[256,640]{1,0:T(8,128)(2,1)S(1)}, u32[]{:S(2)}, u32[]{:S(2)}) collective-permute-start(bf16[256,640]{1,0:T(8,128)(2,1)} %collective-permute-done.9.refs_1_), channel_id=1, source_target_pairs={{0,1},{1,2},{2,3},{3,0},{4,5},{5,6},{6,7},{7,4},{8,9},{9,10},{10,1... | collective-permute-start | bytes 983048 | tf_op jit(solution)/shard_map/ppermute | solution.py:221
  44.4 21.7 %collective-permute-start.13 = (bf16[256,640]{1,0:T(8,128)(2,1)}, bf16[256,640]{1,0:T(8,128)(2,1)S(1)}, u32[]{:S(2)}, u32[]{:S(2)}) collective-permute-start(bf16[256,640]{1,0:T(8,128)(2,1)} %collective-permute-done.10.refs_2_), channel_id=1, source_target_pairs={{0,3},{1,0},{2,1},{3,2},{4,7},{5,4},{6,5},{7,6},{8,11},{9,8},{10,9... | collective-permute-start | bytes 983048 | tf_op jit(solution)/shard_map/ppermute | solution.py:221
  45.8 15.1 %collective-permute-start.14 = (bf16[4,1600,128]{2,1,0:T(8,128)(2,1)S(1)}, bf16[4,1600,128]{2,1,0:T(8,128)(2,1)S(1)}, u32[]{:S(2)}, u32[]{:S(2)}) collective-permute-start(bf16[4,1600,128]{2,1,0:T(8,128)(2,1)S(1)} %slice.116), channel_id=1, source_target_pairs={{0,4},{4,0},{1,5},{5,1},{2,6},{6,2},{3,7},{7,3},{8,12},{12,8},{9,1... | collective-permute-start | bytes 4915208 | tf_op jit(solution)/shard_map/ppermute | solution.py:292
  60.9 22.3 %collective-permute-start.6 = (bf16[512,640]{1,0:T(8,128)(2,1)S(1)}, bf16[512,640]{1,0:T(8,128)(2,1)S(1)}, u32[]{:S(2)}, u32[]{:S(2)}) collective-permute-start(bf16[512,640]{1,0:T(8,128)(2,1)S(1)} %get-tuple-element.20), channel_id=1, source_target_pairs={{0,3},{1,0},{2,1},{3,2},{4,7},{5,4},{6,5},{7,6},{8,11},{9,8},{10,9... | collective-permute-start | bytes 1966088 | tf_op jit(solution)/shard_map/ppermute | solution.py:221
  61.4 4.7 %copy-start.5 = (f32[32,2560]{1,0:T(8,128)S(1)}, f32[32,2560]{1,0:T(8,128)}, u32[]{:S(2)}) copy-start(f32[32,2560]{1,0:T(8,128)} %get-tuple-element.42.refs_10_) | copy-start | bytes 983044
  61.4 4.7 %copy-start.7 = (bf16[32,2560]{1,0:T(8,128)(2,1)S(1)}, bf16[32,2560]{1,0:T(8,128)(2,1)}, u32[]{:S(2)}) copy-start(bf16[32,2560]{1,0:T(8,128)(2,1)} %get-tuple-element.49.refs_13_) | copy-start | bytes 491524
  64.4 22.4 %collective-permute-start.4 = (bf16[512,640]{1,0:T(8,128)(2,1)S(1)}, bf16[512,640]{1,0:T(8,128)(2,1)S(1)}, u32[]{:S(2)}, u32[]{:S(2)}) collective-permute-start(bf16[512,640]{1,0:T(8,128)(2,1)S(1)} %get-tuple-element.19), channel_id=1, source_target_pairs={{0,1},{1,2},{2,3},{3,0},{4,5},{5,6},{6,7},{7,4},{8,9},{9,10},{10,1... | collective-permute-start | bytes 1966088 | tf_op jit(solution)/shard_map/ppermute | solution.py:221
  81.1 18.0 %collective-permute-start.17 = (bf16[512,640]{1,0:T(8,128)(2,1)}, bf16[512,640]{1,0:T(8,128)(2,1)}, u32[]{:S(2)}, u32[]{:S(2)}) collective-permute-start(bf16[512,640]{1,0:T(8,128)(2,1)} %get-tuple-element.26), channel_id=1, source_target_pairs={{0,3},{1,0},{2,1},{3,2},{4,7},{5,4},{6,5},{7,6},{8,11},{9,8},{10,9... | collective-permute-start | bytes 1966088 | tf_op jit(solution)/shard_map/ppermute | solution.py:221
  82.8 20.2 %collective-permute-start.15 = (bf16[512,640]{1,0:T(8,128)(2,1)}, bf16[512,640]{1,0:T(8,128)(2,1)}, u32[]{:S(2)}, u32[]{:S(2)}) collective-permute-start(bf16[512,640]{1,0:T(8,128)(2,1)} %get-tuple-element.25), channel_id=1, source_target_pairs={{0,1},{1,2},{2,3},{3,0},{4,5},{5,6},{6,7},{7,4},{8,9},{9,10},{10,1... | collective-permute-start | bytes 1966088 | tf_op jit(solution)/shard_map/ppermute | solution.py:221
  83.2 4.5 %copy-start.12 = (bf16[512,640]{1,0:T(8,128)(2,1)}, bf16[512,640]{1,0:T(8,128)(2,1)S(1)}, u32[]{:S(2)}) copy-start(bf16[512,640]{1,0:T(8,128)(2,1)S(1)} %collective-permute-done.6) | copy-start | bytes 1966084
  84.0 22.1 %collective-permute-start.7 = (bf16[256,640]{1,0:T(8,128)(2,1)}, bf16[256,640]{1,0:T(8,128)(2,1)}, u32[]{:S(2)}, u32[]{:S(2)}) collective-permute-start(bf16[256,640]{1,0:T(8,128)(2,1)} %slice_add_fusion.2), channel_id=1, source_target_pairs={{0,3},{1,0},{2,1},{3,2},{4,7},{5,4},{6,5},{7,6},{8,11},{9,8},{10,9... | collective-permute-start | bytes 983048 | tf_op jit(solution)/shard_map/ppermute | solution.py:221
  86.8 0.9 copy-start.14
  87.8 21.2 %collective-permute-start.5 = (bf16[256,640]{1,0:T(8,128)(2,1)}, bf16[256,640]{1,0:T(8,128)(2,1)}, u32[]{:S(2)}, u32[]{:S(2)}) collective-permute-start(bf16[256,640]{1,0:T(8,128)(2,1)} %slice_add_fusion.3), channel_id=1, source_target_pairs={{0,1},{1,2},{2,3},{3,0},{4,5},{5,6},{6,7},{7,4},{8,9},{9,10},{10,1... | collective-permute-start | bytes 983048 | tf_op jit(solution)/shard_map/ppermute | solution.py:221
  87.8 29.2 %all-to-all-start.1 = ((bf16[4,160,1280]{2,1,0:T(8,128)(2,1)}), bf16[4,160,1280]{2,1,0:T(8,128)(2,1)S(1)}, u32[]{:S(2)}, u32[]{:S(2)}) async-start(bf16[4,160,1280]{2,1,0:T(8,128)(2,1)} %get-tuple-element.22.refs_14_), calls=%async_computation.1 | async-start | bytes 3276800 | tf_op jit(solution)/shard_map/all_to_all | solution.py:296
  92.2 16.7 %copy-start.10 = (f32[512,640]{1,0:T(8,128)S(1)}, f32[512,640]{1,0:T(8,128)}, u32[]{:S(2)}) copy-start(f32[512,640]{1,0:T(8,128)} %get-tuple-element.17) | copy-start | bytes 3932164
  92.3 16.7 %copy-start.13 = (bf16[512,640]{1,0:T(8,128)(2,1)S(1)}, bf16[512,640]{1,0:T(8,128)(2,1)}, u32[]{:S(2)}) copy-start(bf16[512,640]{1,0:T(8,128)(2,1)} %copy-done.12) | copy-start | bytes 1966084
  100.1 11.9 %collective-permute-start.18 = (bf16[256,640]{1,0:T(8,128)(2,1)S(1)}, bf16[256,640]{1,0:T(8,128)(2,1)S(1)}, u32[]{:S(2)}, u32[]{:S(2)}) collective-permute-start(bf16[256,640]{1,0:T(8,128)(2,1)S(1)} %slice_add_fusion), channel_id=1, source_target_pairs={{0,3},{1,0},{2,1},{3,2},{4,7},{5,4},{6,5},{7,6},{8,11},{9,8},{10,9... | collective-permute-start | bytes 983048 | tf_op jit(solution)/shard_map/ppermute | solution.py:221
  104.0 10.5 %collective-permute-start.16 = (bf16[256,640]{1,0:T(8,128)(2,1)S(1)}, bf16[256,640]{1,0:T(8,128)(2,1)S(1)}, u32[]{:S(2)}, u32[]{:S(2)}) collective-permute-start(bf16[256,640]{1,0:T(8,128)(2,1)S(1)} %slice_add_fusion.1), channel_id=1, source_target_pairs={{0,1},{1,2},{2,3},{3,0},{4,5},{5,6},{6,7},{7,4},{8,9},{9,10},{10,1... | collective-permute-start | bytes 983048 | tf_op jit(solution)/shard_map/ppermute | solution.py:221
  109.0 5.6 %copy-start.11 = (f32[512,640]{1,0:T(8,128)S(1)}, f32[512,640]{1,0:T(8,128)}, u32[]{:S(2)}) copy-start(f32[512,640]{1,0:T(8,128)} %get-tuple-element.23) | copy-start | bytes 3932164

commit v5 on v4

--- a/solution.py
+++ b/solution.py
@@ -47,7 +47,6 @@
     key_copy = pltpu.make_async_copy(kw_hbm, kw, sems.at[0])
     value_copy = pltpu.make_async_copy(vw_hbm, vw, sems.at[1])
     key_copy.start()
-    value_copy.start()
 
     def column(k):
         return pl.multiple_of(lax.rem(z + k, 4) * width, 128)
@@ -92,6 +91,7 @@
         top = [(near[0], 0), (far[0], 0), (near[1], 0)]
         bottom = [(near[2], half), (far[1], half), (near[3], half)]
     lax.fori_loop(0, groups // 2, functools.partial(normalise_group, top), 0)
+    value_copy.start()
     lax.fori_loop(groups // 2, groups, functools.partial(normalise_group, bottom), 0)
 
     key_copy.wait()

time: 119 us -> 119 us (level)
  no operation moved by 1% of the time
where the time goes in v5:
time: 119 us; the launch traced here: 118 us
  Pallas kernels  36.3 us (31%)
  starting transfers between devices  32.3 us (27%)
  waiting for transfers between devices  31.2 us (26%)
  local copies, waits for them, and re-layouts  8.79 us (7%)
  other arithmetic  8.67 us (7%)
    pallas_call x2, Pallas kernels, ffn(): pl.pallas_call(ffn_kernel, out_shape=[jax.ShapeDtypeStruct((rows, width),...  30 us
    ppermute x18, waiting for transfers between devices, shift(): return lax.ppermute(array, 'z', [(i, (i + by) % 4) for i in range(4)])  23.8 us
    ppermute x18, starting transfers between devices, shift(): return lax.ppermute(array, 'z', [(i, (i + by) % 4) for i in range(4)])  22.9 us
    all_to_all x1, waiting for transfers between devices, local(): lax.all_to_all(sent, 'x', split_axis=0, concat_axis=0, tiled=True)  7.41 us
    all_to_all x1, starting transfers between devices, local(): lax.all_to_all(sent, 'x', split_axis=0, concat_axis=0, tiled=True)  4.96 us
    all_to_all x1, starting transfers between devices, local(): lax.all_to_all(update_parts, 'y', split_axis=0, concat_axis=0, tiled=True)  4.46 us
    pallas_call x1, Pallas kernels, update_products(): pl.pallas_call(update_kernel, out_shape=[jax.ShapeDtypeStruct((share, uni...  3.07 us
    convert_element_type x2, other arithmetic, local(): outputs.append(total.astype(jnp.bfloat16))  2.86 us
  transfers between devices with their start and end apart: 21, of which 8 were waited for; matrix products, arithmetic and copies ran while one was open for 13% of the time, Pallas kernels for 30%

profile of v5, /device:TPU:2, one launch (start us, length us, event | category | flops | bytes accessed | tf_op | source)
XLA Modules:
  0.0 118.1 jit_solution(2147772413092249911)
XLA Ops:
  0.7 0.0 copy-start.3
  0.7 2.3 %fusion = (bf16[512,640]{1,0:T(8,128)(2,1)S(1)}, bf16[512,640]{1,0:T(8,128)(2,1)}) fusion(bf16[1024,640]{1,0:T(8,128)(2,1)} %param.10), kind=kLoop, calls=%fused_computation.13 | loop fusion | bytes 2621440 | tf_op jit(solution)/shard_map/slice | solution.py:245
  3.0 1.9 %collective-permute-start.1 = (bf16[512,640]{1,0:T(8,128)(2,1)S(1)}, bf16[512,640]{1,0:T(8,128)(2,1)}, u32[]{:S(2)}, u32[]{:S(2)}) collective-permute-start(bf16[512,640]{1,0:T(8,128)(2,1)S(1)} %get-tuple-element.35.x0._), channel_id=1, source_target_pairs={{0,1},{1,2},{2,3},{3,0},{4,5},{5,6},{6,7},{7,4},{8,9},{9,10},{10,1... | collective-permute-start | bytes 1966088 | tf_op jit(solution)/shard_map/ppermute | solution.py:221
  4.9 2.1 %collective-permute-start = (bf16[512,640]{1,0:T(8,128)(2,1)S(1)}, bf16[512,640]{1,0:T(8,128)(2,1)}, u32[]{:S(2)}, u32[]{:S(2)}) collective-permute-start(bf16[512,640]{1,0:T(8,128)(2,1)S(1)} %get-tuple-element.35.x0._), channel_id=1, source_target_pairs={{0,3},{1,0},{2,1},{3,2},{4,7},{5,4},{6,5},{7,6},{8,11},{9,8},{10,9... | collective-permute-start | bytes 1966088 | tf_op jit(solution)/shard_map/ppermute | solution.py:221
  7.0 0.1 copy.13.weight
  7.2 2.1 %shard_map.122 = bf16[4,1920,128]{2,1,0:T(8,128)(2,1)} custom-call(s32[1]{0:T(128)} %bitcast.2.place, f32[64,1]{1,0:T(8,128)S(1)} %copy.13.weight, bf16[64,2560]{1,0:T(8,128)(2,1)S(1)} %copy-done, bf16[64,2560]{1,0:T(8,128)(2,1)S(1)} %copy-done.1, bf16[64,1280]{1,0:T(8,128)(2,1)S(1)} %copy-done.3, bf16[64,1280]{1,0:T(8,128)(2,1)S(1)} %copy-done.2, ...), custom_call_target="tpu_custom_call" | custom-call | bytes 4194304 | tf_op jit(solution)/shard_map/pallas_call | solution.py:261
  9.3 5.0 %all-to-all-start = ((bf16[4,1920,128]{2,1,0:T(8,128)(2,1)}), bf16[4,1920,128]{2,1,0:T(8,128)(2,1)S(1)}, u32[]{:S(2)}, u32[]{:S(2)}) async-start(bf16[4,1920,128]{2,1,0:T(8,128)(2,1)} %shard_map.122), calls=%async_computation | async-start | bytes 3932160 | tf_op jit(solution)/shard_map/all_to_all | solution.py:269
  14.3 2.0 %fusion.1 = (bf16[256,640]{1,0:T(8,128)(2,1)}, bf16[256,640]{1,0:T(8,128)(2,1)}) fusion(bf16[1024,640]{1,0:T(8,128)(2,1)} %param.10), kind=kLoop, calls=%fused_computation.14 | loop fusion | bytes 1310720 | tf_op jit(solution)/shard_map/slice | solution.py:246
  16.2 2.0 %collective-permute-start.10 = (bf16[256,640]{1,0:T(8,128)(2,1)}, bf16[256,640]{1,0:T(8,128)(2,1)}, u32[]{:S(2)}, u32[]{:S(2)}) collective-permute-start(bf16[256,640]{1,0:T(8,128)(2,1)} %get-tuple-element.37), channel_id=1, source_target_pairs={{0,3},{1,0},{2,1},{3,2},{4,7},{5,4},{6,5},{7,6},{8,11},{9,8},{10,9... | collective-permute-start | bytes 983048 | tf_op jit(solution)/shard_map/ppermute | solution.py:221
  18.3 0.0 collective-permute-start.9
  18.4 0.0 copy-start.4
  18.4 0.9 slice_convert_fusion.1
  19.3 3.4 %collective-permute-done.1.refs_1_ = bf16[512,640]{1,0:T(8,128)(2,1)} collective-permute-done((bf16[512,640]{1,0:T(8,128)(2,1)S(1)}, bf16[512,640]{1,0:T(8,128)(2,1)}, u32[]{:S(2)}, u32[]{:S(2)}) %collective-permute-start.1) | collective-permute-done | bytes 655392 | tf_op jit(solution)/shard_map/ppermute | solution.py:221
  22.7 1.7 %slice.110 = bf16[256,640]{1,0:T(8,128)(2,1)} slice(bf16[512,640]{1,0:T(8,128)(2,1)} %collective-permute-done.1.refs_1_), slice={[0:256], [0:640]} | slice | bytes 655360 | tf_op jit(solution)/shard_map/slice | solution.py:249
  24.4 1.7 %slice.111 = bf16[256,640]{1,0:T(8,128)(2,1)} slice(bf16[512,640]{1,0:T(8,128)(2,1)} %collective-permute-done.refs_0_), slice={[256:512], [0:640]} | slice | bytes 655360 | tf_op jit(solution)/shard_map/slice | solution.py:250
  26.2 3.2 %collective-permute-start.3 = (bf16[256,640]{1,0:T(8,128)(2,1)}, bf16[256,640]{1,0:T(8,128)(2,1)}, u32[]{:S(2)}, u32[]{:S(2)}) collective-permute-start(bf16[256,640]{1,0:T(8,128)(2,1)} %slice.111), channel_id=1, source_target_pairs={{0,3},{1,0},{2,1},{3,2},{4,7},{5,4},{6,5},{7,6},{8,11},{9,8},{10,9... | collective-permute-start | bytes 983048 | tf_op jit(solution)/shard_map/ppermute | solution.py:221
  29.4 0.7 fusion.3
  30.1 7.4 %all-to-all-done.gathered = bf16[4,1920,128]{2,1,0:T(8,128)(2,1)S(1)} async-done(((bf16[4,1920,128]{2,1,0:T(8,128)(2,1)}), bf16[4,1920,128]{2,1,0:T(8,128)(2,1)S(1)}, u32[]{:S(2)}, u32[]{:S(2)}) %all-to-all-start) | async-done | bytes 1966112 | tf_op jit(solution)/shard_map/all_to_all | solution.py:269
  37.5 0.1 slice.116
  37.6 1.8 %collective-permute-start.8 = (bf16[256,640]{1,0:T(8,128)(2,1)}, bf16[256,640]{1,0:T(8,128)(2,1)S(1)}, u32[]{:S(2)}, u32[]{:S(2)}) collective-permute-start(bf16[256,640]{1,0:T(8,128)(2,1)} %get-tuple-element.38), channel_id=1, source_target_pairs={{0,3},{1,0},{2,1},{3,2},{4,7},{5,4},{6,5},{7,6},{8,11},{9,8},{10,9... | collective-permute-start | bytes 983048 | tf_op jit(solution)/shard_map/ppermute | solution.py:221
  39.4 0.3 collective-permute-start.12
  39.7 4.7 %collective-permute-done.2.refs_2_ = bf16[256,640]{1,0:T(8,128)(2,1)} collective-permute-done((bf16[256,640]{1,0:T(8,128)(2,1)}, bf16[256,640]{1,0:T(8,128)(2,1)}, u32[]{:S(2)}, u32[]{:S(2)}) %collective-permute-start.2) | collective-permute-done | bytes 327712 | tf_op jit(solution)/shard_map/ppermute | solution.py:221
  44.4 1.4 %collective-permute-start.13 = (bf16[256,640]{1,0:T(8,128)(2,1)}, bf16[256,640]{1,0:T(8,128)(2,1)S(1)}, u32[]{:S(2)}, u32[]{:S(2)}) collective-permute-start(bf16[256,640]{1,0:T(8,128)(2,1)} %collective-permute-done.10.refs_2_), channel_id=1, source_target_pairs={{0,3},{1,0},{2,1},{3,2},{4,7},{5,4},{6,5},{7,6},{8,11},{9,8},{10,9... | collective-permute-start | bytes 983048 | tf_op jit(solution)/shard_map/ppermute | solution.py:221
  45.9 15.0 %shard_map.121 = (f32[512,640]{1,0:T(8,128)}, bf16[512,640]{1,0:T(8,128)(2,1)S(1)}, bf16[512,640]{1,0:T(8,128)(2,1)S(1)}, bf16[256,640]{1,0:T(8,128)(2,1)S(1)}, bf16[256,640]{1,0:T(8,128)(2,1)S(1)}) custom-call(s32[1]{0:T(128)} %bitcast.place.refs_12_, bf16[512,640]{1,0:T(8,128)(2,1)S(1)} %get-tuple-element.35.x0._, ...), custom_call_target="tpu_custom_call" | custom-call | flops 26843545600 | bytes 23592960 | tf_op jit(solution)/shard_map/pallas_call | solution.py:131
  60.9 0.5 collective-permute-start.6
  61.4 3.1 %shard_map.123 = (f32[160,1280]{1,0:T(8,128)S(1)}, bf16[4,160,1280]{2,1,0:T(8,128)(2,1)}) custom-call(s32[1]{0:T(128)} %bitcast.1.place, bf16[4,1920,128]{2,1,0:T(8,128)(2,1)S(1)} %all-to-all-done.gathered, bf16[4,1600,128]{2,1,0:T(8,128)(2,1)S(1)} %collective-permute-done.14.swapped), custom_call_target="tpu_custom_call" | custom-call | flops 3355443200 | bytes 8388608 | tf_op jit(solution)/shard_map/pallas_call | solution.py:204
  64.4 1.6 %collective-permute-start.4 = (bf16[512,640]{1,0:T(8,128)(2,1)S(1)}, bf16[512,640]{1,0:T(8,128)(2,1)S(1)}, u32[]{:S(2)}, u32[]{:S(2)}) collective-permute-start(bf16[512,640]{1,0:T(8,128)(2,1)S(1)} %get-tuple-element.19), channel_id=1, source_target_pairs={{0,1},{1,2},{2,3},{3,0},{4,5},{5,6},{6,7},{7,4},{8,9},{9,10},{10,1... | collective-permute-start | bytes 1966088 | tf_op jit(solution)/shard_map/ppermute | solution.py:221
  66.1 15.0 %shard_map.124 = (f32[512,640]{1,0:T(8,128)}, bf16[512,640]{1,0:T(8,128)(2,1)}, bf16[512,640]{1,0:T(8,128)(2,1)}, bf16[256,640]{1,0:T(8,128)(2,1)S(1)}, bf16[256,640]{1,0:T(8,128)(2,1)S(1)}) custom-call(s32[1]{0:T(128)} %bitcast.place.refs_12_, bf16[512,640]{1,0:T(8,128)(2,1)} %get-tuple-element.36.x0, bf16[256,640]{1,0:T(8,128)(2,1)S(1)} %collective-permute-done.8.refs_0_, ...), custom_call_target="tpu_custom_call" | custom-call | flops 26843545600 | bytes 23592960 | tf_op jit(solution)/shard_map/pallas_call | solution.py:131
  81.1 1.7 %collective-permute-start.17 = (bf16[512,640]{1,0:T(8,128)(2,1)}, bf16[512,640]{1,0:T(8,128)(2,1)}, u32[]{:S(2)}, u32[]{:S(2)}) collective-permute-start(bf16[512,640]{1,0:T(8,128)(2,1)} %get-tuple-element.26), channel_id=1, source_target_pairs={{0,3},{1,0},{2,1},{3,2},{4,7},{5,4},{6,5},{7,6},{8,11},{9,8},{10,9... | collective-permute-start | bytes 1966088 | tf_op jit(solution)/shard_map/ppermute | solution.py:221
  82.8 0.4 collective-permute-start.15
  83.2 0.8 slice_add_fusion.2
  84.0 2.8 %collective-permute-start.7 = (bf16[256,640]{1,0:T(8,128)(2,1)}, bf16[256,640]{1,0:T(8,128)(2,1)}, u32[]{:S(2)}, u32[]{:S(2)}) collective-permute-start(bf16[256,640]{1,0:T(8,128)(2,1)} %slice_add_fusion.2), channel_id=1, source_target_pairs={{0,3},{1,0},{2,1},{3,2},{4,7},{5,4},{6,5},{7,6},{8,11},{9,8},{10,9... | collective-permute-start | bytes 983048 | tf_op jit(solution)/shard_map/ppermute | solution.py:221
  86.8 0.8 slice_add_fusion.3
  87.7 0.1 copy-done.14
  87.8 4.5 %all-to-all-start.1 = ((bf16[4,160,1280]{2,1,0:T(8,128)(2,1)}), bf16[4,160,1280]{2,1,0:T(8,128)(2,1)S(1)}, u32[]{:S(2)}, u32[]{:S(2)}) async-start(bf16[4,160,1280]{2,1,0:T(8,128)(2,1)} %get-tuple-element.22.refs_14_), calls=%async_computation.1 | async-start | bytes 3276800 | tf_op jit(solution)/shard_map/all_to_all | solution.py:296
  92.3 6.8 %collective-permute-done.17 = bf16[512,640]{1,0:T(8,128)(2,1)} collective-permute-done((bf16[512,640]{1,0:T(8,128)(2,1)}, bf16[512,640]{1,0:T(8,128)(2,1)}, u32[]{:S(2)}, u32[]{:S(2)}) %collective-permute-start.17) | collective-permute-done | bytes 655392 | tf_op jit(solution)/shard_map/ppermute | solution.py:221
  99.1 1.0 slice_add_fusion
  100.1 2.9 %collective-permute-start.18 = (bf16[256,640]{1,0:T(8,128)(2,1)S(1)}, bf16[256,640]{1,0:T(8,128)(2,1)S(1)}, u32[]{:S(2)}, u32[]{:S(2)}) collective-permute-start(bf16[256,640]{1,0:T(8,128)(2,1)S(1)} %slice_add_fusion), channel_id=1, source_target_pairs={{0,3},{1,0},{2,1},{3,2},{4,7},{5,4},{6,5},{7,6},{8,11},{9,8},{10,9... | collective-permute-start | bytes 983048 | tf_op jit(solution)/shard_map/ppermute | solution.py:221
  103.0 1.0 slice_add_fusion.1
  104.0 0.1 collective-permute-start.16
  104.1 2.0 %collective-permute-done.7 = bf16[256,640]{1,0:T(8,128)(2,1)} collective-permute-done((bf16[256,640]{1,0:T(8,128)(2,1)}, bf16[256,640]{1,0:T(8,128)(2,1)}, u32[]{:S(2)}, u32[]{:S(2)}) %collective-permute-start.7) | collective-permute-done | bytes 327712 | tf_op jit(solution)/shard_map/ppermute | solution.py:221
  106.1 2.9 %collective-permute-done.5 = bf16[256,640]{1,0:T(8,128)(2,1)} collective-permute-done((bf16[256,640]{1,0:T(8,128)(2,1)}, bf16[256,640]{1,0:T(8,128)(2,1)}, u32[]{:S(2)}, u32[]{:S(2)}) %collective-permute-start.5) | collective-permute-done | bytes 327712 | tf_op jit(solution)/shard_map/ppermute | solution.py:221
  109.0 1.5 %add_convert_fusion.3 = (bf16[256,640]{1,0:T(8,128)(2,1)S(1)}, bf16[256,640]{1,0:T(8,128)(2,1)S(1)}) fusion(bf16[256,640]{1,0:T(8,128)(2,1)} %collective-permute-done.5, f32[512,640]{1,0:T(8,128)S(1)} %copy-done.10, bf16[512,640]{1,0:T(8,128)(2,1)S(1)} %copy-done.13, bf16[256,640]{1,0:T(8,128)(2,1)} %collective-permute-done.7, bf16[512,640]{1,0:T(8,128)(2,1)} %copy-done.14), kind=kLoop, calls=%fused_computation.4 | loop fusion | flops 1638400 | bytes 3276800 | tf_op jit(solution)/shard_map/convert_element_type | solution.py:318
  110.5 1.5 %collective-permute-done.18 = bf16[256,640]{1,0:T(8,128)(2,1)S(1)} collective-permute-done((bf16[256,640]{1,0:T(8,128)(2,1)S(1)}, bf16[256,640]{1,0:T(8,128)(2,1)S(1)}, u32[]{:S(2)}, u32[]{:S(2)}) %collective-permute-start.18) | collective-permute-done | bytes 327712 | tf_op jit(solution)/shard_map/ppermute | solution.py:221
  112.0 2.5 %collective-permute-done.16 = bf16[256,640]{1,0:T(8,128)(2,1)S(1)} collective-permute-done((bf16[256,640]{1,0:T(8,128)(2,1)S(1)}, bf16[256,640]{1,0:T(8,128)(2,1)S(1)}, u32[]{:S(2)}, u32[]{:S(2)}) %collective-permute-start.16) | collective-permute-done | bytes 327712 | tf_op jit(solution)/shard_map/ppermute | solution.py:221
  114.5 1.3 %add_convert_fusion.1 = (bf16[256,640]{1,0:T(8,128)(2,1)S(1)}, bf16[256,640]{1,0:T(8,128)(2,1)S(1)}) fusion(bf16[256,640]{1,0:T(8,128)(2,1)S(1)} %collective-permute-done.16, f32[512,640]{1,0:T(8,128)S(1)} %copy-done.11, bf16[512,640]{1,0:T(8,128)(2,1)} %collective-permute-done.17, bf16[256,640]{1,0:T(8,128)(2,1)S(1)} %collective-permute-done.18, ...), kind=kLoop, calls=%fused_computation.2 | loop fusion | flops 1638400 | bytes 3276800 | tf_op jit(solution)/shard_map/convert_element_type | solution.py:318
  115.8 1.2 pad_maximum_fusion
  117.0 1.1 shard_map.125
  (54 shorter events, 0.1 us)
Async XLA Ops:
  0.6 6.4 %copy-start.17 = (s32[64]{0:T(128)S(1)}, s32[64]{0:T(128)}, u32[]{:S(2)}) copy-start(s32[64]{0:T(128)} %param.19) | copy-start | bytes 772
  0.6 6.5 %copy-start = (bf16[64,2560]{1,0:T(8,128)(2,1)S(1)}, bf16[64,2560]{1,0:T(8,128)(2,1)}, u32[]{:S(2)}) copy-start(bf16[64,2560]{1,0:T(8,128)(2,1)} %key_left.1) | copy-start | bytes 983044
  0.7 6.5 %copy-start.1 = (bf16[64,2560]{1,0:T(8,128)(2,1)S(1)}, bf16[64,2560]{1,0:T(8,128)(2,1)}, u32[]{:S(2)}) copy-start(bf16[64,2560]{1,0:T(8,128)(2,1)} %value_right.1) | copy-start | bytes 983044
  0.7 6.5 %copy-start.3 = (bf16[64,1280]{1,0:T(8,128)(2,1)S(1)}, bf16[64,1280]{1,0:T(8,128)(2,1)}, u32[]{:S(2)}) copy-start(bf16[64,1280]{1,0:T(8,128)(2,1)} %key_right.1) | copy-start | bytes 491524
  0.7 6.5 %copy-start.2 = (bf16[64,1280]{1,0:T(8,128)(2,1)S(1)}, bf16[64,1280]{1,0:T(8,128)(2,1)}, u32[]{:S(2)}) copy-start(bf16[64,1280]{1,0:T(8,128)(2,1)} %value_left.1) | copy-start | bytes 491524
  3.0 19.7 %collective-permute-start.1 = (bf16[512,640]{1,0:T(8,128)(2,1)S(1)}, bf16[512,640]{1,0:T(8,128)(2,1)}, u32[]{:S(2)}, u32[]{:S(2)}) collective-permute-start(bf16[512,640]{1,0:T(8,128)(2,1)S(1)} %get-tuple-element.35.x0._), channel_id=1, source_target_pairs={{0,1},{1,2},{2,3},{3,0},{4,5},{5,6},{6,7},{7,4},{8,9},{9,10},{10,1... | collective-permute-start | bytes 1966088 | tf_op jit(solution)/shard_map/ppermute | solution.py:221
  4.9 19.5 %collective-permute-start = (bf16[512,640]{1,0:T(8,128)(2,1)S(1)}, bf16[512,640]{1,0:T(8,128)(2,1)}, u32[]{:S(2)}, u32[]{:S(2)}) collective-permute-start(bf16[512,640]{1,0:T(8,128)(2,1)S(1)} %get-tuple-element.35.x0._), channel_id=1, source_target_pairs={{0,3},{1,0},{2,1},{3,2},{4,7},{5,4},{6,5},{7,6},{8,11},{9,8},{10,9... | collective-permute-start | bytes 1966088 | tf_op jit(solution)/shard_map/ppermute | solution.py:221
  9.3 9.0 %copy-start.15 = (f32[2560]{0:T(1024)S(1)}, f32[2560]{0:T(1024)}, u32[]{:S(2)}) copy-start(f32[2560]{0:T(1024)} %param.11) | copy-start | bytes 30724
  9.3 9.0 %copy-start.16 = (f32[2560]{0:T(1024)S(1)}, f32[2560]{0:T(1024)}, u32[]{:S(2)}) copy-start(f32[2560]{0:T(1024)} %param.12) | copy-start | bytes 30724
  9.3 28.1 %all-to-all-start = ((bf16[4,1920,128]{2,1,0:T(8,128)(2,1)}), bf16[4,1920,128]{2,1,0:T(8,128)(2,1)S(1)}, u32[]{:S(2)}, u32[]{:S(2)}) async-start(bf16[4,1920,128]{2,1,0:T(8,128)(2,1)} %shard_map.122), calls=%async_computation | async-start | bytes 3932160 | tf_op jit(solution)/shard_map/all_to_all | solution.py:269
  16.2 23.2 %collective-permute-start.10 = (bf16[256,640]{1,0:T(8,128)(2,1)}, bf16[256,640]{1,0:T(8,128)(2,1)}, u32[]{:S(2)}, u32[]{:S(2)}) collective-permute-start(bf16[256,640]{1,0:T(8,128)(2,1)} %get-tuple-element.37), channel_id=1, source_target_pairs={{0,3},{1,0},{2,1},{3,2},{4,7},{5,4},{6,5},{7,6},{8,11},{9,8},{10,9... | collective-permute-start | bytes 983048 | tf_op jit(solution)/shard_map/ppermute | solution.py:221
  18.3 46.2 %collective-permute-start.11 = (bf16[256,640]{1,0:T(8,128)(2,1)}, bf16[256,640]{1,0:T(8,128)(2,1)}, u32[]{:S(2)}, u32[]{:S(2)}) collective-permute-start(bf16[256,640]{1,0:T(8,128)(2,1)} %get-tuple-element.37), channel_id=1, source_target_pairs={{0,1},{1,2},{2,3},{3,0},{4,5},{5,6},{6,7},{7,4},{8,9},{9,10},{10,1... | collective-permute-start | bytes 983048 | tf_op jit(solution)/shard_map/ppermute | solution.py:221
  18.3 19.3 %collective-permute-start.9 = (bf16[256,640]{1,0:T(8,128)(2,1)}, bf16[256,640]{1,0:T(8,128)(2,1)}, u32[]{:S(2)}, u32[]{:S(2)}) collective-permute-start(bf16[256,640]{1,0:T(8,128)(2,1)} %get-tuple-element.38), channel_id=1, source_target_pairs={{0,1},{1,2},{2,3},{3,0},{4,5},{5,6},{6,7},{7,4},{8,9},{9,10},{10,1... | collective-permute-start | bytes 983048 | tf_op jit(solution)/shard_map/ppermute | solution.py:221
  18.4 11.0 %copy-start.4 = (bf16[64,1280]{1,0:T(8,128)(2,1)S(1)}, bf16[64,1280]{1,0:T(8,128)(2,1)}, u32[]{:S(2)}) copy-start(bf16[64,1280]{1,0:T(8,128)(2,1)} %key_right.1) | copy-start | bytes 491524
  24.4 19.9 %collective-permute-start.2 = (bf16[256,640]{1,0:T(8,128)(2,1)}, bf16[256,640]{1,0:T(8,128)(2,1)}, u32[]{:S(2)}, u32[]{:S(2)}) collective-permute-start(bf16[256,640]{1,0:T(8,128)(2,1)} %slice.110), channel_id=1, source_target_pairs={{0,1},{1,2},{2,3},{3,0},{4,5},{5,6},{6,7},{7,4},{8,9},{9,10},{10,1... | collective-permute-start | bytes 983048 | tf_op jit(solution)/shard_map/ppermute | solution.py:221
  26.2 19.7 %collective-permute-start.3 = (bf16[256,640]{1,0:T(8,128)(2,1)}, bf16[256,640]{1,0:T(8,128)(2,1)}, u32[]{:S(2)}, u32[]{:S(2)}) collective-permute-start(bf16[256,640]{1,0:T(8,128)(2,1)} %slice.111), channel_id=1, source_target_pairs={{0,3},{1,0},{2,1},{3,2},{4,7},{5,4},{6,5},{7,6},{8,11},{9,8},{10,9... | collective-permute-start | bytes 983048 | tf_op jit(solution)/shard_map/ppermute | solution.py:221
  30.1 15.8 %copy-start.6 = (f32[32,2560]{1,0:T(8,128)S(1)}, f32[32,2560]{1,0:T(8,128)}, u32[]{:S(2)}) copy-start(f32[32,2560]{1,0:T(8,128)} %get-tuple-element.41.refs_8_) | copy-start | bytes 983044
  30.1 15.8 %copy-start.8 = (bf16[32,2560]{1,0:T(8,128)(2,1)S(1)}, bf16[32,2560]{1,0:T(8,128)(2,1)}, u32[]{:S(2)}) copy-start(bf16[32,2560]{1,0:T(8,128)(2,1)} %get-tuple-element.50.refs_11_) | copy-start | bytes 491524
  30.1 15.8 %copy-start.9 = (bf16[32,1280]{1,0:T(8,128)(2,1)S(1)}, bf16[32,1280]{1,0:T(8,128)(2,1)}, u32[]{:S(2)}) copy-start(bf16[32,1280]{1,0:T(8,128)(2,1)} %get-tuple-element.52.refs_9_) | copy-start | bytes 245764
  37.6 28.5 %collective-permute-start.8 = (bf16[256,640]{1,0:T(8,128)(2,1)}, bf16[256,640]{1,0:T(8,128)(2,1)S(1)}, u32[]{:S(2)}, u32[]{:S(2)}) collective-permute-start(bf16[256,640]{1,0:T(8,128)(2,1)} %get-tuple-element.38), channel_id=1, source_target_pairs={{0,3},{1,0},{2,1},{3,2},{4,7},{5,4},{6,5},{7,6},{8,11},{9,8},{10,9... | collective-permute-start | bytes 983048 | tf_op jit(solution)/shard_map/ppermute | solution.py:221
  39.4 26.7 %collective-permute-start.12 = (bf16[256,640]{1,0:T(8,128)(2,1)}, bf16[256,640]{1,0:T(8,128)(2,1)S(1)}, u32[]{:S(2)}, u32[]{:S(2)}) collective-permute-start(bf16[256,640]{1,0:T(8,128)(2,1)} %collective-permute-done.9.refs_1_), channel_id=1, source_target_pairs={{0,1},{1,2},{2,3},{3,0},{4,5},{5,6},{6,7},{7,4},{8,9},{9,10},{10,1... | collective-permute-start | bytes 983048 | tf_op jit(solution)/shard_map/ppermute | solution.py:221
  44.4 21.7 %collective-permute-start.13 = (bf16[256,640]{1,0:T(8,128)(2,1)}, bf16[256,640]{1,0:T(8,128)(2,1)S(1)}, u32[]{:S(2)}, u32[]{:S(2)}) collective-permute-start(bf16[256,640]{1,0:T(8,128)(2,1)} %collective-permute-done.10.refs_2_), channel_id=1, source_target_pairs={{0,3},{1,0},{2,1},{3,2},{4,7},{5,4},{6,5},{7,6},{8,11},{9,8},{10,9... | collective-permute-start | bytes 983048 | tf_op jit(solution)/shard_map/ppermute | solution.py:221
  45.8 15.1 %collective-permute-start.14 = (bf16[4,1600,128]{2,1,0:T(8,128)(2,1)S(1)}, bf16[4,1600,128]{2,1,0:T(8,128)(2,1)S(1)}, u32[]{:S(2)}, u32[]{:S(2)}) collective-permute-start(bf16[4,1600,128]{2,1,0:T(8,128)(2,1)S(1)} %slice.116), channel_id=1, source_target_pairs={{0,4},{4,0},{1,5},{5,1},{2,6},{6,2},{3,7},{7,3},{8,12},{12,8},{9,1... | collective-permute-start | bytes 4915208 | tf_op jit(solution)/shard_map/ppermute | solution.py:292
  60.9 22.3 %collective-permute-start.6 = (bf16[512,640]{1,0:T(8,128)(2,1)S(1)}, bf16[512,640]{1,0:T(8,128)(2,1)S(1)}, u32[]{:S(2)}, u32[]{:S(2)}) collective-permute-start(bf16[512,640]{1,0:T(8,128)(2,1)S(1)} %get-tuple-element.20), channel_id=1, source_target_pairs={{0,3},{1,0},{2,1},{3,2},{4,7},{5,4},{6,5},{7,6},{8,11},{9,8},{10,9... | collective-permute-start | bytes 1966088 | tf_op jit(solution)/shard_map/ppermute | solution.py:221
  61.4 4.7 %copy-start.5 = (f32[32,2560]{1,0:T(8,128)S(1)}, f32[32,2560]{1,0:T(8,128)}, u32[]{:S(2)}) copy-start(f32[32,2560]{1,0:T(8,128)} %get-tuple-element.42.refs_10_) | copy-start | bytes 983044
  61.4 4.7 %copy-start.7 = (bf16[32,2560]{1,0:T(8,128)(2,1)S(1)}, bf16[32,2560]{1,0:T(8,128)(2,1)}, u32[]{:S(2)}) copy-start(bf16[32,2560]{1,0:T(8,128)(2,1)} %get-tuple-element.49.refs_13_) | copy-start | bytes 491524
  64.4 22.4 %collective-permute-start.4 = (bf16[512,640]{1,0:T(8,128)(2,1)S(1)}, bf16[512,640]{1,0:T(8,128)(2,1)S(1)}, u32[]{:S(2)}, u32[]{:S(2)}) collective-permute-start(bf16[512,640]{1,0:T(8,128)(2,1)S(1)} %get-tuple-element.19), channel_id=1, source_target_pairs={{0,1},{1,2},{2,3},{3,0},{4,5},{5,6},{6,7},{7,4},{8,9},{9,10},{10,1... | collective-permute-start | bytes 1966088 | tf_op jit(solution)/shard_map/ppermute | solution.py:221
  81.1 18.0 %collective-permute-start.17 = (bf16[512,640]{1,0:T(8,128)(2,1)}, bf16[512,640]{1,0:T(8,128)(2,1)}, u32[]{:S(2)}, u32[]{:S(2)}) collective-permute-start(bf16[512,640]{1,0:T(8,128)(2,1)} %get-tuple-element.26), channel_id=1, source_target_pairs={{0,3},{1,0},{2,1},{3,2},{4,7},{5,4},{6,5},{7,6},{8,11},{9,8},{10,9... | collective-permute-start | bytes 1966088 | tf_op jit(solution)/shard_map/ppermute | solution.py:221
  82.8 20.2 %collective-permute-start.15 = (bf16[512,640]{1,0:T(8,128)(2,1)}, bf16[512,640]{1,0:T(8,128)(2,1)}, u32[]{:S(2)}, u32[]{:S(2)}) collective-permute-start(bf16[512,640]{1,0:T(8,128)(2,1)} %get-tuple-element.25), channel_id=1, source_target_pairs={{0,1},{1,2},{2,3},{3,0},{4,5},{5,6},{6,7},{7,4},{8,9},{9,10},{10,1... | collective-permute-start | bytes 1966088 | tf_op jit(solution)/shard_map/ppermute | solution.py:221
  83.2 4.5 %copy-start.12 = (bf16[512,640]{1,0:T(8,128)(2,1)}, bf16[512,640]{1,0:T(8,128)(2,1)S(1)}, u32[]{:S(2)}) copy-start(bf16[512,640]{1,0:T(8,128)(2,1)S(1)} %collective-permute-done.6) | copy-start | bytes 1966084
  84.0 22.1 %collective-permute-start.7 = (bf16[256,640]{1,0:T(8,128)(2,1)}, bf16[256,640]{1,0:T(8,128)(2,1)}, u32[]{:S(2)}, u32[]{:S(2)}) collective-permute-start(bf16[256,640]{1,0:T(8,128)(2,1)} %slice_add_fusion.2), channel_id=1, source_target_pairs={{0,3},{1,0},{2,1},{3,2},{4,7},{5,4},{6,5},{7,6},{8,11},{9,8},{10,9... | collective-permute-start | bytes 983048 | tf_op jit(solution)/shard_map/ppermute | solution.py:221
  86.8 0.9 copy-start.14
  87.8 21.2 %collective-permute-start.5 = (bf16[256,640]{1,0:T(8,128)(2,1)}, bf16[256,640]{1,0:T(8,128)(2,1)}, u32[]{:S(2)}, u32[]{:S(2)}) collective-permute-start(bf16[256,640]{1,0:T(8,128)(2,1)} %slice_add_fusion.3), channel_id=1, source_target_pairs={{0,1},{1,2},{2,3},{3,0},{4,5},{5,6},{6,7},{7,4},{8,9},{9,10},{10,1... | collective-permute-start | bytes 983048 | tf_op jit(solution)/shard_map/ppermute | solution.py:221
  87.8 29.2 %all-to-all-start.1 = ((bf16[4,160,1280]{2,1,0:T(8,128)(2,1)}), bf16[4,160,1280]{2,1,0:T(8,128)(2,1)S(1)}, u32[]{:S(2)}, u32[]{:S(2)}) async-start(bf16[4,160,1280]{2,1,0:T(8,128)(2,1)} %get-tuple-element.22.refs_14_), calls=%async_computation.1 | async-start | bytes 3276800 | tf_op jit(solution)/shard_map/all_to_all | solution.py:296
  92.2 16.7 %copy-start.10 = (f32[512,640]{1,0:T(8,128)S(1)}, f32[512,640]{1,0:T(8,128)}, u32[]{:S(2)}) copy-start(f32[512,640]{1,0:T(8,128)} %get-tuple-element.17) | copy-start | bytes 3932164
  92.3 16.7 %copy-start.13 = (bf16[512,640]{1,0:T(8,128)(2,1)S(1)}, bf16[512,640]{1,0:T(8,128)(2,1)}, u32[]{:S(2)}) copy-start(bf16[512,640]{1,0:T(8,128)(2,1)} %copy-done.12) | copy-start | bytes 1966084
  100.1 11.9 %collective-permute-start.18 = (bf16[256,640]{1,0:T(8,128)(2,1)S(1)}, bf16[256,640]{1,0:T(8,128)(2,1)S(1)}, u32[]{:S(2)}, u32[]{:S(2)}) collective-permute-start(bf16[256,640]{1,0:T(8,128)(2,1)S(1)} %slice_add_fusion), channel_id=1, source_target_pairs={{0,3},{1,0},{2,1},{3,2},{4,7},{5,4},{6,5},{7,6},{8,11},{9,8},{10,9... | collective-permute-start | bytes 983048 | tf_op jit(solution)/shard_map/ppermute | solution.py:221
  104.0 10.5 %collective-permute-start.16 = (bf16[256,640]{1,0:T(8,128)(2,1)S(1)}, bf16[256,640]{1,0:T(8,128)(2,1)S(1)}, u32[]{:S(2)}, u32[]{:S(2)}) collective-permute-start(bf16[256,640]{1,0:T(8,128)(2,1)S(1)} %slice_add_fusion.1), channel_id=1, source_target_pairs={{0,1},{1,2},{2,3},{3,0},{4,5},{5,6},{6,7},{7,4},{8,9},{9,10},{10,1... | collective-permute-start | bytes 983048 | tf_op jit(solution)/shard_map/ppermute | solution.py:221
  109.0 5.5 %copy-start.11 = (f32[512,640]{1,0:T(8,128)S(1)}, f32[512,640]{1,0:T(8,128)}, u32[]{:S(2)}) copy-start(f32[512,640]{1,0:T(8,128)} %get-tuple-element.23) | copy-start | bytes 3932164
